TPU v7x, 32 devices: a whole 2x2x4 slice. The times are simulated.
32 devices in a mesh: groups: 2 (over y), patch: 16 (over z, x, core).
Axes of the slice: x: 2, y: 2, z: 4, core: 2. Of those that a mesh axis runs over, the one named last changes fastest.
Arguments:
- node_feat: bfloat16 [8192, 512], P(('groups', 'patch')), parts along dimension 0, may hold values from -6 to 6
- local_edges: bfloat16 [24576, 512], P(('groups', 'patch')), parts along dimension 0, may hold values from -6 to 6
- far_edges: bfloat16 [8192, 512], P(('groups', 'patch')), parts along dimension 0, may hold values from -6 to 6
- local_send: int32 [24576], P(('groups', 'patch')), parts along dimension 0, may hold values from 0 to 255
- local_recv: int32 [24576], P(('groups', 'patch')), parts along dimension 0, may hold values from 0 to 255
- far_send: int32 [8192], P(('groups', 'patch')), parts along dimension 0, may hold values from 0 to 4095, as said below
- far_recv: int32 [8192], P(('groups', 'patch')), parts along dimension 0, may hold values from 0 to 4095, as said below
- edge_in: bfloat16 [2, 1536, 512], replicated, may hold values from -0.15625 to 0.15625
- edge_out: bfloat16 [2, 512, 512], replicated, may hold values from -0.25 to 0.25
- node_in: bfloat16 [2, 1024, 512], replicated, may hold values from -0.1875 to 0.1875
- node_out: bfloat16 [2, 512, 512], replicated, may hold values from -0.25 to 0.25
- edge_bias: float32 [2, 512], replicated, may hold values from -3 to 3
- edge_gain: float32 [2, 512], replicated, may hold values from 0.5 to 1.5
- edge_shift: float32 [2, 512], replicated, may hold values from -3 to 3
- node_bias: float32 [2, 512], replicated, may hold values from -3 to 3
- node_gain: float32 [2, 512], replicated, may hold values from 0.5 to 1.5
- node_shift: float32 [2, 512], replicated, may hold values from -3 to 3
Outputs:
- nodes_out: bfloat16 [8192, 512], P(('groups', 'patch')), parts along dimension 0
- local_out: bfloat16 [24576, 512], P(('groups', 'patch')), parts along dimension 0
- far_out: bfloat16 [8192, 512], P(('groups', 'patch')), parts along dimension 0
There are 2 independent parts, one for each index of `groups`. A program takes and returns all parts, laid end to end along the dimension named above; an argument that names none is the same for every part. Nothing has to cross between parts.
Inputs may be any that keep to these rules, and one draw needn't show every extreme that they name: `far_send`: every sender lies among the first 64 nodes of its patch's block of 256. Of the 256 edges of one owner (aligned blocks of the array), at most 40 have their sender on any one patch, and exactly 40 do for some patch of every owner. `far_recv`: every receiver lies among the first 64 nodes of its patch's block of 256. Of the 256 edges of one owner (aligned blocks of the array), at most 40 have their receiver on any one patch, and exactly 40 do for some patch of every owner.
All inputs are finite; a program needn't handle non-finite values.
Results may differ from a plain program's by a relative error of at most 0.0075.
Values may be sent and summed in bfloat16 or wider, within the bound.
No kernel may reach another device: no remote copies, remote signals or barrier semaphores. Data moves between devices by JAX's collectives and lax.ppermute only.
A program may use at most 64 MiB of HBM per device.

v0:
```python
import jax
import jax.numpy as jnp
from jax import lax
from jax.sharding import PartitionSpec as P


def layer_norm(values, gain, shift):
    mean_value = jnp.mean(values, axis=-1, keepdims=True)
    centred = values - mean_value
    variance = jnp.mean(centred * centred, axis=-1, keepdims=True)
    return centred * lax.rsqrt(variance + 1e-05) * gain + shift


def edge_update(edges, senders, receivers, w_in, w_out, bias, gain, shift):
    width = edges.shape[1]
    pre_act = jnp.dot(edges, w_in[:width], preferred_element_type=jnp.float32)
    pre_act = pre_act + jnp.dot(
        senders, w_in[width : 2 * width], preferred_element_type=jnp.float32
    )
    pre_act = (
        pre_act + jnp.dot(receivers, w_in[2 * width :], preferred_element_type=jnp.float32) + bias
    )
    hidden = jax.nn.silu(pre_act).astype(jnp.bfloat16)
    normed = layer_norm(jnp.dot(hidden, w_out, preferred_element_type=jnp.float32), gain, shift)
    return (normed.astype(jnp.bfloat16), (edges.astype(jnp.float32) + normed).astype(jnp.bfloat16))


def node_update(nodes, summed, w_in, w_out, bias, gain, shift):
    width = nodes.shape[1]
    summed_b = summed.astype(jnp.bfloat16)
    pre_act = jnp.dot(nodes, w_in[:width], preferred_element_type=jnp.float32)
    pre_act = pre_act + jnp.dot(summed_b, w_in[width:], preferred_element_type=jnp.float32) + bias
    hidden = jax.nn.silu(pre_act).astype(jnp.bfloat16)
    normed = layer_norm(jnp.dot(hidden, w_out, preferred_element_type=jnp.float32), gain, shift)
    return (nodes.astype(jnp.float32) + normed).astype(jnp.bfloat16)


def place_slots(global_ids, node_count, devices):
    target = global_ids // node_count
    within = global_ids % node_count
    member = (target[:, None] == jnp.arange(devices, dtype=jnp.int32)[None, :]).astype(jnp.int32)
    ranking = jnp.sum((jnp.cumsum(member, axis=0) - 1) * member, axis=1)
    return (target, within, ranking)


def slot_onehot(position, slots):
    return (position[:, None] == jnp.arange(slots, dtype=jnp.int32)[None, :]).astype(jnp.int32)


def slot_table(onehot, values, empty_value):
    filled = jnp.sum(onehot, axis=0)
    total = jnp.sum(onehot * values[:, None], axis=0)
    return total + (1 - filled) * empty_value


def column_sum(onehot, rows):
    return lax.dot_general(
        onehot, rows, (((0,), (0,)), ((), ())), preferred_element_type=jnp.float32
    )


def body(
    node_feat,
    local_edges,
    far_edges,
    local_send,
    local_recv,
    far_send,
    far_recv,
    edge_in,
    edge_out,
    node_in,
    node_out,
    edge_bias,
    edge_gain,
    edge_shift,
    node_bias,
    node_gain,
    node_shift,
):
    devices = lax.axis_size("patch")
    node_count = node_feat.shape[0]
    width = node_feat.shape[1]
    far_count = far_edges.shape[0]
    local_count = local_edges.shape[0]
    capacity = 5 * far_count // (2 * devices)
    slots = devices * capacity
    s_target, s_within, s_rank = place_slots(far_send, node_count, devices)
    r_target, r_within, r_rank = place_slots(far_recv, node_count, devices)
    s_position = s_target * capacity + s_rank
    r_position = r_target * capacity + r_rank
    s_onehot = slot_onehot(s_position, slots)
    r_onehot = slot_onehot(r_position, slots)
    send_requests = slot_table(s_onehot, s_within, 0).reshape(devices, capacity)
    recv_requests = slot_table(r_onehot, r_within, 0).reshape(devices, capacity)
    edge_order = slot_table(r_onehot, jnp.arange(far_count, dtype=jnp.int32), far_count).reshape(
        devices, capacity
    )
    row_labels = slot_table(r_onehot, r_within, -1).reshape(devices, capacity)
    node_range = jnp.arange(node_count, dtype=jnp.int32)
    local_onehot = (local_recv[:, None] == node_range[None, :]).astype(jnp.bfloat16)
    nodes = node_feat
    edges = jnp.concatenate([local_edges, far_edges], axis=0)
    for layer_index in range(edge_in.shape[0]):

        def serve(requests, current=nodes):
            wanted_send, wanted_recv = requests
            return (
                lax.all_to_all(
                    jnp.take(current, wanted_send, axis=0),
                    "patch",
                    split_axis=0,
                    concat_axis=0,
                    tiled=True,
                ),
                lax.all_to_all(
                    jnp.take(current, wanted_recv, axis=0),
                    "patch",
                    split_axis=0,
                    concat_axis=0,
                    tiled=True,
                ),
            )

        got_send, got_recv = serve(
            (
                lax.all_to_all(send_requests, "patch", split_axis=0, concat_axis=0, tiled=True),
                lax.all_to_all(recv_requests, "patch", split_axis=0, concat_axis=0, tiled=True),
            )
        )
        far_senders = jnp.take(got_send.reshape(-1, width), s_position, axis=0)
        far_receivers = jnp.take(got_recv.reshape(-1, width), r_position, axis=0)
        send_rows = jnp.concatenate([jnp.take(nodes, local_send, axis=0), far_senders], axis=0)
        recv_rows = jnp.concatenate([jnp.take(nodes, local_recv, axis=0), far_receivers], axis=0)
        message, edges = edge_update(
            edges,
            send_rows,
            recv_rows,
            edge_in[layer_index],
            edge_out[layer_index],
            edge_bias[layer_index],
            edge_gain[layer_index],
            edge_shift[layer_index],
        )
        padded = jnp.concatenate(
            [message[local_count:], jnp.zeros((1, width), jnp.bfloat16)], axis=0
        )
        outgoing = jnp.take(padded, edge_order, axis=0)
        incoming, labels = (
            lax.all_to_all(outgoing, "patch", split_axis=0, concat_axis=0, tiled=True),
            lax.all_to_all(row_labels, "patch", split_axis=0, concat_axis=0, tiled=True),
        )
        far_onehot = (labels.reshape(-1)[:, None] == node_range[None, :]).astype(jnp.bfloat16)
        summed = column_sum(local_onehot, message[:local_count]) + column_sum(
            far_onehot, incoming.reshape(-1, width)
        )
        nodes = node_update(
            nodes,
            summed,
            node_in[layer_index],
            node_out[layer_index],
            node_bias[layer_index],
            node_gain[layer_index],
            node_shift[layer_index],
        )
    return (nodes, edges[:local_count], edges[local_count:])


def solution(mesh):
    in_specs = (
        P(("groups", "patch"), None),
        P(("groups", "patch"), None),
        P(("groups", "patch"), None),
        P(("groups", "patch")),
        P(("groups", "patch")),
        P(("groups", "patch")),
        P(("groups", "patch")),
        P(),
        P(),
        P(),
        P(),
        P(),
        P(),
        P(),
        P(),
        P(),
        P(),
    )
    out_specs = (
        P(("groups", "patch"), None),
        P(("groups", "patch"), None),
        P(("groups", "patch"), None),
    )
    return jax.shard_map(body, mesh=mesh, in_specs=in_specs, out_specs=out_specs, check_vma=False)
```

profile of v0, /device:TPU:0, one launch (start us, length us, event | category | flops | bytes accessed | tf_op | source)
XLA Modules:
  0.0 212.5 jit_solution(11815983477479721029)
XLA Ops:
  3.2 7.4 %all-to-all-start.2 = ((s32[16,1,40]{2,1,0:T(1,128)}), s32[16,1,40]{2,1,0:T(1,128)S(1)}, u32[]{:S(2)}, u32[]{:S(2)}) async-start(s32[16,1,40]{2,1,0:T(1,128)} %all_to_all.45), calls=%async_computation.2 | async-start | bytes 16384 | tf_op jit(solution)/shard_map/all_to_all | solution.py:128
  20.7 6.0 %all-to-all-start = ((s32[16,1,40]{2,1,0:T(1,128)}), s32[16,1,40]{2,1,0:T(1,128)S(1)}, u32[]{:S(2)}, u32[]{:S(2)}) async-start(s32[16,1,40]{2,1,0:T(1,128)} %all_to_all.41), calls=%async_computation | async-start | bytes 16384 | tf_op jit(solution)/shard_map/all_to_all | solution.py:127
  26.8 2.8 %gather_fusion.4 = bf16[640,512]{1,0:T(8,128)(2,1)S(1)} fusion(bf16[256,512]{1,0:T(8,128)(2,1)S(1)} %copy-done, s32[1024]{0:T(1024)S(1)} %get-tuple-element.45), kind=kCustom, calls=%fused_computation.7.clone | custom fusion | bytes 1313280 | tf_op jit(solution)/shard_map/jit(_take)/gather | solution.py:117
  33.0 3.6 %all-to-all-start.3 = ((bf16[16,40,512]{2,1,0:T(8,128)(2,1)}), bf16[16,40,512]{2,1,0:T(8,128)(2,1)S(1)}, u32[]{:S(2)}, u32[]{:S(2)}) async-start(bf16[16,40,512]{2,1,0:T(8,128)(2,1)} %broadcast_select_fusion.7), calls=%async_computation.3 | async-start | bytes 1310720 | tf_op jit(solution)/shard_map/all_to_all | solution.py:116
  36.8 2.8 %gather_fusion.1 = bf16[640,512]{1,0:T(8,128)(2,1)S(1)} fusion(bf16[256,512]{1,0:T(8,128)(2,1)S(1)} %copy-done, s32[1024]{0:T(1024)S(1)} %get-tuple-element.47), kind=kCustom, calls=%fused_computation.1.clone | custom fusion | bytes 1313280 | tf_op jit(solution)/shard_map/jit(_take)/gather | solution.py:110
  40.7 12.6 %all-to-all-done.3 = bf16[16,40,512]{2,1,0:T(8,128)(2,1)S(1)} async-done(((bf16[16,40,512]{2,1,0:T(8,128)(2,1)}), bf16[16,40,512]{2,1,0:T(8,128)(2,1)S(1)}, u32[]{:S(2)}, u32[]{:S(2)}) %all-to-all-start.3) | async-done | bytes 655392 | tf_op jit(solution)/shard_map/all_to_all | solution.py:116
  53.2 4.8 %all-to-all-start.1 = ((bf16[16,40,512]{2,1,0:T(8,128)(2,1)}), bf16[16,40,512]{2,1,0:T(8,128)(2,1)S(1)}, u32[]{:S(2)}, u32[]{:S(2)}) async-start(bf16[16,40,512]{2,1,0:T(8,128)(2,1)} %broadcast_select_fusion.9), calls=%async_computation.1 | async-start | bytes 1310720 | tf_op jit(solution)/shard_map/all_to_all | solution.py:109
  64.3 3.1 %fusion.56 = f32[1024,512]{1,0:T(8,128)} fusion(bf16[1024,512]{1,0:T(8,128)(2,1)S(1)} %constant_dynamic-update-slice_fusion, bf16[2,1536,512]{2,1,0:T(8,128)(2,1)} %param.32), kind=kOutput, calls=%fused_computation.90 | convolution fusion | flops 536870912 | bytes 3670016 | tf_op jit(solution)/shard_map/dot_general | solution.py:16
  74.6 4.8 %all-to-all-start.4 = ((s32[16,1,40]{2,1,0:T(1,128)}), s32[16,1,40]{2,1,0:T(1,128)S(1)}, u32[]{:S(2)}, u32[]{:S(2)}) async-start(s32[16,1,40]{2,1,0:T(1,128)} %add.246), calls=%async_computation.4 | async-start | bytes 16384 | tf_op jit(solution)/shard_map/all_to_all | solution.py:151
  80.7 3.1 %fusion.8 = f32[1024,512]{1,0:T(8,128)} fusion(bf16[256,512]{1,0:T(8,128)(2,1)S(1)} %broadcast_select_fusion.13, bf16[768,512]{1,0:T(8,128)(2,1)S(1)} %copy-done.11, bf16[2,1536,512]{2,1,0:T(8,128)(2,1)} %param.32), kind=kOutput, calls=%fused_computation.34 | convolution fusion | flops 538968064 | bytes 3670016 | tf_op jit(solution)/shard_map/dot_general | solution.py:17
  83.8 4.0 %fusion.110 = (f32[1024]{0:T(1024)S(1)}, f32[1024,512]{1,0:T(8,128)S(1)}) fusion(bf16[2,512,512]{2,1,0:T(8,128)(2,1)} %param.33, f32[1024,512]{1,0:T(8,128)} %fusion.56, f32[1024,512]{1,0:T(8,128)} %fusion.8, bf16[256,512]{1,0:T(8,128)(2,1)S(1)} %copy-done.12, bf16[768,512]{1,0:T(8,128)(2,1)S(1)} %copy-done.9, f32[512]{0:T(512)S(1)} %bitcast.154, ...), kind=kOutput, calls=%fused_computation.199 | convolution fusion | flops 1080556544 | bytes 8394752 | tf_op jit(solution)/shard_map/dot_general | solution.py:24
  94.5 6.1 %all-to-all-start.5 = ((bf16[16,40,512]{2,1,0:T(8,128)(2,1)}), bf16[16,40,512]{2,1,0:T(8,128)(2,1)S(1)}, u32[]{:S(2)}, u32[]{:S(2)}) async-start(bf16[16,40,512]{2,1,0:T(8,128)(2,1)} %broadcast_select_fusion.5), calls=%async_computation.5 | async-start | bytes 1310720 | tf_op jit(solution)/shard_map/all_to_all | solution.py:150
  107.1 10.2 %all-to-all-done.5 = bf16[16,40,512]{2,1,0:T(8,128)(2,1)S(1)} async-done(((bf16[16,40,512]{2,1,0:T(8,128)(2,1)}), bf16[16,40,512]{2,1,0:T(8,128)(2,1)S(1)}, u32[]{:S(2)}, u32[]{:S(2)}) %all-to-all-start.5) | async-done | bytes 655392 | tf_op jit(solution)/shard_map/all_to_all | solution.py:150
  122.5 2.8 %gather_fusion.8 = bf16[640,512]{1,0:T(8,128)(2,1)S(1)} fusion(bf16[256,512]{1,0:T(8,128)(2,1)S(1)} %add_convert_fusion.3, s32[1024]{0:T(1024)S(1)} %get-tuple-element.47), kind=kCustom, calls=%fused_computation.8.clone | custom fusion | bytes 1313280 | tf_op jit(solution)/shard_map/jit(_take)/gather | solution.py:110
  126.3 4.8 %all-to-all-start.6 = ((bf16[16,40,512]{2,1,0:T(8,128)(2,1)}), bf16[16,40,512]{2,1,0:T(8,128)(2,1)S(1)}, u32[]{:S(2)}, u32[]{:S(2)}) async-start(bf16[16,40,512]{2,1,0:T(8,128)(2,1)} %broadcast_select_fusion.8), calls=%async_computation.6 | async-start | bytes 1310720 | tf_op jit(solution)/shard_map/all_to_all | solution.py:109
  134.9 12.8 %all-to-all-done.6 = bf16[16,40,512]{2,1,0:T(8,128)(2,1)S(1)} async-done(((bf16[16,40,512]{2,1,0:T(8,128)(2,1)}), bf16[16,40,512]{2,1,0:T(8,128)(2,1)S(1)}, u32[]{:S(2)}, u32[]{:S(2)}) %all-to-all-start.6) | async-done | bytes 655392 | tf_op jit(solution)/shard_map/all_to_all | solution.py:109
  147.7 4.8 %all-to-all-start.7 = ((bf16[16,40,512]{2,1,0:T(8,128)(2,1)}), bf16[16,40,512]{2,1,0:T(8,128)(2,1)S(1)}, u32[]{:S(2)}, u32[]{:S(2)}) async-start(bf16[16,40,512]{2,1,0:T(8,128)(2,1)} %broadcast_select_fusion.6), calls=%async_computation.7 | async-start | bytes 1310720 | tf_op jit(solution)/shard_map/all_to_all | solution.py:116
  152.5 3.1 %fusion.45 = f32[1024,512]{1,0:T(8,128)} fusion(bf16[1024,512]{1,0:T(8,128)(2,1)S(1)} %get-tuple-element.16, bf16[2,1536,512]{2,1,0:T(8,128)(2,1)} %param.32), kind=kOutput, calls=%fused_computation.80 | convolution fusion | flops 536870912 | bytes 3670016 | tf_op jit(solution)/shard_map/dot_general | solution.py:16
  155.6 3.3 %gather_fusion.7 = bf16[768,512]{1,0:T(8,128)(2,1)} fusion(bf16[256,512]{1,0:T(8,128)(2,1)S(1)} %add_convert_fusion.3, s32[1024]{0:T(1024)S(1)} %copy-done.14), kind=kCustom, calls=%fused_computation.5.clone | custom fusion | bytes 1575936 | tf_op jit(solution)/shard_map/jit(_take)/gather | solution.py:133
  158.9 3.3 %gather_fusion.10 = bf16[768,512]{1,0:T(8,128)(2,1)} fusion(bf16[256,512]{1,0:T(8,128)(2,1)S(1)} %add_convert_fusion.3, s32[1024]{0:T(1024)S(1)} %copy-done.16), kind=kCustom, calls=%fused_computation.6.clone | custom fusion | bytes 1575936 | tf_op jit(solution)/shard_map/jit(_take)/gather | solution.py:134
  170.5 3.4 %fusion.18 = f32[1024,512]{1,0:T(8,128)} fusion(bf16[256,512]{1,0:T(8,128)(2,1)S(1)} %broadcast_select_fusion.12, bf16[768,512]{1,0:T(8,128)(2,1)} %broadcast_select_fusion.2, bf16[2,1536,512]{2,1,0:T(8,128)(2,1)} %param.32), kind=kOutput, calls=%fused_computation.41 | convolution fusion | flops 538968064 | bytes 3670016 | tf_op jit(solution)/shard_map/dot_general | solution.py:17
  173.9 5.3 %fusion.116 = (f32[1024]{0:T(1024)S(1)}, f32[1024,512]{1,0:T(8,128)}) fusion(bf16[2,512,512]{2,1,0:T(8,128)(2,1)} %param.33, f32[1024,512]{1,0:T(8,128)} %fusion.45, f32[1024,512]{1,0:T(8,128)} %fusion.18, bf16[256,512]{1,0:T(8,128)(2,1)S(1)} %broadcast_select_fusion.10, bf16[768,512]{1,0:T(8,128)(2,1)S(1)} %copy-done.10, f32[512]{0:T(512)S(1)} %bitcast.152, ...), kind=kOutput, calls=%fused_computation.201 | convolution fusion | flops 1080556544 | bytes 8394752 | tf_op jit(solution)/shard_map/dot_general | solution.py:24
  186.9 4.8 %all-to-all-start.8 = ((bf16[16,40,512]{2,1,0:T(8,128)(2,1)}), bf16[16,40,512]{2,1,0:T(8,128)(2,1)S(1)}, u32[]{:S(2)}, u32[]{:S(2)}) async-start(bf16[16,40,512]{2,1,0:T(8,128)(2,1)} %broadcast_select_fusion.4), calls=%async_computation.8 | async-start | bytes 1310720 | tf_op jit(solution)/shard_map/all_to_all | solution.py:150
  194.7 13.6 %all-to-all-done.8 = bf16[16,40,512]{2,1,0:T(8,128)(2,1)S(1)} async-done(((bf16[16,40,512]{2,1,0:T(8,128)(2,1)}), bf16[16,40,512]{2,1,0:T(8,128)(2,1)S(1)}, u32[]{:S(2)}, u32[]{:S(2)}) %all-to-all-start.8) | async-done | bytes 655392 | tf_op jit(solution)/shard_map/all_to_all | solution.py:150
  (207 shorter events, 77.8 us)
Async XLA Ops:
  0.6 26.2 %copy-start = (bf16[256,512]{1,0:T(8,128)(2,1)S(1)}, bf16[256,512]{1,0:T(8,128)(2,1)}, u32[]{:S(2)}) copy-start(bf16[256,512]{1,0:T(8,128)(2,1)} %param.25) | copy-start | bytes 786436
  2.3 70.0 %copy-start.38 = (pred[256]{0:T(512)(128)(4,1)}, pred[256]{0:T(512)(128)(4,1)S(1)}, u32[]{:S(2)}) copy-start(pred[256]{0:T(512)(128)(4,1)S(1)} %get-tuple-element.10) | copy-start | bytes 772
  3.2 17.4 %all-to-all-start.2 = ((s32[16,1,40]{2,1,0:T(1,128)}), s32[16,1,40]{2,1,0:T(1,128)S(1)}, u32[]{:S(2)}, u32[]{:S(2)}) async-start(s32[16,1,40]{2,1,0:T(1,128)} %all_to_all.45), calls=%async_computation.2 | async-start | bytes 16384 | tf_op jit(solution)/shard_map/all_to_all | solution.py:128
  12.0 51.1 %copy-start.28 = (pred[768]{0:T(1024)(128)(4,1)}, pred[768]{0:T(1024)(128)(4,1)S(1)}, u32[]{:S(2)}) copy-start(pred[768]{0:T(1024)(128)(4,1)S(1)} %compare_and_fusion.4) | copy-start | bytes 2308
  12.1 59.0 %copy-start.26 = (s32[1024]{0:T(1024)}, s32[1024]{0:T(1024)S(1)}, u32[]{:S(2)}) copy-start(s32[1024]{0:T(1024)S(1)} %pad_clamp_fusion.1) | copy-start | bytes 12292
  13.8 66.8 %copy-start.40 = (pred[256]{0:T(512)(128)(4,1)}, pred[256]{0:T(512)(128)(4,1)S(1)}, u32[]{:S(2)}) copy-start(pred[256]{0:T(512)(128)(4,1)S(1)} %get-tuple-element.12) | copy-start | bytes 772
  19.9 59.5 %copy-start.27 = (s32[1024]{0:T(1024)}, s32[1024]{0:T(1024)S(1)}, u32[]{:S(2)}) copy-start(s32[1024]{0:T(1024)S(1)} %pad_clamp_fusion.4) | copy-start | bytes 12292
  20.7 12.3 %all-to-all-start = ((s32[16,1,40]{2,1,0:T(1,128)}), s32[16,1,40]{2,1,0:T(1,128)S(1)}, u32[]{:S(2)}, u32[]{:S(2)}) async-start(s32[16,1,40]{2,1,0:T(1,128)} %all_to_all.41), calls=%async_computation | async-start | bytes 16384 | tf_op jit(solution)/shard_map/all_to_all | solution.py:127
  33.0 20.2 %all-to-all-start.3 = ((bf16[16,40,512]{2,1,0:T(8,128)(2,1)}), bf16[16,40,512]{2,1,0:T(8,128)(2,1)S(1)}, u32[]{:S(2)}, u32[]{:S(2)}) async-start(bf16[16,40,512]{2,1,0:T(8,128)(2,1)} %broadcast_select_fusion.7), calls=%async_computation.3 | async-start | bytes 1310720 | tf_op jit(solution)/shard_map/all_to_all | solution.py:116
  36.7 33.4 %copy-start.30 = (pred[768]{0:T(1024)(128)(4,1)}, pred[768]{0:T(1024)(128)(4,1)S(1)}, u32[]{:S(2)}) copy-start(pred[768]{0:T(1024)(128)(4,1)S(1)} %compare_and_fusion.3) | copy-start | bytes 2308
  36.7 56.8 %copy-start.18 = (pred[16,40]{1,0:T(8,128)(4,1)}, pred[16,40]{1,0:T(8,128)(4,1)S(1)}, u32[]{:S(2)}) copy-start(pred[16,40]{1,0:T(8,128)(4,1)S(1)} %compare_and_fusion) | copy-start | bytes 1924
  36.8 30.6 %copy-start.15 = (s32[1024]{0:T(1024)}, s32[1024]{0:T(1024)S(1)}, u32[]{:S(2)}) copy-start(s32[1024]{0:T(1024)S(1)} %get-tuple-element.46) | copy-start | bytes 12292
  39.6 21.1 %copy-start.22 = (pred[16,40]{1,0:T(8,128)(4,1)}, pred[16,40]{1,0:T(8,128)(4,1)S(1)}, u32[]{:S(2)}) copy-start(pred[16,40]{1,0:T(8,128)(4,1)S(1)} %compare_and_fusion.2) | copy-start | bytes 1924
  53.2 21.4 %all-to-all-start.1 = ((bf16[16,40,512]{2,1,0:T(8,128)(2,1)}), bf16[16,40,512]{2,1,0:T(8,128)(2,1)S(1)}, u32[]{:S(2)}, u32[]{:S(2)}) async-start(bf16[16,40,512]{2,1,0:T(8,128)(2,1)} %broadcast_select_fusion.9), calls=%async_computation.1 | async-start | bytes 1310720 | tf_op jit(solution)/shard_map/all_to_all | solution.py:109
  72.3 8.4 %copy-start.11 = (bf16[768,512]{1,0:T(8,128)(2,1)S(1)}, bf16[768,512]{1,0:T(8,128)(2,1)}, u32[]{:S(2)}) copy-start(bf16[768,512]{1,0:T(8,128)(2,1)} %broadcast_select_fusion.3) | copy-start | bytes 2359300
  74.6 19.9 %all-to-all-start.4 = ((s32[16,1,40]{2,1,0:T(1,128)}), s32[16,1,40]{2,1,0:T(1,128)S(1)}, u32[]{:S(2)}, u32[]{:S(2)}) async-start(s32[16,1,40]{2,1,0:T(1,128)} %add.246), calls=%async_computation.4 | async-start | bytes 16384 | tf_op jit(solution)/shard_map/all_to_all | solution.py:151
  93.5 8.4 %copy-start.44 = (f32[2,512]{1,0:T(2,128)S(1)}, f32[2,512]{1,0:T(2,128)}, u32[]{:S(2)}) copy-start(f32[2,512]{1,0:T(2,128)} %param.41) | copy-start | bytes 12292
  94.5 24.1 %copy-start.6 = (bf16[1024,512]{1,0:T(8,128)(2,1)S(1)}, bf16[1024,512]{1,0:T(8,128)(2,1)}, u32[]{:S(2)}) copy-start(bf16[1024,512]{1,0:T(8,128)(2,1)} %copy-done.5) | copy-start | bytes 3145732
  94.5 22.7 %all-to-all-start.5 = ((bf16[16,40,512]{2,1,0:T(8,128)(2,1)}), bf16[16,40,512]{2,1,0:T(8,128)(2,1)S(1)}, u32[]{:S(2)}, u32[]{:S(2)}) async-start(bf16[16,40,512]{2,1,0:T(8,128)(2,1)} %broadcast_select_fusion.5), calls=%async_computation.5 | async-start | bytes 1310720 | tf_op jit(solution)/shard_map/all_to_all | solution.py:150
  126.3 21.4 %all-to-all-start.6 = ((bf16[16,40,512]{2,1,0:T(8,128)(2,1)}), bf16[16,40,512]{2,1,0:T(8,128)(2,1)S(1)}, u32[]{:S(2)}, u32[]{:S(2)}) async-start(bf16[16,40,512]{2,1,0:T(8,128)(2,1)} %broadcast_select_fusion.8), calls=%async_computation.6 | async-start | bytes 1310720 | tf_op jit(solution)/shard_map/all_to_all | solution.py:109
  147.7 21.4 %all-to-all-start.7 = ((bf16[16,40,512]{2,1,0:T(8,128)(2,1)}), bf16[16,40,512]{2,1,0:T(8,128)(2,1)S(1)}, u32[]{:S(2)}, u32[]{:S(2)}) async-start(bf16[16,40,512]{2,1,0:T(8,128)(2,1)} %broadcast_select_fusion.6), calls=%async_computation.7 | async-start | bytes 1310720 | tf_op jit(solution)/shard_map/all_to_all | solution.py:116
  186.9 21.4 %all-to-all-start.8 = ((bf16[16,40,512]{2,1,0:T(8,128)(2,1)}), bf16[16,40,512]{2,1,0:T(8,128)(2,1)S(1)}, u32[]{:S(2)}, u32[]{:S(2)}) async-start(bf16[16,40,512]{2,1,0:T(8,128)(2,1)} %broadcast_select_fusion.4), calls=%async_computation.8 | async-start | bytes 1310720 | tf_op jit(solution)/shard_map/all_to_all | solution.py:150
  191.6 17.1 %copy-start.25 = (s32[768]{0:T(1024)S(1)}, s32[768]{0:T(1024)}, u32[]{:S(2)}) copy-start(s32[768]{0:T(1024)} %param.29) | copy-start | bytes 9220
  191.6 17.1 %copy-start.46 = (f32[1,512]{1,0:T(1,128)S(1)}, f32[1,512]{1,0:T(1,128)}, u32[]{:S(2)}) copy-start(f32[1,512]{1,0:T(1,128)} %get-tuple-element.22) | copy-start | bytes 6148
  (32 other events, 111.3 us)
where the time goes:
time: 214 us; the launch traced here: 213 us
  waiting for transfers between devices  54.9 us (26%)
  local copies, waits for them, and re-layouts  49.9 us (23%)
  starting transfers between devices  47 us (22%)
  matrix products  32.5 us (15%)
  other arithmetic  26.6 us (12%)
    all_to_all x2, waiting for transfers between devices, body(): lax.all_to_all(outgoing, 'patch', split_axis=0, concat_axis=0, tiled=True)  23.8 us
    all_to_all x2, waiting for transfers between devices, serve(): lax.all_to_all(jnp.take(current, wanted_recv, axis=0), 'patch', split_axi...  14.6 us
    all_to_all x2, waiting for transfers between devices, serve(): lax.all_to_all(jnp.take(current, wanted_send, axis=0), 'patch', split_axi...  14.3 us
    all_to_all x2, starting transfers between devices, body(): lax.all_to_all(outgoing, 'patch', split_axis=0, concat_axis=0, tiled=True)  10.9 us
    all_to_all x2, starting transfers between devices, serve(): lax.all_to_all(jnp.take(current, wanted_send, axis=0), 'patch', split_axi...  9.54 us
    dot_general x2, matrix products, edge_update(): jnp.dot(hidden, w_out, preferred_element_type=jnp.float32)  9.35 us
    all_to_all x2, starting transfers between devices, serve(): lax.all_to_all(jnp.take(current, wanted_recv, axis=0), 'patch', split_axi...  8.41 us
    all_to_all x1, starting transfers between devices, body(): lax.all_to_all(recv_requests, 'patch', split_axis=0, concat_axis=0, tiled...  7.36 us
  transfers between devices with their start and end apart: 9, of which 7 were waited for; matrix products, arithmetic and copies ran while one was open for 34% of the time, Pallas kernels for 0%

commit v1 on v0

v1 whole, which is shorter than its diff:
```python
import functools

import jax
import jax.numpy as jnp
from jax import lax
from jax.experimental import pallas as pl
from jax.experimental.pallas import tpu as pltpu
from jax.sharding import PartitionSpec as P

COARSE = 64
PLANE = 4
BF = jnp.bfloat16
F32 = jnp.float32
I32 = jnp.int32


def mm(left, right):
    return jnp.dot(left, right, preferred_element_type=F32)


def silu(values):
    half = 0.5 * values
    return half * jnp.tanh(half) + half


def layer_norm(values, gain, shift):
    mean_value = jnp.mean(values, axis=-1, keepdims=True)
    centred = values - mean_value
    variance = jnp.mean(centred * centred, axis=-1, keepdims=True)
    return centred * lax.rsqrt(variance + 1e-05) * gain + shift


def match_rows(column, count, offset=0):
    where = lax.broadcasted_iota(I32, (column.shape[0], count), 1) + offset
    return jnp.where(where == column, 1.0, 0.0).astype(BF)


def match_columns(row, count, offset=0):
    where = lax.broadcasted_iota(I32, (count, row.shape[1]), 0) + offset
    return jnp.where(where == row, 1.0, 0.0).astype(BF)


def as_column(row):
    tall = jnp.broadcast_to(row.astype(F32), (8, row.shape[1]))
    return jnp.transpose(tall)[:, :1].astype(I32)


def bits(count):
    assert count & (count - 1) == 0
    return count.bit_length() - 1


def prep_kernel(node_count, lines, slot, own_ref, fs_ref, fr_ref, fe_ref, pos_ref, *slot_refs):
    own = own_ref[0]
    own_q, own_z = own & (PLANE - 1), lax.shift_right_logical(own, bits(PLANE))
    fs, fr = fs_ref[...], fr_ref[...]
    count = fs.shape[1]
    shift = bits(node_count)
    s_patch, s_within = lax.shift_right_logical(fs, shift), fs & (node_count - 1)
    r_patch, r_within = lax.shift_right_logical(fr, shift), fr & (node_count - 1)
    r_q = r_patch & (PLANE - 1)
    member = r_q ^ own_q
    s_rel = s_patch ^ (own_z * PLANE + r_q)
    s_z = lax.shift_right_logical(s_rel, bits(PLANE))
    s_block = (s_rel & (PLANE - 1)) * lines + (s_z ^ lax.shift_right_logical(s_z, 1))
    r_z = lax.shift_right_logical(r_patch, bits(PLANE)) ^ own_z
    r_block = (r_z ^ lax.shift_right_logical(r_z, 1)) + 1
    flags = jnp.where(lax.broadcasted_iota(I32, (8, count), 0) == member, 1.0, 0.0)
    before = jnp.where(
        lax.broadcasted_iota(I32, (count, count), 0) < lax.broadcasted_iota(I32, (count, count), 1),
        1.0,
        0.0,
    ).astype(BF)
    rank = jnp.sum(flags * mm(flags.astype(BF), before), axis=0, keepdims=True)
    pos = member * slot + rank.astype(I32)
    pos_ref[...] = pos
    row_at = lax.broadcasted_iota(I32, (8, count), 0)
    meta = jnp.where(row_at == 0, s_block, 0)
    meta = jnp.where(row_at == 1, s_within, meta)
    meta = jnp.where(row_at == 2, r_block, meta)
    meta = jnp.where(row_at == 3, r_within, meta).astype(F32).astype(BF)
    for m, ref in enumerate(slot_refs):
        moved = match_columns(pos - m * slot, slot)
        ref[0:slot, :] = mm(moved, fe_ref[...]).astype(BF)
        tail = lax.dot_general(meta, moved, (((1,), (1,)), ((), ())), preferred_element_type=F32)
        ref[slot:, :] = jnp.zeros((ref.shape[0] - slot, ref.shape[1]), BF)
        ref[slot : slot + 16, 0:slot] = jnp.concatenate(
            [tail, jnp.zeros((8, slot), F32)], axis=0
        ).astype(BF)


def edge_mlp(edges, senders, receivers, w_in, w_out, vec_ref):
    stacked = jnp.concatenate([edges, senders, receivers], axis=1)
    hidden = silu(mm(stacked, w_in) + vec_ref[0:1, :]).astype(BF)
    return layer_norm(mm(hidden, w_out), vec_ref[1:2, :], vec_ref[2:3, :])


def local_kernel(
    block, nodes_ref, edges_ref, send_ref, recv_ref, win_ref, wout_ref, vec_ref, new_ref, sum_ref
):
    node_count = nodes_ref.shape[0]
    nodes = nodes_ref[...]
    for i in range(edges_ref.shape[0] // block):
        rows = slice(i * block, (i + 1) * block)
        send, recv = send_ref[:, rows], recv_ref[:, rows]
        edges = edges_ref[rows, :]
        normed = edge_mlp(
            edges,
            mm(match_rows(as_column(send), node_count), nodes).astype(BF),
            mm(match_rows(as_column(recv), node_count), nodes).astype(BF),
            win_ref[...],
            wout_ref[...],
            vec_ref,
        )
        new_ref[rows, :] = (edges.astype(F32) + normed).astype(BF)
        part = mm(match_columns(recv, node_count), normed.astype(BF))
        if i == 0:
            sum_ref[...] = part
        else:
            sum_ref[...] += part


def far_kernel(lines, slot, *refs):
    slots, tables = refs[0:PLANE], refs[PLANE : 2 * PLANE]
    win_ref, wout_ref, vec_ref = refs[2 * PLANE : 2 * PLANE + 3]
    outs = refs[2 * PLANE + 3 :]
    new_refs, own_ref, part_refs = outs[0:PLANE], outs[PLANE], outs[PLANE + 1 :]
    span = lines * COARSE
    total = None
    for pair in range(0, PLANE, 2):
        columns_s, columns_r, rows_r = [], [], []
        for ref in slots[pair : pair + 2]:
            meta = ref[slot : slot + 16, :].astype(F32)[0:8, 0 : -(-slot // 128) * 128]
            tall = jnp.transpose(meta)[0:slot, :]
            columns_s.append((tall[:, 0:1] * COARSE + tall[:, 1:2]).astype(I32))
            columns_r.append((tall[:, 2:3] * COARSE + tall[:, 3:4]).astype(I32) - COARSE)
            rows_r.append((meta[2:3, 0:slot] * COARSE + meta[3:4, 0:slot]).astype(I32) - COARSE)
        column_s, column_r = jnp.concatenate(columns_s, axis=0), jnp.concatenate(columns_r, axis=0)
        senders = None
        for q, table in enumerate(tables):
            piece = mm(match_rows(column_s, span, q * span), table[...])
            senders = piece if senders is None else senders + piece
        receivers = mm(match_rows(column_r, span), tables[0][...])
        edges = jnp.concatenate([ref[0:slot, :] for ref in slots[pair : pair + 2]], axis=0)
        normed = edge_mlp(
            edges, senders.astype(BF), receivers.astype(BF), win_ref[...], wout_ref[...], vec_ref
        )
        new = (edges.astype(F32) + normed).astype(BF)
        message = normed.astype(BF)
        for i in range(2):
            new_refs[pair + i][0:slot, :] = new[i * slot : (i + 1) * slot, :]
            new_refs[pair + i][slot:, :] = slots[pair + i][slot:, :]
            part = mm(match_columns(rows_r[i], span), message[i * slot : (i + 1) * slot, :])
            total = part if total is None else total + part
    own_ref[...] = total[0:COARSE, :]
    for i, ref in enumerate(part_refs):
        ref[...] = total[(i + 1) * COARSE : (i + 2) * COARSE, :].astype(BF)


def node_kernel(nodes_ref, sum_ref, own_ref, *refs):
    part_refs, (win_ref, wout_ref, vec_ref), outs = refs[:-5], refs[-5:-2], refs[-2:]
    far = own_ref[...]
    for ref in part_refs:
        far = far + ref[...].astype(F32)
    sums = jnp.concatenate([sum_ref[0:COARSE, :] + far, sum_ref[COARSE:, :]], axis=0).astype(BF)
    nodes = nodes_ref[...]
    stacked = jnp.concatenate([nodes, sums], axis=1)
    hidden = silu(mm(stacked, win_ref[...]) + vec_ref[0:1, :]).astype(BF)
    normed = layer_norm(mm(hidden, wout_ref[...]), vec_ref[1:2, :], vec_ref[2:3, :])
    new = (nodes.astype(F32) + normed).astype(BF)
    outs[0][...] = new
    outs[1][...] = new[0:COARSE, :]


def restore_kernel(slot, pos_ref, *refs):
    slots, out_ref = refs[:-1], refs[-1]
    column = as_column(pos_ref[...])
    total = None
    for m, ref in enumerate(slots):
        piece = mm(match_rows(column - m * slot, slot), ref[0:slot, :])
        total = piece if total is None else total + piece
    out_ref[...] = total.astype(BF)


def call(kernel, outs, args, flops, limit, scalars=0):
    bytes_accessed = sum(a.size * a.dtype.itemsize for a in args)
    bytes_accessed += sum(o.size * o.dtype.itemsize for o in outs)
    specs = [pl.BlockSpec(memory_space=pltpu.SMEM)] * scalars
    specs += [pl.BlockSpec(memory_space=pltpu.VMEM)] * (len(args) - scalars)
    return pl.pallas_call(
        kernel,
        out_shape=outs,
        in_specs=specs,
        out_specs=[pl.BlockSpec(memory_space=pltpu.VMEM)] * len(outs),
        compiler_params=pltpu.CompilerParams(vmem_limit_bytes=limit),
        cost_estimate=pl.CostEstimate(flops=flops, bytes_accessed=bytes_accessed, transcendentals=0),
    )(*args)


def body(
    node_feat,
    local_edges,
    far_edges,
    local_send,
    local_recv,
    far_send,
    far_recv,
    edge_in,
    edge_out,
    node_in,
    node_out,
    edge_bias,
    edge_gain,
    edge_shift,
    node_bias,
    node_gain,
    node_shift,
):
    devices = lax.axis_size("patch")
    lines = devices // PLANE
    node_count, width = node_feat.shape
    far_count, local_count = far_edges.shape[0], local_edges.shape[0]
    slot = lines * (5 * far_count // (2 * devices))
    padded = -(-(slot + 4) // 16) * 16
    layers = edge_in.shape[0]
    limit = (24 if lines <= 4 else 56) * 2**20
    shape = jax.ShapeDtypeStruct
    place = [0] * lines
    for z in range(lines):
        place[z ^ (z >> 1)] = z

    def swap(values, distance):
        return lax.ppermute(values, "patch", [(i, i ^ distance) for i in range(devices)])

    def gather(own):
        if lines == 4:
            z3, z1 = swap(own, 12), swap(own, 4)
            z2 = swap(z3, 4)
            first = jnp.concatenate([own, z1, z3], axis=0)
            table = jnp.concatenate([first, z2], axis=0)
            across = jnp.concatenate([swap(first, 2), swap(z2, 2)], axis=0)
        else:
            table = jnp.concatenate(
                [own if z == 0 else swap(own, PLANE * z) for z in place], axis=0
            )
            across = swap(table, 2)
        return (table, swap(table, 1), across, swap(across, 1))

    own = lax.axis_index("patch").reshape(1).astype(I32)
    fs, fr = far_send.reshape(1, -1), far_recv.reshape(1, -1)
    ls, lr = local_send.reshape(1, -1), local_recv.reshape(1, -1)
    prepared = call(
        functools.partial(prep_kernel, node_count, lines, slot),
        [shape((1, far_count), I32)] + [shape((padded, width), BF)] * PLANE,
        [own, fs, fr, far_edges],
        2 * PLANE * slot * far_count * width,
        limit,
        scalars=1,
    )
    pos, slots = prepared[0], prepared[1:]
    slots = [slots[0]] + [swap(slots[m], m) for m in range(1, PLANE)]
    nodes, coarse, local = node_feat, node_feat[:COARSE], local_edges
    for l in range(layers):
        edge_vec = jnp.stack([edge_bias[l], edge_gain[l], edge_shift[l]])
        node_vec = jnp.stack([node_bias[l], node_gain[l], node_shift[l]])
        tables = gather(coarse)
        far_rows = PLANE * slot
        far = call(
            functools.partial(far_kernel, lines, slot),
            [shape((padded, width), BF)] * PLANE
            + [shape((COARSE, width), F32)]
            + [shape((COARSE, width), BF)] * (lines - 1),
            [*slots, *tables, edge_in[l], edge_out[l], edge_vec],
            2 * far_rows * width * (6 * lines * COARSE + 4 * width),
            limit,
        )
        slots = far[:PLANE]
        parts = [swap(v, PLANE * place[i + 1]) for i, v in enumerate(far[PLANE + 1 :])]
        local, sums = call(
            functools.partial(local_kernel, min(local_count, 256)),
            [shape((local_count, width), BF), shape((node_count, width), F32)],
            [nodes, local, ls, lr, edge_in[l], edge_out[l], edge_vec],
            2 * local_count * width * (3 * node_count + 4 * width),
            limit,
        )
        nodes, coarse = call(
            node_kernel,
            [shape((node_count, width), BF), shape((COARSE, width), BF)],
            [nodes, sums, far[PLANE], *parts, node_in[l], node_out[l], node_vec],
            2 * node_count * width * 3 * width,
            limit,
        )
    slots = [slots[0]] + [swap(slots[m], m) for m in range(1, PLANE)]
    far_out = call(
        functools.partial(restore_kernel, slot),
        [shape((far_count, width), BF)],
        [pos, *slots],
        2 * PLANE * slot * far_count * width,
        limit,
    )[0]
    return (nodes, local, far_out)


def solution(mesh):
    split = P(("groups", "patch"), None)
    line = P(("groups", "patch"))
    return jax.shard_map(
        body,
        mesh=mesh,
        in_specs=(split,) * 3 + (line,) * 4 + (P(),) * 10,
        out_specs=(split,) * 3,
        check_vma=False,
    )
```

time: 214 us -> 86.6 us (0.40)
  local copies, waits for them, and re-layouts: 49.9 us -> 8.85 us
  matrix products: 32.5 us -> 0 us
  waiting for transfers between devices: 54.9 us -> 26.5 us
  other arithmetic: 26.6 us -> 0.09 us
  Pallas kernels: 0 us -> 22.3 us
  starting transfers between devices: 47 us -> 27.5 us
    all_to_all x9 -> x0, waiting for transfers between devices: 54.9 us -> none  [the longest x2 23.8 us: body(): lax.all_to_all(outgoing, 'patch', split_axis=0, concat_axis=0, tiled=True)]
    all_to_all x9 -> x0, starting transfers between devices: 47 us -> none  [the longest x2 10.9 us: body(): lax.all_to_all(outgoing, 'patch', split_axis=0, concat_axis=0, tiled=True)]
    gather x14 -> x0, local copies, waits for them, and re-layouts: 33.8 us -> none  [the longest x2 6.02 us: body(): jnp.take(nodes, local_recv, axis=0)]
    dot_general x14 -> x0, matrix products: 32.5 us -> none  [the longest x2 9.35 us: edge_update(): jnp.dot(hidden, w_out, preferred_element_type=jnp.float32)]
    ppermute x0 -> x26, starting transfers between devices: none -> 27.5 us  [swap(): lax.ppermute(values, 'patch', [(i, i ^ distance) for i in range(devices)])]
    ppermute x0 -> x26, waiting for transfers between devices: none -> 26.5 us  [swap(): lax.ppermute(values, 'patch', [(i, i ^ distance) for i in range(devices)])]
    pallas_call x0 -> x8, Pallas kernels: none -> 22.3 us  [call(): pl.pallas_call(kernel, out_shape=outs, in_specs=specs, out_specs=[pl.Bloc...]
    select_n x23 -> x0, other arithmetic: 15.5 us -> none  [the longest x3 4.14 us: body(): jnp.take(nodes, local_send, axis=0)]
  transfers between devices with their start and end apart: 9 -> 26, of which waited for: 7 -> 12; matrix products, arithmetic and copies ran while one was open for 34% -> 3% of each run, Pallas kernels for 0% -> 13%
where the time goes in v1:
time: 86.6 us; the launch traced here: 86.3 us
  starting transfers between devices  27.5 us (32%)
  waiting for transfers between devices  26.5 us (31%)
  Pallas kernels  22.3 us (26%)
  local copies, waits for them, and re-layouts  8.85 us (10%)
  between operations  1.01 us (1%)
    ppermute x26, starting transfers between devices, swap(): lax.ppermute(values, 'patch', [(i, i ^ distance) for i in range(devices)])  27.5 us
    ppermute x26, waiting for transfers between devices, swap(): lax.ppermute(values, 'patch', [(i, i ^ distance) for i in range(devices)])  26.5 us
    pallas_call x8, Pallas kernels, call(): pl.pallas_call(kernel, out_shape=outs, in_specs=specs, out_specs=[pl.Bloc...  22.3 us
    unnamed x37, local copies, waits for them, and re-layouts  5.56 us
    squeeze x1, local copies, waits for them, and re-layouts, body(): edge_in[l]  2.11 us
  transfers between devices with their start and end apart: 26, of which 12 were waited for; matrix products, arithmetic and copies ran while one was open for 3% of the time, Pallas kernels for 13%

profile of v1, /device:TPU:0, one launch (start us, length us, event | category | flops | bytes accessed | tf_op | source)
XLA Modules:
  0.0 86.3 jit_solution(8292661791736458987)
XLA Ops:
  1.5 5.0 %collective-permute-start.4 = (bf16[64,512]{1,0:T(8,128)(2,1)S(1)}, bf16[64,512]{1,0:T(8,128)(2,1)S(1)}, u32[]{:S(2)}, u32[]{:S(2)}) collective-permute-start(bf16[64,512]{1,0:T(8,128)(2,1)S(1)} %slice.72), channel_id=1, source_target_pairs={{0,12},{1,13},{2,14},{3,15},{4,8},{5,9},{6,10},{7,11},{8,4},{9,5},... | collective-permute-start | bytes 196616 | tf_op jit(solution)/shard_map/ppermute | solution.py:233
  9.5 1.6 %collective-permute-start.1 = (bf16[176,512]{1,0:T(8,128)(2,1)S(1)}, bf16[176,512]{1,0:T(8,128)(2,1)S(1)}, u32[]{:S(2)}, u32[]{:S(2)}) collective-permute-start(bf16[176,512]{1,0:T(8,128)(2,1)S(1)} %get-tuple-element.34), channel_id=1, source_target_pairs={{0,2},{1,3},{2,0},{3,1},{4,6},{5,7},{6,4},{7,5},{8,10},{9,11},{10,... | collective-permute-start | bytes 540680 | tf_op jit(solution)/shard_map/ppermute | solution.py:233
  11.3 2.1 %slice_bitcast_fusion = (bf16[1536,512]{1,0:T(8,128)(2,1)S(1)}, bf16[1536,512]{1,0:T(8,128)(2,1)S(1)}) fusion(bf16[2,1536,512]{2,1,0:T(8,128)(2,1)} %param.24), kind=kLoop, calls=%fused_computation | loop fusion | bytes 6291456 | tf_op jit(solution)/shard_map/squeeze | solution.py:282
  13.5 1.5 %copy-done.5 = bf16[2,1024,512]{2,1,0:T(8,128)(2,1)S(1)} copy-done((bf16[2,1024,512]{2,1,0:T(8,128)(2,1)S(1)}, bf16[2,1024,512]{2,1,0:T(8,128)(2,1)}, u32[]{:S(2)}) %copy-start.5) | copy-done | bytes 2097176
  17.1 1.5 %collective-permute-start.7 = (bf16[192,512]{1,0:T(8,128)(2,1)S(1)}, bf16[192,512]{1,0:T(8,128)(2,1)S(1)}, u32[]{:S(2)}, u32[]{:S(2)}) collective-permute-start(bf16[192,512]{1,0:T(8,128)(2,1)S(1)} %pad_maximum_fusion.1), channel_id=1, source_target_pairs={{0,2},{1,3},{2,0},{3,1},{4,6},{5,7},{6,4},{7,5},{8,10},{9,11},{10,... | collective-permute-start | bytes 589832 | tf_op jit(solution)/shard_map/ppermute | solution.py:233
  18.6 2.0 %collective-permute-start.5 = (bf16[64,512]{1,0:T(8,128)(2,1)S(1)}, bf16[64,512]{1,0:T(8,128)(2,1)S(1)}, u32[]{:S(2)}, u32[]{:S(2)}) collective-permute-start(bf16[64,512]{1,0:T(8,128)(2,1)S(1)} %collective-permute-done.4), channel_id=1, source_target_pairs={{0,4},{1,5},{2,6},{3,7},{4,0},{5,1},{6,2},{7,3},{8,12},{9,13},{10,... | collective-permute-start | bytes 196616 | tf_op jit(solution)/shard_map/ppermute | solution.py:233
  20.6 2.3 %collective-permute-done.5 = bf16[64,512]{1,0:T(8,128)(2,1)S(1)} collective-permute-done((bf16[64,512]{1,0:T(8,128)(2,1)S(1)}, bf16[64,512]{1,0:T(8,128)(2,1)S(1)}, u32[]{:S(2)}, u32[]{:S(2)}) %collective-permute-start.5) | collective-permute-done | bytes 65568 | tf_op jit(solution)/shard_map/ppermute | solution.py:233
  26.0 2.8 %collective-permute-done.8 = bf16[64,512]{1,0:T(8,128)(2,1)S(1)} collective-permute-done((bf16[64,512]{1,0:T(8,128)(2,1)S(1)}, bf16[64,512]{1,0:T(8,128)(2,1)S(1)}, u32[]{:S(2)}, u32[]{:S(2)}) %collective-permute-start.8) | collective-permute-done | bytes 65568 | tf_op jit(solution)/shard_map/ppermute | solution.py:233
  28.9 4.4 %shard_map.184 = (bf16[768,512]{1,0:T(8,128)(2,1)S(1)}, f32[256,512]{1,0:T(8,128)S(1)}) custom-call(bf16[256,512]{1,0:T(8,128)(2,1)S(1)} %copy-done, bf16[768,512]{1,0:T(8,128)(2,1)S(1)} %copy-done.1, s32[1,768]{1,0:T(1,128)S(1)} %reshape.21.send_ref, s32[1,768]{1,0:T(1,128)S(1)} %reshape.22.recv_ref, ...), custom_call_target="tpu_custom_call" | custom-call | flops 2214592512 | bytes 4468736 | tf_op jit(solution)/shard_map/pallas_call | solution.py:190
  33.3 4.2 %shard_map.186 = (bf16[176,512]{1,0:T(8,128)(2,1)S(1)}, bf16[176,512]{1,0:T(8,128)(2,1)S(1)}, bf16[176,512]{1,0:T(8,128)(2,1)S(1)}, bf16[176,512]{1,0:T(8,128)(2...) custom-call(bf16[176,512]{1,0:T(8,128)(2,1)S(1)} %get-tuple-element., ...), custom_call_target="tpu_custom_call" | custom-call | flops 2348810240 | bytes 4921344 | tf_op jit(solution)/shard_map/pallas_call | solution.py:190
  37.6 2.1 %collective-permute-start.10 = (bf16[64,512]{1,0:T(8,128)(2,1)S(1)}, bf16[64,512]{1,0:T(8,128)(2,1)S(1)}, u32[]{:S(2)}, u32[]{:S(2)}) collective-permute-start(bf16[64,512]{1,0:T(8,128)(2,1)S(1)} %get-tuple-element.37), channel_id=1, source_target_pairs={{0,4},{1,5},{2,6},{3,7},{4,0},{5,1},{6,2},{7,3},{8,12},{9,13},{10,... | collective-permute-start | bytes 196616 | tf_op jit(solution)/shard_map/ppermute | solution.py:233
  39.7 1.5 %collective-permute-start.12 = (bf16[64,512]{1,0:T(8,128)(2,1)S(1)}, bf16[64,512]{1,0:T(8,128)(2,1)S(1)}, u32[]{:S(2)}, u32[]{:S(2)}) collective-permute-start(bf16[64,512]{1,0:T(8,128)(2,1)S(1)} %get-tuple-element.39), channel_id=1, source_target_pairs={{0,8},{1,9},{2,10},{3,11},{4,12},{5,13},{6,14},{7,15},{8,0},{9,1},... | collective-permute-start | bytes 196616 | tf_op jit(solution)/shard_map/ppermute | solution.py:233
  42.4 4.1 %collective-permute-done.11.refs_1_ = bf16[64,512]{1,0:T(8,128)(2,1)S(1)} collective-permute-done((bf16[64,512]{1,0:T(8,128)(2,1)S(1)}, bf16[64,512]{1,0:T(8,128)(2,1)S(1)}, u32[]{:S(2)}, u32[]{:S(2)}) %collective-permute-start.11) | collective-permute-done | bytes 65568 | tf_op jit(solution)/shard_map/ppermute | solution.py:233
  48.9 2.3 %collective-permute-start.14 = (bf16[64,512]{1,0:T(8,128)(2,1)S(1)}, bf16[64,512]{1,0:T(8,128)(2,1)S(1)}, u32[]{:S(2)}, u32[]{:S(2)}) collective-permute-start(bf16[64,512]{1,0:T(8,128)(2,1)S(1)} %get-tuple-element.47), channel_id=1, source_target_pairs={{0,12},{1,13},{2,14},{3,15},{4,8},{5,9},{6,10},{7,11},{8,4},{9,5},... | collective-permute-start | bytes 196616 | tf_op jit(solution)/shard_map/ppermute | solution.py:233
  51.2 1.9 %collective-permute-done.13 = bf16[64,512]{1,0:T(8,128)(2,1)S(1)} collective-permute-done((bf16[64,512]{1,0:T(8,128)(2,1)S(1)}, bf16[64,512]{1,0:T(8,128)(2,1)S(1)}, u32[]{:S(2)}, u32[]{:S(2)}) %collective-permute-start.13) | collective-permute-done | bytes 65568 | tf_op jit(solution)/shard_map/ppermute | solution.py:233
  53.2 1.9 %collective-permute-done.14 = bf16[64,512]{1,0:T(8,128)(2,1)S(1)} collective-permute-done((bf16[64,512]{1,0:T(8,128)(2,1)S(1)}, bf16[64,512]{1,0:T(8,128)(2,1)S(1)}, u32[]{:S(2)}, u32[]{:S(2)}) %collective-permute-start.14) | collective-permute-done | bytes 65568 | tf_op jit(solution)/shard_map/ppermute | solution.py:233
  55.1 1.5 %collective-permute-start.17 = (bf16[192,512]{1,0:T(8,128)(2,1)S(1)}, bf16[192,512]{1,0:T(8,128)(2,1)S(1)}, u32[]{:S(2)}, u32[]{:S(2)}) collective-permute-start(bf16[192,512]{1,0:T(8,128)(2,1)S(1)} %pad_maximum_fusion.2), channel_id=1, source_target_pairs={{0,2},{1,3},{2,0},{3,1},{4,6},{5,7},{6,4},{7,5},{8,10},{9,11},{10,... | collective-permute-start | bytes 589832 | tf_op jit(solution)/shard_map/ppermute | solution.py:233
  57.6 3.3 %collective-permute-done.15 = bf16[64,512]{1,0:T(8,128)(2,1)S(1)} collective-permute-done((bf16[64,512]{1,0:T(8,128)(2,1)S(1)}, bf16[64,512]{1,0:T(8,128)(2,1)S(1)}, u32[]{:S(2)}, u32[]{:S(2)}) %collective-permute-start.15) | collective-permute-done | bytes 65568 | tf_op jit(solution)/shard_map/ppermute | solution.py:233
  61.6 3.9 %collective-permute-done.18 = bf16[64,512]{1,0:T(8,128)(2,1)S(1)} collective-permute-done((bf16[64,512]{1,0:T(8,128)(2,1)S(1)}, bf16[64,512]{1,0:T(8,128)(2,1)S(1)}, u32[]{:S(2)}, u32[]{:S(2)}) %collective-permute-start.18) | collective-permute-done | bytes 65568 | tf_op jit(solution)/shard_map/ppermute | solution.py:233
  65.5 1.5 %collective-permute-done.19.refs_7_ = bf16[256,512]{1,0:T(8,128)(2,1)S(1)} collective-permute-done((bf16[256,512]{1,0:T(8,128)(2,1)S(1)}, bf16[256,512]{1,0:T(8,128)(2,1)S(1)}, u32[]{:S(2)}, u32[]{:S(2)}) %collective-permute-start.19) | collective-permute-done | bytes 262176 | tf_op jit(solution)/shard_map/ppermute | solution.py:233
  67.0 4.2 %shard_map.189 = (bf16[176,512]{1,0:T(8,128)(2,1)S(1)}, bf16[176,512]{1,0:T(8,128)(2,1)S(1)}, bf16[176,512]{1,0:T(8,128)(2,1)S(1)}, bf16[176,512]{1,0:T(8,128)(2...) custom-call(bf16[176,512]{1,0:T(8,128)(2,1)S(1)} %get-tuple-element., ...), custom_call_target="tpu_custom_call" | custom-call | flops 2348810240 | bytes 4921344 | tf_op jit(solution)/shard_map/pallas_call | solution.py:190
  74.4 2.3 %collective-permute-start.21 = (bf16[64,512]{1,0:T(8,128)(2,1)S(1)}, bf16[64,512]{1,0:T(8,128)(2,1)S(1)}, u32[]{:S(2)}, u32[]{:S(2)}) collective-permute-start(bf16[64,512]{1,0:T(8,128)(2,1)S(1)} %get-tuple-element.50), channel_id=1, source_target_pairs={{0,12},{1,13},{2,14},{3,15},{4,8},{5,9},{6,10},{7,11},{8,4},{9,5},... | collective-permute-start | bytes 196616 | tf_op jit(solution)/shard_map/ppermute | solution.py:233
  77.5 5.1 %shard_map.188 = (bf16[768,512]{1,0:T(8,128)(2,1)}, f32[256,512]{1,0:T(8,128)S(1)}) custom-call(bf16[256,512]{1,0:T(8,128)(2,1)S(1)} %get-tuple-element.40.nodes_ref, bf16[768,512]{1,0:T(8,128)(2,1)S(1)} %get-tuple-element.41.edges_ref, s32[1,768]{1,0:T(1,128)S(1)} %reshape.21.send_ref, s32[1,768]{1,0:T(1,128)S(1)} %reshape.22.recv_ref, ...), custom_call_target="tpu_custom_call" | custom-call | flops 2214592512 | bytes 4468736 | tf_op jit(solution)/shard_map/pallas_call | solution.py:190
  83.4 1.6 %shard_map.190 = (bf16[256,512]{1,0:T(8,128)(2,1)}, bf16[64,512]{1,0:T(8,128)(2,1)}) custom-call(bf16[256,512]{1,0:T(8,128)(2,1)S(1)} %get-tuple-element.40.nodes_ref, f32[256,512]{1,0:T(8,128)S(1)} %get-tuple-element.42.sum_ref, f32[64,512]{1,0:T(8,128)S(1)} %get-tuple-element.48.own_ref, bf16[64,512]{1,0:T(8,128)(2,1)S(1)} %collective-permute-done.20.refs_0_, ...), custom_call_target="tpu_custom_call" | custom-call | flops 402653184 | bytes 3020800 | tf_op jit(solution)/shard_map/pallas_call | solution.py:190
  (94 shorter events, 20.5 us)
Async XLA Ops:
  1.5 15.6 %collective-permute-start.4 = (bf16[64,512]{1,0:T(8,128)(2,1)S(1)}, bf16[64,512]{1,0:T(8,128)(2,1)S(1)}, u32[]{:S(2)}, u32[]{:S(2)}) collective-permute-start(bf16[64,512]{1,0:T(8,128)(2,1)S(1)} %slice.72), channel_id=1, source_target_pairs={{0,12},{1,13},{2,14},{3,15},{4,8},{5,9},{6,10},{7,11},{8,4},{9,5},... | collective-permute-start | bytes 196616 | tf_op jit(solution)/shard_map/ppermute | solution.py:233
  6.5 10.5 %collective-permute-start.3 = (bf16[64,512]{1,0:T(8,128)(2,1)S(1)}, bf16[64,512]{1,0:T(8,128)(2,1)S(1)}, u32[]{:S(2)}, u32[]{:S(2)}) collective-permute-start(bf16[64,512]{1,0:T(8,128)(2,1)S(1)} %slice.72), channel_id=1, source_target_pairs={{0,4},{1,5},{2,6},{3,7},{4,0},{5,1},{6,2},{7,3},{8,12},{9,13},{10,... | collective-permute-start | bytes 196616 | tf_op jit(solution)/shard_map/ppermute | solution.py:233
  9.4 23.9 %collective-permute-start = (bf16[176,512]{1,0:T(8,128)(2,1)S(1)}, bf16[176,512]{1,0:T(8,128)(2,1)S(1)}, u32[]{:S(2)}, u32[]{:S(2)}) collective-permute-start(bf16[176,512]{1,0:T(8,128)(2,1)S(1)} %get-tuple-element.33), channel_id=1, source_target_pairs={{0,1},{1,0},{2,3},{3,2},{4,5},{5,4},{6,7},{7,6},{8,9},{9,8},{10,11... | collective-permute-start | bytes 540680 | tf_op jit(solution)/shard_map/ppermute | solution.py:233
  9.5 23.8 %collective-permute-start.1 = (bf16[176,512]{1,0:T(8,128)(2,1)S(1)}, bf16[176,512]{1,0:T(8,128)(2,1)S(1)}, u32[]{:S(2)}, u32[]{:S(2)}) collective-permute-start(bf16[176,512]{1,0:T(8,128)(2,1)S(1)} %get-tuple-element.34), channel_id=1, source_target_pairs={{0,2},{1,3},{2,0},{3,1},{4,6},{5,7},{6,4},{7,5},{8,10},{9,11},{10,... | collective-permute-start | bytes 540680 | tf_op jit(solution)/shard_map/ppermute | solution.py:233
  11.0 22.3 %collective-permute-start.2 = (bf16[176,512]{1,0:T(8,128)(2,1)S(1)}, bf16[176,512]{1,0:T(8,128)(2,1)S(1)}, u32[]{:S(2)}, u32[]{:S(2)}) collective-permute-start(bf16[176,512]{1,0:T(8,128)(2,1)S(1)} %get-tuple-element.35), channel_id=1, source_target_pairs={{0,3},{1,2},{2,1},{3,0},{4,7},{5,6},{6,5},{7,4},{8,11},{9,10},{10,... | collective-permute-start | bytes 540680 | tf_op jit(solution)/shard_map/ppermute | solution.py:233
  17.1 7.4 %collective-permute-start.7 = (bf16[192,512]{1,0:T(8,128)(2,1)S(1)}, bf16[192,512]{1,0:T(8,128)(2,1)S(1)}, u32[]{:S(2)}, u32[]{:S(2)}) collective-permute-start(bf16[192,512]{1,0:T(8,128)(2,1)S(1)} %pad_maximum_fusion.1), channel_id=1, source_target_pairs={{0,2},{1,3},{2,0},{3,1},{4,6},{5,7},{6,4},{7,5},{8,10},{9,11},{10,... | collective-permute-start | bytes 589832 | tf_op jit(solution)/shard_map/ppermute | solution.py:233
  18.6 4.3 %collective-permute-start.5 = (bf16[64,512]{1,0:T(8,128)(2,1)S(1)}, bf16[64,512]{1,0:T(8,128)(2,1)S(1)}, u32[]{:S(2)}, u32[]{:S(2)}) collective-permute-start(bf16[64,512]{1,0:T(8,128)(2,1)S(1)} %collective-permute-done.4), channel_id=1, source_target_pairs={{0,4},{1,5},{2,6},{3,7},{4,0},{5,1},{6,2},{7,3},{8,12},{9,13},{10,... | collective-permute-start | bytes 196616 | tf_op jit(solution)/shard_map/ppermute | solution.py:233
  23.0 10.3 %collective-permute-start.6 = (bf16[256,512]{1,0:T(8,128)(2,1)S(1)}, bf16[256,512]{1,0:T(8,128)(2,1)S(1)}, u32[]{:S(2)}, u32[]{:S(2)}) collective-permute-start(bf16[256,512]{1,0:T(8,128)(2,1)S(1)} %pad_maximum_fusion.refs_4_), channel_id=1, source_target_pairs={{0,1},{1,0},{2,3},{3,2},{4,5},{5,4},{6,7},{7,6},{8,9},{9,8},{10,11... | collective-permute-start | bytes 786440 | tf_op jit(solution)/shard_map/ppermute | solution.py:233
  24.5 4.3 %collective-permute-start.8 = (bf16[64,512]{1,0:T(8,128)(2,1)S(1)}, bf16[64,512]{1,0:T(8,128)(2,1)S(1)}, u32[]{:S(2)}, u32[]{:S(2)}) collective-permute-start(bf16[64,512]{1,0:T(8,128)(2,1)S(1)} %collective-permute-done.5), channel_id=1, source_target_pairs={{0,2},{1,3},{2,0},{3,1},{4,6},{5,7},{6,4},{7,5},{8,10},{9,11},{10,... | collective-permute-start | bytes 196616 | tf_op jit(solution)/shard_map/ppermute | solution.py:233
  28.8 4.5 %collective-permute-start.9 = (bf16[256,512]{1,0:T(8,128)(2,1)S(1)}, bf16[256,512]{1,0:T(8,128)(2,1)S(1)}, u32[]{:S(2)}, u32[]{:S(2)}) collective-permute-start(bf16[256,512]{1,0:T(8,128)(2,1)S(1)} %constant_dynamic-update-slice_fusion.refs_6_), channel_id=1, source_target_pairs={{0,1},{1,0},{2,3},{3,2},{4,5},{5,4},{6,7},{7,6},{8,9},{9,8},{10,11... | collective-permute-start | bytes 786440 | tf_op jit(solution)/shard_map/ppermute | solution.py:233
  37.6 4.9 %collective-permute-start.10 = (bf16[64,512]{1,0:T(8,128)(2,1)S(1)}, bf16[64,512]{1,0:T(8,128)(2,1)S(1)}, u32[]{:S(2)}, u32[]{:S(2)}) collective-permute-start(bf16[64,512]{1,0:T(8,128)(2,1)S(1)} %get-tuple-element.37), channel_id=1, source_target_pairs={{0,4},{1,5},{2,6},{3,7},{4,0},{5,1},{6,2},{7,3},{8,12},{9,13},{10,... | collective-permute-start | bytes 196616 | tf_op jit(solution)/shard_map/ppermute | solution.py:233
  39.7 6.8 %collective-permute-start.11 = (bf16[64,512]{1,0:T(8,128)(2,1)S(1)}, bf16[64,512]{1,0:T(8,128)(2,1)S(1)}, u32[]{:S(2)}, u32[]{:S(2)}) collective-permute-start(bf16[64,512]{1,0:T(8,128)(2,1)S(1)} %get-tuple-element.38), channel_id=1, source_target_pairs={{0,12},{1,13},{2,14},{3,15},{4,8},{5,9},{6,10},{7,11},{8,4},{9,5},... | collective-permute-start | bytes 196616 | tf_op jit(solution)/shard_map/ppermute | solution.py:233
  39.7 8.2 %collective-permute-start.12 = (bf16[64,512]{1,0:T(8,128)(2,1)S(1)}, bf16[64,512]{1,0:T(8,128)(2,1)S(1)}, u32[]{:S(2)}, u32[]{:S(2)}) collective-permute-start(bf16[64,512]{1,0:T(8,128)(2,1)S(1)} %get-tuple-element.39), channel_id=1, source_target_pairs={{0,8},{1,9},{2,10},{3,11},{4,12},{5,13},{6,14},{7,15},{8,0},{9,1},... | collective-permute-start | bytes 196616 | tf_op jit(solution)/shard_map/ppermute | solution.py:233
  48.8 4.3 %collective-permute-start.13 = (bf16[64,512]{1,0:T(8,128)(2,1)S(1)}, bf16[64,512]{1,0:T(8,128)(2,1)S(1)}, u32[]{:S(2)}, u32[]{:S(2)}) collective-permute-start(bf16[64,512]{1,0:T(8,128)(2,1)S(1)} %get-tuple-element.47), channel_id=1, source_target_pairs={{0,4},{1,5},{2,6},{3,7},{4,0},{5,1},{6,2},{7,3},{8,12},{9,13},{10,... | collective-permute-start | bytes 196616 | tf_op jit(solution)/shard_map/ppermute | solution.py:233
  48.9 6.2 %collective-permute-start.14 = (bf16[64,512]{1,0:T(8,128)(2,1)S(1)}, bf16[64,512]{1,0:T(8,128)(2,1)S(1)}, u32[]{:S(2)}, u32[]{:S(2)}) collective-permute-start(bf16[64,512]{1,0:T(8,128)(2,1)S(1)} %get-tuple-element.47), channel_id=1, source_target_pairs={{0,12},{1,13},{2,14},{3,15},{4,8},{5,9},{6,10},{7,11},{8,4},{9,5},... | collective-permute-start | bytes 196616 | tf_op jit(solution)/shard_map/ppermute | solution.py:233
  55.1 6.4 %collective-permute-start.17 = (bf16[192,512]{1,0:T(8,128)(2,1)S(1)}, bf16[192,512]{1,0:T(8,128)(2,1)S(1)}, u32[]{:S(2)}, u32[]{:S(2)}) collective-permute-start(bf16[192,512]{1,0:T(8,128)(2,1)S(1)} %pad_maximum_fusion.2), channel_id=1, source_target_pairs={{0,2},{1,3},{2,0},{3,1},{4,6},{5,7},{6,4},{7,5},{8,10},{9,11},{10,... | collective-permute-start | bytes 589832 | tf_op jit(solution)/shard_map/ppermute | solution.py:233
  60.9 4.5 %collective-permute-start.16 = (bf16[256,512]{1,0:T(8,128)(2,1)S(1)}, bf16[256,512]{1,0:T(8,128)(2,1)S(1)}, u32[]{:S(2)}, u32[]{:S(2)}) collective-permute-start(bf16[256,512]{1,0:T(8,128)(2,1)S(1)} %constant_dynamic-update-slice_fusion.2.refs_4_), channel_id=1, source_target_pairs={{0,1},{1,0},{2,3},{3,2},{4,5},{5,4},{6,7},{7,6},{8,9},{9,8},{10,11... | collective-permute-start | bytes 786440 | tf_op jit(solution)/shard_map/ppermute | solution.py:233
  60.9 4.5 %collective-permute-start.18 = (bf16[64,512]{1,0:T(8,128)(2,1)S(1)}, bf16[64,512]{1,0:T(8,128)(2,1)S(1)}, u32[]{:S(2)}, u32[]{:S(2)}) collective-permute-start(bf16[64,512]{1,0:T(8,128)(2,1)S(1)} %collective-permute-done.15), channel_id=1, source_target_pairs={{0,2},{1,3},{2,0},{3,1},{4,6},{5,7},{6,4},{7,5},{8,10},{9,11},{10,... | collective-permute-start | bytes 196616 | tf_op jit(solution)/shard_map/ppermute | solution.py:233
  71.2 5.5 %collective-permute-start.20 = (bf16[64,512]{1,0:T(8,128)(2,1)S(1)}, bf16[64,512]{1,0:T(8,128)(2,1)S(1)}, u32[]{:S(2)}, u32[]{:S(2)}) collective-permute-start(bf16[64,512]{1,0:T(8,128)(2,1)S(1)} %get-tuple-element.49), channel_id=1, source_target_pairs={{0,4},{1,5},{2,6},{3,7},{4,0},{5,1},{6,2},{7,3},{8,12},{9,13},{10,... | collective-permute-start | bytes 196616 | tf_op jit(solution)/shard_map/ppermute | solution.py:233
  72.4 12.6 %collective-permute-start.23 = (bf16[176,512]{1,0:T(8,128)(2,1)S(1)}, bf16[176,512]{1,0:T(8,128)(2,1)S(1)}, u32[]{:S(2)}, u32[]{:S(2)}) collective-permute-start(bf16[176,512]{1,0:T(8,128)(2,1)S(1)} %get-tuple-element.56), channel_id=1, source_target_pairs={{0,1},{1,0},{2,3},{3,2},{4,5},{5,4},{6,7},{7,6},{8,9},{9,8},{10,11... | collective-permute-start | bytes 540680 | tf_op jit(solution)/shard_map/ppermute | solution.py:233
  72.5 12.5 %collective-permute-start.24 = (bf16[176,512]{1,0:T(8,128)(2,1)S(1)}, bf16[176,512]{1,0:T(8,128)(2,1)S(1)}, u32[]{:S(2)}, u32[]{:S(2)}) collective-permute-start(bf16[176,512]{1,0:T(8,128)(2,1)S(1)} %get-tuple-element.57), channel_id=1, source_target_pairs={{0,2},{1,3},{2,0},{3,1},{4,6},{5,7},{6,4},{7,5},{8,10},{9,11},{10,... | collective-permute-start | bytes 540680 | tf_op jit(solution)/shard_map/ppermute | solution.py:233
  73.2 11.8 %collective-permute-start.25 = (bf16[176,512]{1,0:T(8,128)(2,1)S(1)}, bf16[176,512]{1,0:T(8,128)(2,1)S(1)}, u32[]{:S(2)}, u32[]{:S(2)}) collective-permute-start(bf16[176,512]{1,0:T(8,128)(2,1)S(1)} %get-tuple-element.58), channel_id=1, source_target_pairs={{0,3},{1,2},{2,1},{3,0},{4,7},{5,6},{6,5},{7,4},{8,11},{9,10},{10,... | collective-permute-start | bytes 540680 | tf_op jit(solution)/shard_map/ppermute | solution.py:233
  74.4 8.2 %collective-permute-start.21 = (bf16[64,512]{1,0:T(8,128)(2,1)S(1)}, bf16[64,512]{1,0:T(8,128)(2,1)S(1)}, u32[]{:S(2)}, u32[]{:S(2)}) collective-permute-start(bf16[64,512]{1,0:T(8,128)(2,1)S(1)} %get-tuple-element.50), channel_id=1, source_target_pairs={{0,12},{1,13},{2,14},{3,15},{4,8},{5,9},{6,10},{7,11},{8,4},{9,5},... | collective-permute-start | bytes 196616 | tf_op jit(solution)/shard_map/ppermute | solution.py:233
  76.7 6.7 %collective-permute-start.22 = (bf16[64,512]{1,0:T(8,128)(2,1)S(1)}, bf16[64,512]{1,0:T(8,128)(2,1)S(1)}, u32[]{:S(2)}, u32[]{:S(2)}) collective-permute-start(bf16[64,512]{1,0:T(8,128)(2,1)S(1)} %get-tuple-element.51), channel_id=1, source_target_pairs={{0,8},{1,9},{2,10},{3,11},{4,12},{5,13},{6,14},{7,15},{8,0},{9,1},... | collective-permute-start | bytes 196616 | tf_op jit(solution)/shard_map/ppermute | solution.py:233
  (18 other events, 71.3 us)

commit v2 on v1

v2 whole, which is shorter than its diff:
```python
import functools

import jax
import jax.numpy as jnp
from jax import lax
from jax.experimental import pallas as pl
from jax.experimental.pallas import tpu as pltpu
from jax.sharding import PartitionSpec as P

COARSE = 64
PLANE = 4
BF = jnp.bfloat16
F32 = jnp.float32
I32 = jnp.int32


def mm(left, right):
    return jnp.dot(left, right, preferred_element_type=F32)


def silu(values):
    half = 0.5 * values
    return half * jnp.tanh(half) + half


def layer_norm(values, gain, shift):
    mean_value = jnp.mean(values, axis=-1, keepdims=True)
    centred = values - mean_value
    variance = jnp.mean(centred * centred, axis=-1, keepdims=True)
    return centred * lax.rsqrt(variance + 1e-05) * gain + shift


def match_rows(column, count, offset=0):
    where = lax.broadcasted_iota(I32, (column.shape[0], count), 1) + offset
    return jnp.where(where == column, 1.0, 0.0).astype(BF)


def match_columns(row, count, offset=0):
    where = lax.broadcasted_iota(I32, (count, row.shape[1]), 0) + offset
    return jnp.where(where == row, 1.0, 0.0).astype(BF)


def as_column(row):
    tall = jnp.broadcast_to(row.astype(F32), (8, row.shape[1]))
    return jnp.transpose(tall)[:, :1].astype(I32)


def bits(count):
    assert count & (count - 1) == 0
    return count.bit_length() - 1


def prep_kernel(node_count, lines, slot, own_ref, fs_hbm, fr_hbm, fe_hbm, nodes_hbm, *refs):
    pos_ref, coarse_ref, rest_ref, slot_refs = *refs[0:3], refs[3 : 3 + PLANE]
    fs_ref, fr_ref, fe_ref, sems = refs[3 + PLANE :]
    moves = [
        (fs_hbm, fs_ref),
        (fr_hbm, fr_ref),
        (fe_hbm, fe_ref),
        (nodes_hbm.at[0:COARSE, :], coarse_ref),
        (nodes_hbm.at[COARSE:, :], rest_ref),
    ]
    copies = [pltpu.make_async_copy(a, b, sems.at[i]) for i, (a, b) in enumerate(moves)]
    for copy in copies:
        copy.start()
    for copy in copies[0:3]:
        copy.wait()
    own = own_ref[0]
    own_q, own_z = own & (PLANE - 1), lax.shift_right_logical(own, bits(PLANE))
    fs, fr = fs_ref[...], fr_ref[...]
    count = fs.shape[1]
    shift = bits(node_count)
    s_patch, s_within = lax.shift_right_logical(fs, shift), fs & (node_count - 1)
    r_patch, r_within = lax.shift_right_logical(fr, shift), fr & (node_count - 1)
    r_q = r_patch & (PLANE - 1)
    member = r_q ^ own_q
    s_rel = s_patch ^ (own_z * PLANE + r_q)
    s_z = lax.shift_right_logical(s_rel, bits(PLANE))
    s_block = (s_rel & (PLANE - 1)) * lines + (s_z ^ lax.shift_right_logical(s_z, 1))
    r_z = lax.shift_right_logical(r_patch, bits(PLANE)) ^ own_z
    r_block = (r_z ^ lax.shift_right_logical(r_z, 1)) + 1
    flags = jnp.where(lax.broadcasted_iota(I32, (8, count), 0) == member, 1.0, 0.0)
    before = jnp.where(
        lax.broadcasted_iota(I32, (count, count), 0) < lax.broadcasted_iota(I32, (count, count), 1),
        1.0,
        0.0,
    ).astype(BF)
    rank = jnp.sum(flags * mm(flags.astype(BF), before), axis=0, keepdims=True)
    pos = member * slot + rank.astype(I32)
    pos_ref[...] = pos
    row_at = lax.broadcasted_iota(I32, (8, count), 0)
    meta = jnp.where(row_at == 0, s_block, 0)
    meta = jnp.where(row_at == 1, s_within, meta)
    meta = jnp.where(row_at == 2, r_block, meta)
    meta = jnp.where(row_at == 3, r_within, meta).astype(F32).astype(BF)
    for m, ref in enumerate(slot_refs):
        moved = match_columns(pos - m * slot, slot)
        ref[0:slot, :] = mm(moved, fe_ref[...]).astype(BF)
        tail = lax.dot_general(meta, moved, (((1,), (1,)), ((), ())), preferred_element_type=F32)
        ref[slot:, :] = jnp.zeros((ref.shape[0] - slot, ref.shape[1]), BF)
        ref[slot : slot + 16, 0:slot] = jnp.concatenate(
            [tail, jnp.zeros((8, slot), F32)], axis=0
        ).astype(BF)
    for copy in copies[3:]:
        copy.wait()


def load_kernel(*refs):
    count = len(refs) // 2
    sources, held, sems = refs[:count], refs[count : 2 * count], refs[-1]
    copies = [pltpu.make_async_copy(a, b, sems.at[i]) for i, (a, b) in enumerate(zip(sources, held))]
    for copy in copies:
        copy.start()
    for copy in copies:
        copy.wait()


def edge_tail(pre_act, w_out, bias, gain, shift):
    hidden = silu(pre_act + bias).astype(BF)
    return layer_norm(mm(hidden, w_out), gain, shift)


def local_kernel(layer, rows, *refs):
    coarse_ref, rest_ref, edges_ref, send_ref, recv_ref, win_ref, wout_ref = refs[0:7]
    vec_refs, before, (new_ref, sum_ref) = refs[7:10], refs[10:-2], refs[-2:]
    nodes = jnp.concatenate([coarse_ref[...], rest_ref[...]], axis=0)
    node_count = nodes.shape[0]
    if before:
        new_ref[0 : rows.start, :] = before[0][0 : rows.start, :]
    total = before[1][...] if before else None
    block = min(rows.stop - rows.start, 256)
    for start in range(rows.start, rows.stop, block):
        send = send_ref[start : start + block].reshape(1, -1)
        recv = recv_ref[start : start + block].reshape(1, -1)
        edges = edges_ref[start : start + block, :]
        senders = mm(match_rows(as_column(send), node_count), nodes).astype(BF)
        receivers = mm(match_rows(as_column(recv), node_count), nodes).astype(BF)
        stacked = jnp.concatenate([edges, senders, receivers], axis=1)
        normed = edge_tail(
            mm(stacked, win_ref[layer]), wout_ref[layer], *[v[layer : layer + 1, :] for v in vec_refs]
        )
        new_ref[start : start + block, :] = (edges.astype(F32) + normed).astype(BF)
        part = mm(match_columns(recv, node_count), normed.astype(BF))
        total = part if total is None else total + part
    sum_ref[...] = total


def slot_indices(ref, slot):
    meta = ref[slot : slot + 16, :].astype(F32)[0:8, 0 : -(-slot // 128) * 128]
    tall = jnp.transpose(meta)[0:slot, :]
    send_column = (tall[:, 0:1] * COARSE + tall[:, 1:2]).astype(I32)
    recv_column = (tall[:, 2:3] * COARSE + tall[:, 3:4]).astype(I32) - COARSE
    recv_row = (meta[2:3, 0:slot] * COARSE + meta[3:4, 0:slot]).astype(I32) - COARSE
    return send_column, recv_column, recv_row


def far_first_kernel(layer, lines, slot, *refs):
    slots, tables, win_ref, out_ref = refs[0:PLANE], refs[PLANE : PLANE + 2], refs[-2], refs[-1]
    span = lines * COARSE
    for pair in range(0, PLANE, 2):
        found = [slot_indices(ref, slot) for ref in slots[pair : pair + 2]]
        column_s = jnp.concatenate([f[0] for f in found], axis=0)
        column_r = jnp.concatenate([f[1] for f in found], axis=0)
        senders = mm(match_rows(column_s, span), tables[0][...])
        senders = senders + mm(match_rows(column_s, span, span), tables[1][...])
        receivers = mm(match_rows(column_r, span), tables[0][...])
        edges = jnp.concatenate([ref[0:slot, :] for ref in slots[pair : pair + 2]], axis=0)
        stacked = jnp.concatenate([edges, senders.astype(BF), receivers.astype(BF)], axis=1)
        out_ref[pair * slot : (pair + 2) * slot, :] = mm(stacked, win_ref[layer])


def far_second_kernel(layer, lines, slot, pairs, keep, chained, *refs):
    count = 2 * len(pairs)
    slots, tables, refs = refs[0:count], refs[count : count + 2], refs[count + 2 :]
    pre_ref, sum_ref, win_ref, wout_ref, refs = *refs[0:4], refs[4:]
    vecs, refs = [v[layer : layer + 1, :] for v in refs[0:3]], refs[3:]
    new_refs, outs = refs[0:count], refs[count:]
    span, width = lines * COARSE, pre_ref.shape[1]
    total = None
    for i, pair in enumerate(pairs):
        own = slots[2 * i : 2 * i + 2]
        found = [slot_indices(ref, slot) for ref in own]
        column_s = jnp.concatenate([f[0] for f in found], axis=0)
        senders = mm(match_rows(column_s, span, 2 * span), tables[0][...])
        senders = senders + mm(match_rows(column_s, span, 3 * span), tables[1][...])
        pre_act = pre_ref[pair * slot : (pair + 2) * slot, :]
        pre_act = pre_act + mm(senders.astype(BF), win_ref[layer, width : 2 * width, :])
        normed = edge_tail(pre_act, wout_ref[layer], *vecs)
        edges = jnp.concatenate([ref[0:slot, :] for ref in own], axis=0)
        new = (edges.astype(F32) + normed).astype(BF)
        message = normed.astype(BF)
        for j in range(2):
            new_refs[2 * i + j][0:slot, :] = new[j * slot : (j + 1) * slot, :]
            if keep:
                new_refs[2 * i + j][slot:, :] = own[j][slot:, :]
            part = mm(match_columns(found[j][2], span), message[j * slot : (j + 1) * slot, :])
            total = part if total is None else total + part
    if len(outs) == 1:
        outs[0][...] = total
        outs[0][0:COARSE, :] += sum_ref[0:COARSE, :]
        return
    if chained:
        total = total + sum_ref[...]
        outs[0][...] = total[0:COARSE, :]
    else:
        outs[0][...] = total[0:COARSE, :] + sum_ref[0:COARSE, :]
    for i, ref in enumerate(outs[1:]):
        ref[...] = total[(i + 1) * COARSE : (i + 2) * COARSE, :].astype(BF)


def node_update(layer, nodes, sums, win_ref, wout_ref, vec_refs):
    stacked = jnp.concatenate([nodes, sums.astype(BF)], axis=1)
    bias, gain, shift = [v[layer : layer + 1, :] for v in vec_refs]
    normed = edge_tail(mm(stacked, win_ref[layer]), wout_ref[layer], bias, gain, shift)
    return (nodes.astype(F32) + normed).astype(BF)


def rest_kernel(layer, nodes_ref, sum_ref, win_ref, wout_ref, *refs):
    sums = sum_ref[COARSE:, :]
    refs[-1][...] = node_update(layer, nodes_ref[...], sums, win_ref, wout_ref, refs[0:3])


def coarse_kernel(layer, nodes_ref, rest_ref, own_ref, *refs):
    part_refs, (win_ref, wout_ref), vec_refs, out_ref = refs[:-6], refs[-6:-4], refs[-4:-1], refs[-1]
    sums = own_ref[...]
    for ref in part_refs:
        sums = sums + ref[...].astype(F32)
    out_ref[0:COARSE, :] = node_update(layer, nodes_ref[...], sums, win_ref, wout_ref, vec_refs)
    if out_ref.shape[0] > COARSE:
        out_ref[COARSE:, :] = rest_ref[...]


def restore_kernel(slot, pos_ref, *refs):
    slots, out_ref = refs[:-1], refs[-1]
    column = as_column(pos_ref[...])
    total = None
    for m, ref in enumerate(slots):
        piece = mm(match_rows(column - m * slot, slot), ref[0:slot, :])
        total = piece if total is None else total + piece
    out_ref[...] = total.astype(BF)


def call(kernel, outs, args, flops, limit, first=None, scratch=()):
    bytes_accessed = sum(a.size * a.dtype.itemsize for a in args)
    bytes_accessed += sum(o.size * o.dtype.itemsize for o in outs)
    whole = pl.BlockSpec(memory_space=pltpu.VMEM)
    specs = [whole] * len(args)
    if first is not None:
        specs = [pl.BlockSpec(memory_space=pltpu.SMEM)] * first
        specs += [pl.BlockSpec(memory_space=pltpu.HBM)] * (len(args) - first)
        args = list(args[:first]) + [
            pltpu.with_memory_space_constraint(a, pltpu.HBM) for a in args[first:]
        ]
    return pl.pallas_call(
        kernel,
        out_shape=outs,
        in_specs=specs,
        out_specs=[whole] * len(outs),
        scratch_shapes=scratch,
        compiler_params=pltpu.CompilerParams(vmem_limit_bytes=limit),
        cost_estimate=pl.CostEstimate(flops=flops, bytes_accessed=bytes_accessed, transcendentals=0),
    )(*args)


def body(
    node_feat,
    local_edges,
    far_edges,
    local_send,
    local_recv,
    far_send,
    far_recv,
    edge_in,
    edge_out,
    node_in,
    node_out,
    edge_bias,
    edge_gain,
    edge_shift,
    node_bias,
    node_gain,
    node_shift,
):
    devices = lax.axis_size("patch")
    lines = devices // PLANE
    node_count, width = node_feat.shape
    far_count, local_count = far_edges.shape[0], local_edges.shape[0]
    slot = lines * (5 * far_count // (2 * devices))
    padded = -(-(slot + 4) // 16) * 16
    layers = edge_in.shape[0]
    limit = (24 if lines <= 4 else 56) * 2**20
    shape = jax.ShapeDtypeStruct
    place = [0] * lines
    for z in range(lines):
        place[z ^ (z >> 1)] = z

    def swap(values, distance):
        return lax.ppermute(values, "patch", [(i, i ^ distance) for i in range(devices)])

    own = lax.axis_index("patch").reshape(1).astype(I32)
    fs, fr = far_send.reshape(1, -1), far_recv.reshape(1, -1)
    tied = lax.optimization_barrier
    prepared = call(
        functools.partial(prep_kernel, node_count, lines, slot),
        [shape((1, far_count), I32), shape((COARSE, width), BF)]
        + [shape((node_count - COARSE, width), BF)]
        + [shape((padded, width), BF)] * PLANE,
        [own, fs, fr, far_edges, node_feat],
        2 * PLANE * slot * far_count * width,
        limit,
        first=1,
        scratch=[
            pltpu.VMEM((1, far_count), I32),
            pltpu.VMEM((1, far_count), I32),
            pltpu.VMEM((far_count, width), BF),
            pltpu.SemaphoreType.DMA((5,)),
        ],
    )
    pos, coarse, rest, slots = *prepared[0:3], prepared[3:]
    slots = [slots[0]] + [swap(slots[m], m) for m in range(1, PLANE)]
    fetched = [local_edges, local_send, local_recv, edge_in, edge_out, node_in, node_out]
    fetched += [edge_bias, edge_gain, edge_shift, node_bias, node_gain, node_shift]
    fetched = call(
        load_kernel,
        [shape(v.shape, v.dtype) for v in fetched],
        fetched,
        0,
        limit,
        first=0,
        scratch=[pltpu.SemaphoreType.DMA((len(fetched),))],
    )
    far_rows, span = PLANE * slot, lines * COARSE
    hop = None
    if lines == 4:
        hop = [swap(coarse, 12), swap(coarse, 4)]
        *hop, fetched, slots = tied((*hop, fetched, slots))
    local, local_send, local_recv, edge_in, edge_out, node_in, node_out = fetched[0:7]
    edge_vecs, node_vecs = fetched[7:10], fetched[10:13]
    for l in range(layers):
        last = l == layers - 1
        cut = local_count // 3 * 2 // 256 * 256
        pieces = [slice(0, cut), slice(cut, local_count)] if cut else [slice(0, local_count)]

        def local_part(rows, before=()):
            return call(
                functools.partial(local_kernel, l, rows),
                [shape((rows.stop, width), BF), shape((node_count, width), F32)],
                [coarse, rest, local, local_send, local_recv, edge_in, edge_out, *edge_vecs, *before],
                2 * (rows.stop - rows.start) * width * (3 * node_count + 4 * width),
                limit,
            )

        done = local_part(pieces[0])
        if lines == 4:
            z3, z1 = hop if l == 0 else (swap(coarse, 12), swap(coarse, 4))
            if l:
                z3, z1, done = tied((z3, z1, done))
            near = jnp.concatenate([coarse, z1, z3], axis=0)
            z2, near_across = swap(z3, 4), swap(near, 2)
            for rows in pieces[1:]:
                done = local_part(rows, done)
            z2, done = tied((z2, done))
            table = jnp.concatenate([near, z2], axis=0)
            across = [near_across, swap(z2, 2)]
        else:
            table = [coarse if z == 0 else swap(coarse, PLANE * z) for z in place]
            table = jnp.concatenate(table, axis=0)
            across = [swap(table, 2)]
            for rows in pieces[1:]:
                done = local_part(rows, done)
        local, sums = done
        tables = [table, swap(table, 1)]
        pre_act = call(
            functools.partial(far_first_kernel, l, lines, slot),
            [shape((far_rows, width), F32)],
            [*slots, *tables, edge_in],
            2 * far_rows * width * (3 * span + 3 * width),
            limit,
        )[0]
        across[-1], pre_act = tied((across[-1], pre_act))
        across = jnp.concatenate(across, axis=0)
        tables += [across, swap(across, 1)]
        kept = [shape((slot if last else padded, width), BF)]
        parts_shape = [shape((COARSE, width), F32)] + [shape((COARSE, width), BF)] * (lines - 1)
        ends = [pre_act, sums, edge_in, edge_out, *edge_vecs]
        work = 2 * far_rows * width * (3 * span + 2 * width)
        if last:
            far = call(
                functools.partial(far_second_kernel, l, lines, slot, (2,), False, False),
                kept * 2 + [shape((span, width), F32)],
                [*slots[2:], *tables[2:], *ends],
                work // 2,
                limit,
            )
            ends[1] = far[2]
            more = call(
                functools.partial(far_second_kernel, l, lines, slot, (0,), False, True),
                kept * 2 + parts_shape,
                [*slots[:2], *tables[2:], *ends],
                work // 2,
                limit,
            )
            slots, parts = [*more[:2], *far[:2]], more[2:]
        else:
            far = call(
                functools.partial(far_second_kernel, l, lines, slot, (0, 2), True, False),
                kept * 4 + parts_shape,
                [*slots, *tables[2:], *ends],
                work,
                limit,
            )
            slots, parts = [*far[:PLANE]], far[PLANE:]
        far_parts = [swap(parts[i], PLANE * place[i]) for i in range(lines - 1, 0, -1)]
        parts = [parts[0]] + far_parts[::-1]
        ends = [node_in, node_out, *node_vecs]
        rest = call(
            functools.partial(rest_kernel, l),
            [shape((node_count - COARSE, width), BF)],
            [rest, sums, *ends],
            6 * (node_count - COARSE) * width * width,
            limit,
        )[0]
        coarse = call(
            functools.partial(coarse_kernel, l),
            [shape((node_count if last else COARSE, width), BF)],
            [coarse, rest, *parts, *ends],
            6 * COARSE * width * width,
            limit,
        )[0]
    slots = [slots[0]] + [swap(slots[m], m) for m in range(1, PLANE)]
    far_out = call(
        functools.partial(restore_kernel, slot),
        [shape((far_count, width), BF)],
        [pos, *slots],
        2 * PLANE * slot * far_count * width,
        limit,
    )[0]
    return (coarse, local, far_out)


def solution(mesh):
    split = P(("groups", "patch"), None)
    line = P(("groups", "patch"))
    return jax.shard_map(
        body,
        mesh=mesh,
        in_specs=(split,) * 3 + (line,) * 4 + (P(),) * 10,
        out_specs=(split,) * 3,
        check_vma=False,
    )
```

time: 86.6 us -> 77.6 us (0.90)
  local copies, waits for them, and re-layouts: 8.85 us -> 0.07 us
  Pallas kernels: 22.3 us -> 30.3 us
  waiting for transfers between devices: 26.5 us -> 18.9 us
    pallas_call x8 -> x16, Pallas kernels: 22.3 us -> 30.3 us  [call(): pl.pallas_call(kernel, out_shape=outs, in_specs=specs, out_specs=[whole]...]
    ppermute x26, waiting for transfers between devices: 26.5 us -> 18.9 us  [swap(): lax.ppermute(values, 'patch', [(i, i ^ distance) for i in range(devices)])]
    unnamed x37 -> x5, local copies, waits for them, and re-layouts: 5.56 us -> 0.05 us
    squeeze x4 -> x0, local copies, waits for them, and re-layouts: 2.39 us -> none  [the longest x1 2.11 us: body(): edge_in[l]]
    slice x5 -> x0, local copies, waits for them, and re-layouts: 0.87 us -> none  [the longest x1 0.85 us: body(): nodes, coarse, local = (node_feat, node_feat[:COARSE], local_edges)]
  transfers between devices with their start and end apart: 26 -> 26, of which waited for: 12 -> 15; matrix products, arithmetic and copies ran while one was open for 3% -> 0% of each run, Pallas kernels for 13% -> 26%
where the time goes in v2:
time: 77.6 us; the launch traced here: 77.4 us
  Pallas kernels  30.3 us (39%)
  starting transfers between devices  27.2 us (35%)
  waiting for transfers between devices  18.9 us (24%)
  between operations  0.9 us (1%)
    pallas_call x16, Pallas kernels, call(): pl.pallas_call(kernel, out_shape=outs, in_specs=specs, out_specs=[whole]...  30.3 us
    ppermute x26, starting transfers between devices, swap(): lax.ppermute(values, 'patch', [(i, i ^ distance) for i in range(devices)])  27.2 us
    ppermute x26, waiting for transfers between devices, swap(): lax.ppermute(values, 'patch', [(i, i ^ distance) for i in range(devices)])  18.9 us
  transfers between devices with their start and end apart: 26, of which 15 were waited for; matrix products, arithmetic and copies ran while one was open for 0% of the time, Pallas kernels for 26%

profile of v2, /device:TPU:0, one launch (start us, length us, event | category | flops | bytes accessed | tf_op | source)
XLA Modules:
  0.0 77.4 jit_solution(82149328949233001)
XLA Ops:
  0.6 1.6 %shard_map.184 = (s32[1,256]{1,0:T(1,128)S(1)}, bf16[64,512]{1,0:T(8,128)(2,1)S(1)}, bf16[192,512]{1,0:T(8,128)(2,1)S(1)}, bf16[176,512]{1,0:T(8,128)(2,1)S(1)},...) custom-call(s32[1]{0:T(128)} %bitcast.own_ref, s32[1,256]{1,0:T(1,128)} %bitcast.3, ...), custom_call_target="tpu_custom_call" | custom-call | flops 167772160 | bytes 1510404 | tf_op jit(solution)/shard_map/pallas_call | solution.py:254
  2.7 2.6 %collective-permute-start.3 = (bf16[176,512]{1,0:T(8,128)(2,1)S(1)}, bf16[176,512]{1,0:T(8,128)(2,1)S(1)}, u32[]{:S(2)}, u32[]{:S(2)}) collective-permute-start(bf16[176,512]{1,0:T(8,128)(2,1)S(1)} %get-tuple-element.98), channel_id=1, source_target_pairs={{0,2},{1,3},{2,0},{3,1},{4,6},{5,7},{6,4},{7,5},{8,10},{9,11},{10,... | collective-permute-start | bytes 540680 | tf_op jit(solution)/shard_map/ppermute | solution.py:298
  5.4 1.8 %collective-permute-start.1 = (bf16[64,512]{1,0:T(8,128)(2,1)S(1)}, bf16[64,512]{1,0:T(8,128)(2,1)S(1)}, u32[]{:S(2)}, u32[]{:S(2)}) collective-permute-start(bf16[64,512]{1,0:T(8,128)(2,1)S(1)} %get-tuple-element.81.refs_0_.nodes_ref), channel_id=1, source_target_pairs={{0,4},{1,5},{2,6},{3,7},{4,0},{5,1},{6,2},{7,3},{8,12},{9,13},{10,... | collective-permute-start | bytes 196616 | tf_op jit(solution)/shard_map/ppermute | solution.py:298
  7.2 2.5 %collective-permute-start = (bf16[64,512]{1,0:T(8,128)(2,1)S(1)}, bf16[64,512]{1,0:T(8,128)(2,1)S(1)}, u32[]{:S(2)}, u32[]{:S(2)}) collective-permute-start(bf16[64,512]{1,0:T(8,128)(2,1)S(1)} %get-tuple-element.81.refs_0_.nodes_ref), channel_id=1, source_target_pairs={{0,12},{1,13},{2,14},{3,15},{4,8},{5,9},{6,10},{7,11},{8,4},{9,5},... | collective-permute-start | bytes 196616 | tf_op jit(solution)/shard_map/ppermute | solution.py:298
  9.7 3.5 %shard_map.185 = (bf16[768,512]{1,0:T(8,128)(2,1)S(1)}, s32[768]{0:T(1024)S(1)}, s32[768]{0:T(1024)S(1)}, bf16[2,1536,512]{2,1,0:T(8,128)(2,1)S(1)}, bf16[2,512,...) custom-call(bf16[768,512]{1,0:T(8,128)(2,1)} %refs_0_.1, ...), custom_call_target="tpu_custom_call" | custom-call | bytes 16314368 | tf_op jit(solution)/shard_map/pallas_call | solution.py:254
  14.0 1.7 %collective-permute-start.5 = (bf16[64,512]{1,0:T(8,128)(2,1)S(1)}, bf16[64,512]{1,0:T(8,128)(2,1)S(1)}, u32[]{:S(2)}, u32[]{:S(2)}) collective-permute-start(bf16[64,512]{1,0:T(8,128)(2,1)S(1)} %collective-permute-done), channel_id=1, source_target_pairs={{0,4},{1,5},{2,6},{3,7},{4,0},{5,1},{6,2},{7,3},{8,12},{9,13},{10,... | collective-permute-start | bytes 196616 | tf_op jit(solution)/shard_map/ppermute | solution.py:298
  15.7 1.6 %collective-permute-start.6 = (bf16[192,512]{1,0:T(8,128)(2,1)S(1)}, bf16[192,512]{1,0:T(8,128)(2,1)S(1)}, u32[]{:S(2)}, u32[]{:S(2)}) collective-permute-start(bf16[192,512]{1,0:T(8,128)(2,1)S(1)} %pad_maximum_fusion.1), channel_id=1, source_target_pairs={{0,2},{1,3},{2,0},{3,1},{4,6},{5,7},{6,4},{7,5},{8,10},{9,11},{10,... | collective-permute-start | bytes 589832 | tf_op jit(solution)/shard_map/ppermute | solution.py:298
  17.3 2.6 %shard_map.186 = (bf16[512,512]{1,0:T(8,128)(2,1)S(1)}, f32[256,512]{1,0:T(8,128)S(1)}) custom-call(bf16[64,512]{1,0:T(8,128)(2,1)S(1)} %get-tuple-element.81.refs_0_.nodes_ref, bf16[192,512]{1,0:T(8,128)(2,1)S(1)} %get-tuple-element.82.refs_1_.nodes_ref, bf16[768,512]{1,0:T(8,128)(2,1)S(1)} %get-tuple-element.101.refs_2_, ...), custom_call_target="tpu_custom_call" | custom-call | flops 1476395008 | bytes 6309888 | tf_op jit(solution)/shard_map/pallas_call | solution.py:254
  19.9 1.7 %shard_map.187 = (bf16[768,512]{1,0:T(8,128)(2,1)S(1)}, f32[256,512]{1,0:T(8,128)S(1)}) custom-call(bf16[64,512]{1,0:T(8,128)(2,1)S(1)} %get-tuple-element.81.refs_0_.nodes_ref, bf16[192,512]{1,0:T(8,128)(2,1)S(1)} %get-tuple-element.82.refs_1_.nodes_ref, bf16[768,512]{1,0:T(8,128)(2,1)S(1)} %get-tuple-element.101.refs_2_, ...), custom_call_target="tpu_custom_call" | custom-call | flops 738197504 | bytes 7620608 | tf_op jit(solution)/shard_map/pallas_call | solution.py:254
  23.3 2.0 %shard_map.189.refs_6_ = f32[640,512]{1,0:T(8,128)S(1)} custom-call(bf16[176,512]{1,0:T(8,128)(2,1)S(1)} %get-tuple-element.119.refs_0_, bf16[176,512]{1,0:T(8,128)(2,1)S(1)} %collective-permute-done.2.refs_1_, bf16[176,512]{1,0:T(8,128)(2,1)S(1)} %collective-permute-done.3.refs_2_, bf16[176,512]{1,0:T(8,128)(2,1)S(1)} %collective-permute-done.4.refs_3_, ...), custom_call_target="tpu_custom_call" | custom-call | flops 1509949440 | bytes 5701632 | tf_op jit(solution)/shard_map/pallas_call | solution.py:254
  26.3 1.5 %collective-permute-done.9.refs_5_ = bf16[256,512]{1,0:T(8,128)(2,1)S(1)} collective-permute-done((bf16[256,512]{1,0:T(8,128)(2,1)S(1)}, bf16[256,512]{1,0:T(8,128)(2,1)S(1)}, u32[]{:S(2)}, u32[]{:S(2)}) %collective-permute-start.9) | collective-permute-done | bytes 262176 | tf_op jit(solution)/shard_map/ppermute | solution.py:298
  27.8 3.2 %shard_map.190 = (bf16[176,512]{1,0:T(8,128)(2,1)S(1)}, bf16[176,512]{1,0:T(8,128)(2,1)S(1)}, bf16[176,512]{1,0:T(8,128)(2,1)S(1)}, bf16[176,512]{1,0:T(8,128)(2...) custom-call(bf16[176,512]{1,0:T(8,128)(2,1)S(1)} %get-tuple-element., ...), custom_call_target="tpu_custom_call" | custom-call | flops 1174405120 | bytes 8335360 | tf_op jit(solution)/shard_map/pallas_call | solution.py:254
  31.5 3.6 %collective-permute-start.11 = (bf16[64,512]{1,0:T(8,128)(2,1)S(1)}, bf16[64,512]{1,0:T(8,128)(2,1)S(1)}, u32[]{:S(2)}, u32[]{:S(2)}) collective-permute-start(bf16[64,512]{1,0:T(8,128)(2,1)S(1)} %get-tuple-element.129), channel_id=1, source_target_pairs={{0,12},{1,13},{2,14},{3,15},{4,8},{5,9},{6,10},{7,11},{8,4},{9,5},... | collective-permute-start | bytes 196616 | tf_op jit(solution)/shard_map/ppermute | solution.py:298
  35.9 3.4 %collective-permute-done.11.refs_1_ = bf16[64,512]{1,0:T(8,128)(2,1)S(1)} collective-permute-done((bf16[64,512]{1,0:T(8,128)(2,1)S(1)}, bf16[64,512]{1,0:T(8,128)(2,1)S(1)}, u32[]{:S(2)}, u32[]{:S(2)}) %collective-permute-start.11) | collective-permute-done | bytes 65568 | tf_op jit(solution)/shard_map/ppermute | solution.py:298
  39.3 2.1 %collective-permute-done.12.refs_2_ = bf16[64,512]{1,0:T(8,128)(2,1)S(1)} collective-permute-done((bf16[64,512]{1,0:T(8,128)(2,1)S(1)}, bf16[64,512]{1,0:T(8,128)(2,1)S(1)}, u32[]{:S(2)}, u32[]{:S(2)}) %collective-permute-start.12) | collective-permute-done | bytes 65568 | tf_op jit(solution)/shard_map/ppermute | solution.py:298
  42.2 2.0 %collective-permute-start.13 = (bf16[64,512]{1,0:T(8,128)(2,1)S(1)}, bf16[64,512]{1,0:T(8,128)(2,1)S(1)}, u32[]{:S(2)}, u32[]{:S(2)}) collective-permute-start(bf16[64,512]{1,0:T(8,128)(2,1)S(1)} %shard_map.191.refs_0_.nodes_ref), channel_id=1, source_target_pairs={{0,12},{1,13},{2,14},{3,15},{4,8},{5,9},{6,10},{7,11},{8,4},{9,5},... | collective-permute-start | bytes 196616 | tf_op jit(solution)/shard_map/ppermute | solution.py:298
  44.2 2.7 %shard_map.192 = (bf16[512,512]{1,0:T(8,128)(2,1)S(1)}, f32[256,512]{1,0:T(8,128)S(1)}) custom-call(bf16[64,512]{1,0:T(8,128)(2,1)S(1)} %shard_map.191.refs_0_.nodes_ref, bf16[192,512]{1,0:T(8,128)(2,1)S(1)} %shard_map.188.rest_ref.refs_1_.nodes_ref, bf16[768,512]{1,0:T(8,128)(2,1)S(1)} %get-tuple-element.131.refs_2_, s32[768]{0:T(1024)S(1)} %get-tuple-element.102.refs_3_, ...), custom_call_target="tpu_custom_call" | custom-call | flops 1476395008 | bytes 6309888 | tf_op jit(solution)/shard_map/pallas_call | solution.py:254
  50.0 2.5 %shard_map.193 = (bf16[768,512]{1,0:T(8,128)(2,1)}, f32[256,512]{1,0:T(8,128)S(1)}) custom-call(bf16[64,512]{1,0:T(8,128)(2,1)S(1)} %shard_map.191.refs_0_.nodes_ref, bf16[192,512]{1,0:T(8,128)(2,1)S(1)} %shard_map.188.rest_ref.refs_1_.nodes_ref, bf16[768,512]{1,0:T(8,128)(2,1)S(1)} %get-tuple-element.131.refs_2_, s32[768]{0:T(1024)S(1)} %get-tuple-element.102.refs_3_, ...), custom_call_target="tpu_custom_call" | custom-call | flops 738197504 | bytes 7620608 | tf_op jit(solution)/shard_map/pallas_call | solution.py:254
  55.2 2.0 %shard_map.195.refs_4_ = f32[640,512]{1,0:T(8,128)S(1)} custom-call(bf16[176,512]{1,0:T(8,128)(2,1)S(1)} %get-tuple-element.140.refs_0_, bf16[176,512]{1,0:T(8,128)(2,1)S(1)} %get-tuple-element.141.refs_1_, bf16[176,512]{1,0:T(8,128)(2,1)S(1)} %get-tuple-element.144.refs_2_.refs_0_, bf16[176,512]{1,0:T(8,128)(2,1)S(1)} %get-tuple-element.145.refs_3_.refs_1_, ...), custom_call_target="tpu_custom_call" | custom-call | flops 1509949440 | bytes 5701632 | tf_op jit(solution)/shard_map/pallas_call | solution.py:254
  57.3 1.5 %collective-permute-done.19.refs_3_ = bf16[256,512]{1,0:T(8,128)(2,1)S(1)} collective-permute-done((bf16[256,512]{1,0:T(8,128)(2,1)S(1)}, bf16[256,512]{1,0:T(8,128)(2,1)S(1)}, u32[]{:S(2)}, u32[]{:S(2)}) %collective-permute-start.19) | collective-permute-done | bytes 262176 | tf_op jit(solution)/shard_map/ppermute | solution.py:298
  58.9 1.8 %shard_map.196 = (bf16[160,512]{1,0:T(8,128)(2,1)S(1)}, bf16[160,512]{1,0:T(8,128)(2,1)S(1)}, f32[256,512]{1,0:T(8,128)S(1)}) custom-call(bf16[176,512]{1,0:T(8,128)(2,1)S(1)} %get-tuple-element.144.refs_2_.refs_0_, bf16[176,512]{1,0:T(8,128)(2,1)S(1)} %get-tuple-element.145.refs_3_.refs_1_, ...), custom_call_target="tpu_custom_call" | custom-call | flops 587202560 | bytes 7778304 | tf_op jit(solution)/shard_map/pallas_call | solution.py:254
  60.6 1.8 %shard_map.197 = (bf16[160,512]{1,0:T(8,128)(2,1)S(1)}, bf16[160,512]{1,0:T(8,128)(2,1)S(1)}, f32[64,512]{1,0:T(8,128)S(1)}, bf16[64,512]{1,0:T(8,128)(2,1)S(1)}...) custom-call(bf16[176,512]{1,0:T(8,128)(2,1)S(1)} %get-tuple-element.140.refs_0_, ...), custom_call_target="tpu_custom_call" | custom-call | flops 587202560 | bytes 7581696 | tf_op jit(solution)/shard_map/pallas_call | solution.py:254
  65.3 2.0 %collective-permute-start.21 = (bf16[64,512]{1,0:T(8,128)(2,1)S(1)}, bf16[64,512]{1,0:T(8,128)(2,1)S(1)}, u32[]{:S(2)}, u32[]{:S(2)}) collective-permute-start(bf16[64,512]{1,0:T(8,128)(2,1)S(1)} %get-tuple-element.151), channel_id=1, source_target_pairs={{0,12},{1,13},{2,14},{3,15},{4,8},{5,9},{6,10},{7,11},{8,4},{9,5},... | collective-permute-start | bytes 196616 | tf_op jit(solution)/shard_map/ppermute | solution.py:298
  71.4 3.3 %collective-permute-done.22.refs_2_ = bf16[64,512]{1,0:T(8,128)(2,1)S(1)} collective-permute-done((bf16[64,512]{1,0:T(8,128)(2,1)S(1)}, bf16[64,512]{1,0:T(8,128)(2,1)S(1)}, u32[]{:S(2)}, u32[]{:S(2)}) %collective-permute-start.22) | collective-permute-done | bytes 65568 | tf_op jit(solution)/shard_map/ppermute | solution.py:298
  (55 shorter events, 21.7 us)
Async XLA Ops:
  2.2 11.2 %collective-permute-start.2 = (bf16[176,512]{1,0:T(8,128)(2,1)S(1)}, bf16[176,512]{1,0:T(8,128)(2,1)S(1)}, u32[]{:S(2)}, u32[]{:S(2)}) collective-permute-start(bf16[176,512]{1,0:T(8,128)(2,1)S(1)} %get-tuple-element.97), channel_id=1, source_target_pairs={{0,1},{1,0},{2,3},{3,2},{4,5},{5,4},{6,7},{7,6},{8,9},{9,8},{10,11... | collective-permute-start | bytes 540680 | tf_op jit(solution)/shard_map/ppermute | solution.py:298
  2.7 10.7 %collective-permute-start.3 = (bf16[176,512]{1,0:T(8,128)(2,1)S(1)}, bf16[176,512]{1,0:T(8,128)(2,1)S(1)}, u32[]{:S(2)}, u32[]{:S(2)}) collective-permute-start(bf16[176,512]{1,0:T(8,128)(2,1)S(1)} %get-tuple-element.98), channel_id=1, source_target_pairs={{0,2},{1,3},{2,0},{3,1},{4,6},{5,7},{6,4},{7,5},{8,10},{9,11},{10,... | collective-permute-start | bytes 540680 | tf_op jit(solution)/shard_map/ppermute | solution.py:298
  5.3 8.7 %collective-permute-start.4 = (bf16[176,512]{1,0:T(8,128)(2,1)S(1)}, bf16[176,512]{1,0:T(8,128)(2,1)S(1)}, u32[]{:S(2)}, u32[]{:S(2)}) collective-permute-start(bf16[176,512]{1,0:T(8,128)(2,1)S(1)} %get-tuple-element.99), channel_id=1, source_target_pairs={{0,3},{1,2},{2,1},{3,0},{4,7},{5,6},{6,5},{7,4},{8,11},{9,10},{10,... | collective-permute-start | bytes 540680 | tf_op jit(solution)/shard_map/ppermute | solution.py:298
  5.4 7.8 %collective-permute-start.1 = (bf16[64,512]{1,0:T(8,128)(2,1)S(1)}, bf16[64,512]{1,0:T(8,128)(2,1)S(1)}, u32[]{:S(2)}, u32[]{:S(2)}) collective-permute-start(bf16[64,512]{1,0:T(8,128)(2,1)S(1)} %get-tuple-element.81.refs_0_.nodes_ref), channel_id=1, source_target_pairs={{0,4},{1,5},{2,6},{3,7},{4,0},{5,1},{6,2},{7,3},{8,12},{9,13},{10,... | collective-permute-start | bytes 196616 | tf_op jit(solution)/shard_map/ppermute | solution.py:298
  7.2 6.3 %collective-permute-start = (bf16[64,512]{1,0:T(8,128)(2,1)S(1)}, bf16[64,512]{1,0:T(8,128)(2,1)S(1)}, u32[]{:S(2)}, u32[]{:S(2)}) collective-permute-start(bf16[64,512]{1,0:T(8,128)(2,1)S(1)} %get-tuple-element.81.refs_0_.nodes_ref), channel_id=1, source_target_pairs={{0,12},{1,13},{2,14},{3,15},{4,8},{5,9},{6,10},{7,11},{8,4},{9,5},... | collective-permute-start | bytes 196616 | tf_op jit(solution)/shard_map/ppermute | solution.py:298
  14.0 7.6 %collective-permute-start.5 = (bf16[64,512]{1,0:T(8,128)(2,1)S(1)}, bf16[64,512]{1,0:T(8,128)(2,1)S(1)}, u32[]{:S(2)}, u32[]{:S(2)}) collective-permute-start(bf16[64,512]{1,0:T(8,128)(2,1)S(1)} %collective-permute-done), channel_id=1, source_target_pairs={{0,4},{1,5},{2,6},{3,7},{4,0},{5,1},{6,2},{7,3},{8,12},{9,13},{10,... | collective-permute-start | bytes 196616 | tf_op jit(solution)/shard_map/ppermute | solution.py:298
  15.7 6.9 %collective-permute-start.6 = (bf16[192,512]{1,0:T(8,128)(2,1)S(1)}, bf16[192,512]{1,0:T(8,128)(2,1)S(1)}, u32[]{:S(2)}, u32[]{:S(2)}) collective-permute-start(bf16[192,512]{1,0:T(8,128)(2,1)S(1)} %pad_maximum_fusion.1), channel_id=1, source_target_pairs={{0,2},{1,3},{2,0},{3,1},{4,6},{5,7},{6,4},{7,5},{8,10},{9,11},{10,... | collective-permute-start | bytes 589832 | tf_op jit(solution)/shard_map/ppermute | solution.py:298
  21.7 1.6 %collective-permute-start.8 = (bf16[256,512]{1,0:T(8,128)(2,1)S(1)}, bf16[256,512]{1,0:T(8,128)(2,1)S(1)}, u32[]{:S(2)}, u32[]{:S(2)}) collective-permute-start(bf16[256,512]{1,0:T(8,128)(2,1)S(1)} %constant_dynamic-update-slice_fusion.refs_4_), channel_id=1, source_target_pairs={{0,1},{1,0},{2,3},{3,2},{4,5},{5,4},{6,7},{7,6},{8,9},{9,8},{10,11... | collective-permute-start | bytes 786440 | tf_op jit(solution)/shard_map/ppermute | solution.py:298
  21.8 4.5 %collective-permute-start.7 = (bf16[64,512]{1,0:T(8,128)(2,1)S(1)}, bf16[64,512]{1,0:T(8,128)(2,1)S(1)}, u32[]{:S(2)}, u32[]{:S(2)}) collective-permute-start(bf16[64,512]{1,0:T(8,128)(2,1)S(1)} %collective-permute-done.5), channel_id=1, source_target_pairs={{0,2},{1,3},{2,0},{3,1},{4,6},{5,7},{6,4},{7,5},{8,10},{9,11},{10,... | collective-permute-start | bytes 196616 | tf_op jit(solution)/shard_map/ppermute | solution.py:298
  31.0 4.9 %collective-permute-start.10 = (bf16[64,512]{1,0:T(8,128)(2,1)S(1)}, bf16[64,512]{1,0:T(8,128)(2,1)S(1)}, u32[]{:S(2)}, u32[]{:S(2)}) collective-permute-start(bf16[64,512]{1,0:T(8,128)(2,1)S(1)} %get-tuple-element.128), channel_id=1, source_target_pairs={{0,4},{1,5},{2,6},{3,7},{4,0},{5,1},{6,2},{7,3},{8,12},{9,13},{10,... | collective-permute-start | bytes 196616 | tf_op jit(solution)/shard_map/ppermute | solution.py:298
  31.5 7.8 %collective-permute-start.11 = (bf16[64,512]{1,0:T(8,128)(2,1)S(1)}, bf16[64,512]{1,0:T(8,128)(2,1)S(1)}, u32[]{:S(2)}, u32[]{:S(2)}) collective-permute-start(bf16[64,512]{1,0:T(8,128)(2,1)S(1)} %get-tuple-element.129), channel_id=1, source_target_pairs={{0,12},{1,13},{2,14},{3,15},{4,8},{5,9},{6,10},{7,11},{8,4},{9,5},... | collective-permute-start | bytes 196616 | tf_op jit(solution)/shard_map/ppermute | solution.py:298
  35.1 6.3 %collective-permute-start.12 = (bf16[64,512]{1,0:T(8,128)(2,1)S(1)}, bf16[64,512]{1,0:T(8,128)(2,1)S(1)}, u32[]{:S(2)}, u32[]{:S(2)}) collective-permute-start(bf16[64,512]{1,0:T(8,128)(2,1)S(1)} %get-tuple-element.130), channel_id=1, source_target_pairs={{0,8},{1,9},{2,10},{3,11},{4,12},{5,13},{6,14},{7,15},{8,0},{9,1},... | collective-permute-start | bytes 196616 | tf_op jit(solution)/shard_map/ppermute | solution.py:298
  42.1 4.8 %collective-permute-start.14 = (bf16[64,512]{1,0:T(8,128)(2,1)S(1)}, bf16[64,512]{1,0:T(8,128)(2,1)S(1)}, u32[]{:S(2)}, u32[]{:S(2)}) collective-permute-start(bf16[64,512]{1,0:T(8,128)(2,1)S(1)} %shard_map.191.refs_0_.nodes_ref), channel_id=1, source_target_pairs={{0,4},{1,5},{2,6},{3,7},{4,0},{5,1},{6,2},{7,3},{8,12},{9,13},{10,... | collective-permute-start | bytes 196616 | tf_op jit(solution)/shard_map/ppermute | solution.py:298
  42.2 6.2 %collective-permute-start.13 = (bf16[64,512]{1,0:T(8,128)(2,1)S(1)}, bf16[64,512]{1,0:T(8,128)(2,1)S(1)}, u32[]{:S(2)}, u32[]{:S(2)}) collective-permute-start(bf16[64,512]{1,0:T(8,128)(2,1)S(1)} %shard_map.191.refs_0_.nodes_ref), channel_id=1, source_target_pairs={{0,12},{1,13},{2,14},{3,15},{4,8},{5,9},{6,10},{7,11},{8,4},{9,5},... | collective-permute-start | bytes 196616 | tf_op jit(solution)/shard_map/ppermute | solution.py:298
  48.3 4.3 %collective-permute-start.15 = (bf16[64,512]{1,0:T(8,128)(2,1)S(1)}, bf16[64,512]{1,0:T(8,128)(2,1)S(1)}, u32[]{:S(2)}, u32[]{:S(2)}) collective-permute-start(bf16[64,512]{1,0:T(8,128)(2,1)S(1)} %collective-permute-done.13), channel_id=1, source_target_pairs={{0,4},{1,5},{2,6},{3,7},{4,0},{5,1},{6,2},{7,3},{8,12},{9,13},{10,... | collective-permute-start | bytes 196616 | tf_op jit(solution)/shard_map/ppermute | solution.py:298
  49.4 5.7 %collective-permute-start.16 = (bf16[192,512]{1,0:T(8,128)(2,1)S(1)}, bf16[192,512]{1,0:T(8,128)(2,1)S(1)}, u32[]{:S(2)}, u32[]{:S(2)}) collective-permute-start(bf16[192,512]{1,0:T(8,128)(2,1)S(1)} %pad_maximum_fusion.2), channel_id=1, source_target_pairs={{0,2},{1,3},{2,0},{3,1},{4,6},{5,7},{6,4},{7,5},{8,10},{9,11},{10,... | collective-permute-start | bytes 589832 | tf_op jit(solution)/shard_map/ppermute | solution.py:298
  52.6 2.5 %collective-permute-start.18 = (bf16[256,512]{1,0:T(8,128)(2,1)S(1)}, bf16[256,512]{1,0:T(8,128)(2,1)S(1)}, u32[]{:S(2)}, u32[]{:S(2)}) collective-permute-start(bf16[256,512]{1,0:T(8,128)(2,1)S(1)} %pad_maximum_fusion.refs_4_), channel_id=1, source_target_pairs={{0,1},{1,0},{2,3},{3,2},{4,5},{5,4},{6,7},{7,6},{8,9},{9,8},{10,11... | collective-permute-start | bytes 786440 | tf_op jit(solution)/shard_map/ppermute | solution.py:298
  52.7 4.5 %collective-permute-start.17 = (bf16[64,512]{1,0:T(8,128)(2,1)S(1)}, bf16[64,512]{1,0:T(8,128)(2,1)S(1)}, u32[]{:S(2)}, u32[]{:S(2)}) collective-permute-start(bf16[64,512]{1,0:T(8,128)(2,1)S(1)} %collective-permute-done.15), channel_id=1, source_target_pairs={{0,2},{1,3},{2,0},{3,1},{4,6},{5,7},{6,4},{7,5},{8,10},{9,11},{10,... | collective-permute-start | bytes 196616 | tf_op jit(solution)/shard_map/ppermute | solution.py:298
  62.4 13.7 %collective-permute-start.23 = (bf16[160,512]{1,0:T(8,128)(2,1)S(1)}, bf16[160,512]{1,0:T(8,128)(2,1)S(1)}, u32[]{:S(2)}, u32[]{:S(2)}) collective-permute-start(bf16[160,512]{1,0:T(8,128)(2,1)S(1)} %get-tuple-element.156), channel_id=1, source_target_pairs={{0,1},{1,0},{2,3},{3,2},{4,5},{5,4},{6,7},{7,6},{8,9},{9,8},{10,11... | collective-permute-start | bytes 491528 | tf_op jit(solution)/shard_map/ppermute | solution.py:298
  62.6 13.5 %collective-permute-start.24 = (bf16[160,512]{1,0:T(8,128)(2,1)S(1)}, bf16[160,512]{1,0:T(8,128)(2,1)S(1)}, u32[]{:S(2)}, u32[]{:S(2)}) collective-permute-start(bf16[160,512]{1,0:T(8,128)(2,1)S(1)} %get-tuple-element.157), channel_id=1, source_target_pairs={{0,2},{1,3},{2,0},{3,1},{4,6},{5,7},{6,4},{7,5},{8,10},{9,11},{10,... | collective-permute-start | bytes 491528 | tf_op jit(solution)/shard_map/ppermute | solution.py:298
  64.0 12.2 %collective-permute-start.25 = (bf16[160,512]{1,0:T(8,128)(2,1)S(1)}, bf16[160,512]{1,0:T(8,128)(2,1)S(1)}, u32[]{:S(2)}, u32[]{:S(2)}) collective-permute-start(bf16[160,512]{1,0:T(8,128)(2,1)S(1)} %get-tuple-element.158), channel_id=1, source_target_pairs={{0,3},{1,2},{2,1},{3,0},{4,7},{5,6},{6,5},{7,4},{8,11},{9,10},{10,... | collective-permute-start | bytes 491528 | tf_op jit(solution)/shard_map/ppermute | solution.py:298
  64.3 4.4 %collective-permute-start.20 = (bf16[64,512]{1,0:T(8,128)(2,1)S(1)}, bf16[64,512]{1,0:T(8,128)(2,1)S(1)}, u32[]{:S(2)}, u32[]{:S(2)}) collective-permute-start(bf16[64,512]{1,0:T(8,128)(2,1)S(1)} %get-tuple-element.150), channel_id=1, source_target_pairs={{0,4},{1,5},{2,6},{3,7},{4,0},{5,1},{6,2},{7,3},{8,12},{9,13},{10,... | collective-permute-start | bytes 196616 | tf_op jit(solution)/shard_map/ppermute | solution.py:298
  65.3 6.1 %collective-permute-start.21 = (bf16[64,512]{1,0:T(8,128)(2,1)S(1)}, bf16[64,512]{1,0:T(8,128)(2,1)S(1)}, u32[]{:S(2)}, u32[]{:S(2)}) collective-permute-start(bf16[64,512]{1,0:T(8,128)(2,1)S(1)} %get-tuple-element.151), channel_id=1, source_target_pairs={{0,12},{1,13},{2,14},{3,15},{4,8},{5,9},{6,10},{7,11},{8,4},{9,5},... | collective-permute-start | bytes 196616 | tf_op jit(solution)/shard_map/ppermute | solution.py:298
  68.8 6.0 %collective-permute-start.22 = (bf16[64,512]{1,0:T(8,128)(2,1)S(1)}, bf16[64,512]{1,0:T(8,128)(2,1)S(1)}, u32[]{:S(2)}, u32[]{:S(2)}) collective-permute-start(bf16[64,512]{1,0:T(8,128)(2,1)S(1)} %get-tuple-element.152), channel_id=1, source_target_pairs={{0,8},{1,9},{2,10},{3,11},{4,12},{5,13},{6,14},{7,15},{8,0},{9,1},... | collective-permute-start | bytes 196616 | tf_op jit(solution)/shard_map/ppermute | solution.py:298
  (2 other events, 3.1 us)

commit v3 on v2

--- a/solution.py
+++ b/solution.py
@@ -105,12 +105,13 @@
         copy.wait()
 
 
-def load_kernel(*refs):
-    count = len(refs) // 2
-    sources, held, sems = refs[:count], refs[count : 2 * count], refs[-1]
-    copies = [pltpu.make_async_copy(a, b, sems.at[i]) for i, (a, b) in enumerate(zip(sources, held))]
-    for copy in copies:
-        copy.start()
+def load_kernel(picks, *refs):
+    sources, held, sems = refs[: -len(picks) - 1], refs[-len(picks) - 1 : -1], refs[-1]
+    copies = []
+    for i, (which, layer) in enumerate(picks):
+        source = sources[which] if layer is None else sources[which].at[layer]
+        copies.append(pltpu.make_async_copy(source, held[i], sems.at[i]))
+        copies[i].start()
     for copy in copies:
         copy.wait()
 
@@ -137,7 +138,7 @@
         receivers = mm(match_rows(as_column(recv), node_count), nodes).astype(BF)
         stacked = jnp.concatenate([edges, senders, receivers], axis=1)
         normed = edge_tail(
-            mm(stacked, win_ref[layer]), wout_ref[layer], *[v[layer : layer + 1, :] for v in vec_refs]
+            mm(stacked, win_ref[...]), wout_ref[...], *[v[layer : layer + 1, :] for v in vec_refs]
         )
         new_ref[start : start + block, :] = (edges.astype(F32) + normed).astype(BF)
         part = mm(match_columns(recv, node_count), normed.astype(BF))
@@ -145,66 +146,62 @@
     sum_ref[...] = total
 
 
-def slot_indices(ref, slot):
-    meta = ref[slot : slot + 16, :].astype(F32)[0:8, 0 : -(-slot // 128) * 128]
-    tall = jnp.transpose(meta)[0:slot, :]
-    send_column = (tall[:, 0:1] * COARSE + tall[:, 1:2]).astype(I32)
-    recv_column = (tall[:, 2:3] * COARSE + tall[:, 3:4]).astype(I32) - COARSE
-    recv_row = (meta[2:3, 0:slot] * COARSE + meta[3:4, 0:slot]).astype(I32) - COARSE
-    return send_column, recv_column, recv_row
-
-
-def far_first_kernel(layer, lines, slot, *refs):
-    slots, tables, win_ref, out_ref = refs[0:PLANE], refs[PLANE : PLANE + 2], refs[-2], refs[-1]
+def far_first_kernel(lines, slot, *refs):
+    slots, tables, win_ref = refs[0:PLANE], refs[PLANE : PLANE + 2], refs[PLANE + 2]
+    out_ref, late_ref, *scatter_refs = refs[PLANE + 3 :]
     span = lines * COARSE
     for pair in range(0, PLANE, 2):
-        found = [slot_indices(ref, slot) for ref in slots[pair : pair + 2]]
-        column_s = jnp.concatenate([f[0] for f in found], axis=0)
-        column_r = jnp.concatenate([f[1] for f in found], axis=0)
-        senders = mm(match_rows(column_s, span), tables[0][...])
-        senders = senders + mm(match_rows(column_s, span, span), tables[1][...])
+        columns_s, columns_r, rows_r = [], [], []
+        for ref in slots[pair : pair + 2]:
+            meta = ref[slot : slot + 16, :].astype(F32)[0:8, 0 : -(-slot // 128) * 128]
+            tall = jnp.transpose(meta)[0:slot, :]
+            columns_s.append((tall[:, 0:1] * COARSE + tall[:, 1:2]).astype(I32))
+            columns_r.append((tall[:, 2:3] * COARSE + tall[:, 3:4]).astype(I32) - COARSE)
+            rows_r.append((meta[2:3, 0:slot] * COARSE + meta[3:4, 0:slot]).astype(I32) - COARSE)
+        column_s, column_r = jnp.concatenate(columns_s, axis=0), jnp.concatenate(columns_r, axis=0)
+        senders = None
+        for q, table in enumerate(tables):
+            piece = mm(match_rows(column_s, table.shape[0], q * span), table[...])
+            senders = piece if senders is None else senders + piece
         receivers = mm(match_rows(column_r, span), tables[0][...])
         edges = jnp.concatenate([ref[0:slot, :] for ref in slots[pair : pair + 2]], axis=0)
         stacked = jnp.concatenate([edges, senders.astype(BF), receivers.astype(BF)], axis=1)
-        out_ref[pair * slot : (pair + 2) * slot, :] = mm(stacked, win_ref[layer])
-
-
-def far_second_kernel(layer, lines, slot, pairs, keep, chained, *refs):
-    count = 2 * len(pairs)
-    slots, tables, refs = refs[0:count], refs[count : count + 2], refs[count + 2 :]
-    pre_ref, sum_ref, win_ref, wout_ref, refs = *refs[0:4], refs[4:]
-    vecs, refs = [v[layer : layer + 1, :] for v in refs[0:3]], refs[3:]
-    new_refs, outs = refs[0:count], refs[count:]
-    span, width = lines * COARSE, pre_ref.shape[1]
+        rows = slice(pair * slot, (pair + 2) * slot)
+        out_ref[rows, :] = mm(stacked, win_ref[...])
+        late_ref[rows, :] = match_rows(column_s, 2 * span, 2 * span)
+        scatter_refs[pair // 2][...] = match_columns(jnp.concatenate(rows_r, axis=1), span)
+
+
+def far_second_kernel(layer, lines, slot, keep, *refs):
+    slots, refs = refs[0:PLANE], refs[PLANE:]
+    straight_ref, across_ref, pre_ref, late_ref, *scatter_refs = refs[0:6]
+    sum_ref, win_ref, wout_ref = refs[6:9]
+    vecs, refs = [v[layer : layer + 1, :] for v in refs[9:12]], refs[12:]
+    count = PLANE if keep else 3
+    new_refs, own_ref, part_refs = refs[0:count], refs[count], refs[count + 1 :]
+    width = pre_ref.shape[1]
+    table = jnp.concatenate([straight_ref[...], across_ref[...]], axis=0)
     total = None
-    for i, pair in enumerate(pairs):
-        own = slots[2 * i : 2 * i + 2]
-        found = [slot_indices(ref, slot) for ref in own]
-        column_s = jnp.concatenate([f[0] for f in found], axis=0)
-        senders = mm(match_rows(column_s, span, 2 * span), tables[0][...])
-        senders = senders + mm(match_rows(column_s, span, 3 * span), tables[1][...])
-        pre_act = pre_ref[pair * slot : (pair + 2) * slot, :]
-        pre_act = pre_act + mm(senders.astype(BF), win_ref[layer, width : 2 * width, :])
-        normed = edge_tail(pre_act, wout_ref[layer], *vecs)
-        edges = jnp.concatenate([ref[0:slot, :] for ref in own], axis=0)
+    for pair in range(0, PLANE, 2):
+        rows = slice(pair * slot, (pair + 2) * slot)
+        senders = mm(late_ref[rows, :], table).astype(BF)
+        pre_act = pre_ref[rows, :] + mm(senders, win_ref[width : 2 * width, :])
+        normed = edge_tail(pre_act, wout_ref[...], *vecs)
+        edges = jnp.concatenate([ref[0:slot, :] for ref in slots[pair : pair + 2]], axis=0)
         new = (edges.astype(F32) + normed).astype(BF)
-        message = normed.astype(BF)
         for j in range(2):
-            new_refs[2 * i + j][0:slot, :] = new[j * slot : (j + 1) * slot, :]
+            piece = new[j * slot : (j + 1) * slot, :]
             if keep:
-                new_refs[2 * i + j][slot:, :] = own[j][slot:, :]
-            part = mm(match_columns(found[j][2], span), message[j * slot : (j + 1) * slot, :])
-            total = part if total is None else total + part
-    if len(outs) == 1:
-        outs[0][...] = total
-        outs[0][0:COARSE, :] += sum_ref[0:COARSE, :]
-        return
-    if chained:
-        total = total + sum_ref[...]
-        outs[0][...] = total[0:COARSE, :]
-    else:
-        outs[0][...] = total[0:COARSE, :] + sum_ref[0:COARSE, :]
-    for i, ref in enumerate(outs[1:]):
+                new_refs[pair + j][0:slot, :] = piece
+                new_refs[pair + j][slot:, :] = slots[pair + j][slot:, :]
+            elif j == 0:
+                new_refs[pair][...] = piece
+            else:
+                new_refs[1][pair // 2 * slot : (pair // 2 + 1) * slot, :] = piece
+        part = mm(scatter_refs[pair // 2][...], normed.astype(BF))
+        total = part if total is None else total + part
+    own_ref[...] = total[0:COARSE, :] + sum_ref[0:COARSE, :]
+    for i, ref in enumerate(part_refs):
         ref[...] = total[(i + 1) * COARSE : (i + 2) * COARSE, :].astype(BF)
 
 
@@ -234,8 +231,9 @@
     slots, out_ref = refs[:-1], refs[-1]
     column = as_column(pos_ref[...])
     total = None
-    for m, ref in enumerate(slots):
-        piece = mm(match_rows(column - m * slot, slot), ref[0:slot, :])
+    pieces = [slots[0][...], slots[1][0:slot, :], slots[2][0:slot, :], slots[2][slot:, :]]
+    for m, rows in enumerate(pieces):
+        piece = mm(match_rows(column - m * slot, slot), rows)
         total = piece if total is None else total + piece
     out_ref[...] = total.astype(BF)
 
@@ -318,34 +316,38 @@
     )
     pos, coarse, rest, slots = *prepared[0:3], prepared[3:]
     slots = [slots[0]] + [swap(slots[m], m) for m in range(1, PLANE)]
-    fetched = [local_edges, local_send, local_recv, edge_in, edge_out, node_in, node_out]
-    fetched += [edge_bias, edge_gain, edge_shift, node_bias, node_gain, node_shift]
-    fetched = call(
-        load_kernel,
-        [shape(v.shape, v.dtype) for v in fetched],
-        fetched,
-        0,
-        limit,
-        first=0,
-        scratch=[pltpu.SemaphoreType.DMA((len(fetched),))],
-    )
+    def fetch(sources, picks):
+        pieces = [sources[i] if layer is None else sources[i][0] for i, layer in picks]
+        return call(
+            functools.partial(load_kernel, picks),
+            [shape(v.shape, v.dtype) for v in pieces],
+            sources,
+            0,
+            limit,
+            first=0,
+            scratch=[pltpu.SemaphoreType.DMA((len(picks),))],
+        )
+
+    first = [local_edges, local_send, local_recv, edge_bias, edge_gain, edge_shift]
+    picks = [(i, None) for i in range(len(first))] + [(len(first), 0), (len(first) + 1, 0)]
+    first = fetch([*first, edge_in, edge_out], picks)
     far_rows, span = PLANE * slot, lines * COARSE
+    cut = local_count // 3 * 2 // 256 * 256
+    pieces = [slice(0, cut), slice(cut, local_count)] if cut else [slice(0, local_count)]
     hop = None
     if lines == 4:
         hop = [swap(coarse, 12), swap(coarse, 4)]
-        *hop, fetched, slots = tied((*hop, fetched, slots))
-    local, local_send, local_recv, edge_in, edge_out, node_in, node_out = fetched[0:7]
-    edge_vecs, node_vecs = fetched[7:10], fetched[10:13]
+        hop, first, slots = tied((hop, first, slots))
+    local, local_send, local_recv = first[0:3]
+    edge_vecs, weights = first[3:6], [first[6:8]]
     for l in range(layers):
         last = l == layers - 1
-        cut = local_count // 3 * 2 // 256 * 256
-        pieces = [slice(0, cut), slice(cut, local_count)] if cut else [slice(0, local_count)]
 
         def local_part(rows, before=()):
             return call(
                 functools.partial(local_kernel, l, rows),
                 [shape((rows.stop, width), BF), shape((node_count, width), F32)],
-                [coarse, rest, local, local_send, local_recv, edge_in, edge_out, *edge_vecs, *before],
+                [coarse, rest, local, local_send, local_recv, *weights[l], *edge_vecs, *before],
                 2 * (rows.stop - rows.start) * width * (3 * node_count + 4 * width),
                 limit,
             )
@@ -356,62 +358,62 @@
             if l:
                 z3, z1, done = tied((z3, z1, done))
             near = jnp.concatenate([coarse, z1, z3], axis=0)
-            z2, near_across = swap(z3, 4), swap(near, 2)
-            for rows in pieces[1:]:
-                done = local_part(rows, done)
+            z2 = swap(z3, 4)
+            across = swap(near, 2)
+        else:
+            near = [coarse if z == 0 else swap(coarse, PLANE * z) for z in place]
+            near, z2 = jnp.concatenate(near[:-1], axis=0), near[-1]
+            across = swap(near, 2)
+        if l == 0:
             z2, done = tied((z2, done))
-            table = jnp.concatenate([near, z2], axis=0)
-            across = [near_across, swap(z2, 2)]
-        else:
-            table = [coarse if z == 0 else swap(coarse, PLANE * z) for z in place]
-            table = jnp.concatenate(table, axis=0)
-            across = [swap(table, 2)]
-            for rows in pieces[1:]:
-                done = local_part(rows, done)
-        local, sums = done
+        for rows in pieces[1:]:
+            done = local_part(rows, done)
+        if l:
+            z2, done = tied((z2, done))
+        late = swap(z2, 2)
+        table = jnp.concatenate([near, z2], axis=0)
         tables = [table, swap(table, 1)]
-        pre_act = call(
-            functools.partial(far_first_kernel, l, lines, slot),
-            [shape((far_rows, width), F32)],
-            [*slots, *tables, edge_in],
+        found = call(
+            functools.partial(far_first_kernel, lines, slot),
+            [shape((far_rows, width), F32), shape((far_rows, 2 * span), BF)]
+            + [shape((span, 2 * slot), BF)] * 2,
+            [*slots, *tables, weights[l][0]],
             2 * far_rows * width * (3 * span + 3 * width),
             limit,
-        )[0]
-        across[-1], pre_act = tied((across[-1], pre_act))
-        across = jnp.concatenate(across, axis=0)
-        tables += [across, swap(across, 1)]
-        kept = [shape((slot if last else padded, width), BF)]
-        parts_shape = [shape((COARSE, width), F32)] + [shape((COARSE, width), BF)] * (lines - 1)
-        ends = [pre_act, sums, edge_in, edge_out, *edge_vecs]
-        work = 2 * far_rows * width * (3 * span + 2 * width)
+        )
+        late, found, done = tied((late, found, done))
+        local, sums = done
+        late = jnp.concatenate([across, late], axis=0)
+        late = [late, swap(late, 1)]
+        moved = [shape((padded, width), BF)] * PLANE
         if last:
-            far = call(
-                functools.partial(far_second_kernel, l, lines, slot, (2,), False, False),
-                kept * 2 + [shape((span, width), F32)],
-                [*slots[2:], *tables[2:], *ends],
-                work // 2,
-                limit,
-            )
-            ends[1] = far[2]
-            more = call(
-                functools.partial(far_second_kernel, l, lines, slot, (0,), False, True),
-                kept * 2 + parts_shape,
-                [*slots[:2], *tables[2:], *ends],
-                work // 2,
-                limit,
-            )
-            slots, parts = [*more[:2], *far[:2]], more[2:]
-        else:
-            far = call(
-                functools.partial(far_second_kernel, l, lines, slot, (0, 2), True, False),
-                kept * 4 + parts_shape,
-                [*slots, *tables[2:], *ends],
-                work,
-                limit,
-            )
-            slots, parts = [*far[:PLANE]], far[PLANE:]
+            moved = [shape((rows * slot, width), BF) for rows in (1, 2, 1)]
+        far = call(
+            functools.partial(far_second_kernel, l, lines, slot, not last),
+            moved
+            + [shape((COARSE, width), F32)]
+            + [shape((COARSE, width), BF)] * (lines - 1),
+            [*slots, *late, *found, sums, *weights[l], *edge_vecs],
+            2 * far_rows * width * (3 * span + 2 * width),
+            limit,
+        )
+        slots, parts = [*far[: len(moved)]], far[len(moved) :]
+        if last:
+            kept, paired, crossing = slots
+            paired = swap(paired, 1)
+            crossing = jnp.concatenate([crossing, paired[slot:]], axis=0)
+            slots = [kept, paired, swap(crossing, 2)]
         far_parts = [swap(parts[i], PLANE * place[i]) for i in range(lines - 1, 0, -1)]
-        parts = [parts[0]] + far_parts[::-1]
+        parts = [parts[0], *far_parts]
+        if l == 0:
+            sources = [node_in, node_out, node_bias, node_gain, node_shift]
+            picks = [(i, None) for i in range(len(sources))]
+            for i in range(1, layers):
+                picks += [(len(sources), i), (len(sources) + 1, i)]
+            sources, sums = tied(([*sources, edge_in, edge_out], sums))
+            second = fetch(sources, picks)
+            node_in, node_out, node_vecs = *second[0:2], second[2:5]
+            weights += [second[5 + 2 * i : 7 + 2 * i] for i in range(layers - 1)]
         ends = [node_in, node_out, *node_vecs]
         rest = call(
             functools.partial(rest_kernel, l),
@@ -427,7 +429,6 @@
             6 * COARSE * width * width,
             limit,
         )[0]
-    slots = [slots[0]] + [swap(slots[m], m) for m in range(1, PLANE)]
     far_out = call(
         functools.partial(restore_kernel, slot),
         [shape((far_count, width), BF)],

time: 77.6 us -> 73.4 us (0.946)
  waiting for transfers between devices: 18.9 us -> 15.9 us
    ppermute x26 -> x25, waiting for transfers between devices: 18.9 us -> 15.9 us  [swap(): lax.ppermute(values, 'patch', [(i, i ^ distance) for i in range(devices)])]
    ppermute x26 -> x25, starting transfers between devices: 27.2 us -> 26.6 us  [swap(): lax.ppermute(values, 'patch', [(i, i ^ distance) for i in range(devices)])]
  transfers between devices with their start and end apart: 26 -> 25, of which waited for: 15 -> 14; matrix products, arithmetic and copies ran while one was open for 0% -> 0% of each run, Pallas kernels for 26% -> 29%
where the time goes in v3:
time: 73.4 us; the launch traced here: 73.2 us
  Pallas kernels  29.8 us (41%)
  starting transfers between devices  26.6 us (36%)
  waiting for transfers between devices  15.9 us (22%)
  between operations  0.9 us (1%)
    pallas_call x16, Pallas kernels, call(): pl.pallas_call(kernel, out_shape=outs, in_specs=specs, out_specs=[whole]...  29.8 us
    ppermute x25, starting transfers between devices, swap(): lax.ppermute(values, 'patch', [(i, i ^ distance) for i in range(devices)])  26.6 us
    ppermute x25, waiting for transfers between devices, swap(): lax.ppermute(values, 'patch', [(i, i ^ distance) for i in range(devices)])  15.9 us
  transfers between devices with their start and end apart: 25, of which 14 were waited for; matrix products, arithmetic and copies ran while one was open for 0% of the time, Pallas kernels for 29%

profile of v3, /device:TPU:0, one launch (start us, length us, event | category | flops | bytes accessed | tf_op | source)
XLA Modules:
  0.0 73.2 jit_solution(11582613505282342045)
XLA Ops:
  0.6 1.6 %shard_map.184 = (s32[1,256]{1,0:T(1,128)S(1)}, bf16[64,512]{1,0:T(8,128)(2,1)S(1)}, bf16[192,512]{1,0:T(8,128)(2,1)S(1)}, bf16[176,512]{1,0:T(8,128)(2,1)S(1)},...) custom-call(s32[1]{0:T(128)} %bitcast.own_ref, s32[1,256]{1,0:T(1,128)} %bitcast.3, ...), custom_call_target="tpu_custom_call" | custom-call | flops 167772160 | bytes 1510404 | tf_op jit(solution)/shard_map/pallas_call | solution.py:252
  2.7 2.6 %collective-permute-start.3 = (bf16[176,512]{1,0:T(8,128)(2,1)S(1)}, bf16[176,512]{1,0:T(8,128)(2,1)S(1)}, u32[]{:S(2)}, u32[]{:S(2)}) collective-permute-start(bf16[176,512]{1,0:T(8,128)(2,1)S(1)} %get-tuple-element.114), channel_id=1, source_target_pairs={{0,2},{1,3},{2,0},{3,1},{4,6},{5,7},{6,4},{7,5},{8,10},{9,11},{10,... | collective-permute-start | bytes 540680 | tf_op jit(solution)/shard_map/ppermute | solution.py:296
  5.4 1.8 %collective-permute-start.1 = (bf16[64,512]{1,0:T(8,128)(2,1)S(1)}, bf16[64,512]{1,0:T(8,128)(2,1)S(1)}, u32[]{:S(2)}, u32[]{:S(2)}) collective-permute-start(bf16[64,512]{1,0:T(8,128)(2,1)S(1)} %get-tuple-element.102.refs_0_.nodes_ref), channel_id=1, source_target_pairs={{0,4},{1,5},{2,6},{3,7},{4,0},{5,1},{6,2},{7,3},{8,12},{9,13},{10,... | collective-permute-start | bytes 196616 | tf_op jit(solution)/shard_map/ppermute | solution.py:296
  7.2 2.5 %collective-permute-start = (bf16[64,512]{1,0:T(8,128)(2,1)S(1)}, bf16[64,512]{1,0:T(8,128)(2,1)S(1)}, u32[]{:S(2)}, u32[]{:S(2)}) collective-permute-start(bf16[64,512]{1,0:T(8,128)(2,1)S(1)} %get-tuple-element.102.refs_0_.nodes_ref), channel_id=1, source_target_pairs={{0,12},{1,13},{2,14},{3,15},{4,8},{5,9},{6,10},{7,11},{8,4},{9,5},... | collective-permute-start | bytes 196616 | tf_op jit(solution)/shard_map/ppermute | solution.py:296
  9.7 1.9 %shard_map.185 = (bf16[768,512]{1,0:T(8,128)(2,1)S(1)}, s32[768]{0:T(1024)S(1)}, s32[768]{0:T(1024)S(1)}, f32[2,512]{1,0:T(2,128)S(1)}, f32[2,512]{1,0:T(2,128)S...) custom-call(bf16[768,512]{1,0:T(8,128)(2,1)} %refs_0_.1, s32[768]{0:T(1024)} %refs_1_.1, ...), custom_call_target="tpu_custom_call" | custom-call | bytes 7901184 | tf_op jit(solution)/shard_map/pallas_call | solution.py:252
  11.6 1.8 %collective-permute-done = bf16[64,512]{1,0:T(8,128)(2,1)S(1)} collective-permute-done((bf16[64,512]{1,0:T(8,128)(2,1)S(1)}, bf16[64,512]{1,0:T(8,128)(2,1)S(1)}, u32[]{:S(2)}, u32[]{:S(2)}) %collective-permute-start) | collective-permute-done | bytes 65568 | tf_op jit(solution)/shard_map/ppermute | solution.py:296
  14.0 1.7 %collective-permute-start.5 = (bf16[64,512]{1,0:T(8,128)(2,1)S(1)}, bf16[64,512]{1,0:T(8,128)(2,1)S(1)}, u32[]{:S(2)}, u32[]{:S(2)}) collective-permute-start(bf16[64,512]{1,0:T(8,128)(2,1)S(1)} %collective-permute-done), channel_id=1, source_target_pairs={{0,4},{1,5},{2,6},{3,7},{4,0},{5,1},{6,2},{7,3},{8,12},{9,13},{10,... | collective-permute-start | bytes 196616 | tf_op jit(solution)/shard_map/ppermute | solution.py:296
  15.7 1.6 %collective-permute-start.8 = (bf16[192,512]{1,0:T(8,128)(2,1)S(1)}, bf16[192,512]{1,0:T(8,128)(2,1)S(1)}, u32[]{:S(2)}, u32[]{:S(2)}) collective-permute-start(bf16[192,512]{1,0:T(8,128)(2,1)S(1)} %pad_maximum_fusion.2), channel_id=1, source_target_pairs={{0,2},{1,3},{2,0},{3,1},{4,6},{5,7},{6,4},{7,5},{8,10},{9,11},{10,... | collective-permute-start | bytes 589832 | tf_op jit(solution)/shard_map/ppermute | solution.py:296
  17.3 2.7 %shard_map.186 = (bf16[512,512]{1,0:T(8,128)(2,1)S(1)}, f32[256,512]{1,0:T(8,128)S(1)}) custom-call(bf16[64,512]{1,0:T(8,128)(2,1)S(1)} %get-tuple-element.102.refs_0_.nodes_ref, bf16[192,512]{1,0:T(8,128)(2,1)S(1)} %get-tuple-element.103.refs_1_.nodes_ref, bf16[768,512]{1,0:T(8,128)(2,1)S(1)} %get-tuple-element.117.refs_2_, ...), custom_call_target="tpu_custom_call" | custom-call | flops 1476395008 | bytes 4212736 | tf_op jit(solution)/shard_map/pallas_call | solution.py:252
  20.6 1.7 %shard_map.188 = (bf16[768,512]{1,0:T(8,128)(2,1)S(1)}, f32[256,512]{1,0:T(8,128)S(1)}) custom-call(bf16[64,512]{1,0:T(8,128)(2,1)S(1)} %get-tuple-element.102.refs_0_.nodes_ref, bf16[192,512]{1,0:T(8,128)(2,1)S(1)} %get-tuple-element.103.refs_1_.nodes_ref, bf16[768,512]{1,0:T(8,128)(2,1)S(1)} %get-tuple-element.117.refs_2_, ...), custom_call_target="tpu_custom_call" | custom-call | flops 738197504 | bytes 5523456 | tf_op jit(solution)/shard_map/pallas_call | solution.py:252
  22.6 2.1 %shard_map.187 = (f32[640,512]{1,0:T(8,128)S(1)}, bf16[640,512]{1,0:T(8,128)(2,1)S(1)}, bf16[256,320]{1,0:T(8,128)(2,1)S(1)}, bf16[256,320]{1,0:T(8,128)(2,1)S(1)}) custom-call(bf16[176,512]{1,0:T(8,128)(2,1)S(1)} %get-tuple-element.128.refs_0_, bf16[176,512]{1,0:T(8,128)(2,1)S(1)} %collective-permute-done.2.refs_1_, ...), custom_call_target="tpu_custom_call" | custom-call | flops 1509949440 | bytes 5111808 | tf_op jit(solution)/shard_map/pallas_call | solution.py:252
  24.8 1.5 %collective-permute-done.9.refs_5_ = bf16[256,512]{1,0:T(8,128)(2,1)S(1)} collective-permute-done((bf16[256,512]{1,0:T(8,128)(2,1)S(1)}, bf16[256,512]{1,0:T(8,128)(2,1)S(1)}, u32[]{:S(2)}, u32[]{:S(2)}) %collective-permute-start.9) | collective-permute-done | bytes 262176 | tf_op jit(solution)/shard_map/ppermute | solution.py:296
  26.4 2.4 %shard_map.191 = (bf16[176,512]{1,0:T(8,128)(2,1)S(1)}, bf16[176,512]{1,0:T(8,128)(2,1)S(1)}, bf16[176,512]{1,0:T(8,128)(2,1)S(1)}, bf16[176,512]{1,0:T(8,128)(2...) custom-call(bf16[176,512]{1,0:T(8,128)(2,1)S(1)} %get-tuple-element., ...), custom_call_target="tpu_custom_call" | custom-call | flops 1174405120 | bytes 7221248 | tf_op jit(solution)/shard_map/pallas_call | solution.py:252
  28.8 2.7 %collective-permute-start.10 = (bf16[64,512]{1,0:T(8,128)(2,1)S(1)}, bf16[64,512]{1,0:T(8,128)(2,1)S(1)}, u32[]{:S(2)}, u32[]{:S(2)}) collective-permute-start(bf16[64,512]{1,0:T(8,128)(2,1)S(1)} %get-tuple-element.161), channel_id=1, source_target_pairs={{0,8},{1,9},{2,10},{3,11},{4,12},{5,13},{6,14},{7,15},{8,0},{9,1},... | collective-permute-start | bytes 196616 | tf_op jit(solution)/shard_map/ppermute | solution.py:296
  32.4 2.6 %shard_map.189 = (bf16[2,1024,512]{2,1,0:T(8,128)(2,1)S(1)}, bf16[2,512,512]{2,1,0:T(8,128)(2,1)S(1)}, f32[2,512]{1,0:T(2,128)S(1)}, f32[2,512]{1,0:T(2,128)S(1)...) custom-call(bf16[2,1024,512]{2,1,0:T(8,128)(2,1)} %refs_0_.2, ...), custom_call_target="tpu_custom_call" | custom-call | bytes 12607488 | tf_op jit(solution)/shard_map/pallas_call | solution.py:252
  35.8 2.1 %collective-permute-done.11.refs_1_ = bf16[64,512]{1,0:T(8,128)(2,1)S(1)} collective-permute-done((bf16[64,512]{1,0:T(8,128)(2,1)S(1)}, bf16[64,512]{1,0:T(8,128)(2,1)S(1)}, u32[]{:S(2)}, u32[]{:S(2)}) %collective-permute-start.11) | collective-permute-done | bytes 65568 | tf_op jit(solution)/shard_map/ppermute | solution.py:296
  39.5 2.7 %collective-permute-start.13 = (bf16[64,512]{1,0:T(8,128)(2,1)S(1)}, bf16[64,512]{1,0:T(8,128)(2,1)S(1)}, u32[]{:S(2)}, u32[]{:S(2)}) collective-permute-start(bf16[64,512]{1,0:T(8,128)(2,1)S(1)} %shard_map.192.refs_0_.nodes_ref), channel_id=1, source_target_pairs={{0,12},{1,13},{2,14},{3,15},{4,8},{5,9},{6,10},{7,11},{8,4},{9,5},... | collective-permute-start | bytes 196616 | tf_op jit(solution)/shard_map/ppermute | solution.py:296
  42.1 2.7 %shard_map.193 = (bf16[512,512]{1,0:T(8,128)(2,1)S(1)}, f32[256,512]{1,0:T(8,128)S(1)}) custom-call(bf16[64,512]{1,0:T(8,128)(2,1)S(1)} %shard_map.192.refs_0_.nodes_ref, bf16[192,512]{1,0:T(8,128)(2,1)S(1)} %shard_map.190.rest_ref.refs_1_.nodes_ref, bf16[768,512]{1,0:T(8,128)(2,1)S(1)} %get-tuple-element.164.refs_2_, s32[768]{0:T(1024)S(1)} %get-tuple-element.118.refs_3_, ...), custom_call_target="tpu_custom_call" | custom-call | flops 1476395008 | bytes 4212736 | tf_op jit(solution)/shard_map/pallas_call | solution.py:252
  47.1 2.5 %shard_map.194 = (bf16[768,512]{1,0:T(8,128)(2,1)}, f32[256,512]{1,0:T(8,128)S(1)}) custom-call(bf16[64,512]{1,0:T(8,128)(2,1)S(1)} %shard_map.192.refs_0_.nodes_ref, bf16[192,512]{1,0:T(8,128)(2,1)S(1)} %shard_map.190.rest_ref.refs_1_.nodes_ref, bf16[768,512]{1,0:T(8,128)(2,1)S(1)} %get-tuple-element.164.refs_2_, s32[768]{0:T(1024)S(1)} %get-tuple-element.118.refs_3_, ...), custom_call_target="tpu_custom_call" | custom-call | flops 738197504 | bytes 5523456 | tf_op jit(solution)/shard_map/pallas_call | solution.py:252
  51.5 2.2 %shard_map.195 = (f32[640,512]{1,0:T(8,128)S(1)}, bf16[640,512]{1,0:T(8,128)(2,1)S(1)}, bf16[256,320]{1,0:T(8,128)(2,1)S(1)}, bf16[256,320]{1,0:T(8,128)(2,1)S(1)}) custom-call(bf16[176,512]{1,0:T(8,128)(2,1)S(1)} %get-tuple-element.175.refs_0_, bf16[176,512]{1,0:T(8,128)(2,1)S(1)} %get-tuple-element.176.refs_1_, ...), custom_call_target="tpu_custom_call" | custom-call | flops 1509949440 | bytes 5111808 | tf_op jit(solution)/shard_map/pallas_call | solution.py:252
  54.5 1.5 %collective-permute-done.19.refs_5_ = bf16[256,512]{1,0:T(8,128)(2,1)S(1)} collective-permute-done((bf16[256,512]{1,0:T(8,128)(2,1)S(1)}, bf16[256,512]{1,0:T(8,128)(2,1)S(1)}, u32[]{:S(2)}, u32[]{:S(2)}) %collective-permute-start.19) | collective-permute-done | bytes 262176 | tf_op jit(solution)/shard_map/ppermute | solution.py:296
  56.1 2.4 %shard_map.197 = (bf16[160,512]{1,0:T(8,128)(2,1)S(1)}, bf16[320,512]{1,0:T(8,128)(2,1)S(1)}, bf16[160,512]{1,0:T(8,128)(2,1)S(1)}, f32[64,512]{1,0:T(8,128)S(1)...) custom-call(bf16[176,512]{1,0:T(8,128)(2,1)S(1)} %get-tuple-element.175.refs_0_, ...), custom_call_target="tpu_custom_call" | custom-call | flops 1174405120 | bytes 7155712 | tf_op jit(solution)/shard_map/pallas_call | solution.py:252
  61.7 2.2 %collective-permute-start.20 = (bf16[64,512]{1,0:T(8,128)(2,1)S(1)}, bf16[64,512]{1,0:T(8,128)(2,1)S(1)}, u32[]{:S(2)}, u32[]{:S(2)}) collective-permute-start(bf16[64,512]{1,0:T(8,128)(2,1)S(1)} %get-tuple-element.193), channel_id=1, source_target_pairs={{0,8},{1,9},{2,10},{3,11},{4,12},{5,13},{6,14},{7,15},{8,0},{9,1},... | collective-permute-start | bytes 196616 | tf_op jit(solution)/shard_map/ppermute | solution.py:296
  66.2 3.1 %collective-permute-done.20.refs_0_ = bf16[64,512]{1,0:T(8,128)(2,1)S(1)} collective-permute-done((bf16[64,512]{1,0:T(8,128)(2,1)S(1)}, bf16[64,512]{1,0:T(8,128)(2,1)S(1)}, u32[]{:S(2)}, u32[]{:S(2)}) %collective-permute-start.20) | collective-permute-done | bytes 65568 | tf_op jit(solution)/shard_map/ppermute | solution.py:296
  (55 shorter events, 19.8 us)
Async XLA Ops:
  2.2 11.2 %collective-permute-start.2 = (bf16[176,512]{1,0:T(8,128)(2,1)S(1)}, bf16[176,512]{1,0:T(8,128)(2,1)S(1)}, u32[]{:S(2)}, u32[]{:S(2)}) collective-permute-start(bf16[176,512]{1,0:T(8,128)(2,1)S(1)} %get-tuple-element.113), channel_id=1, source_target_pairs={{0,1},{1,0},{2,3},{3,2},{4,5},{5,4},{6,7},{7,6},{8,9},{9,8},{10,11... | collective-permute-start | bytes 540680 | tf_op jit(solution)/shard_map/ppermute | solution.py:296
  2.7 10.7 %collective-permute-start.3 = (bf16[176,512]{1,0:T(8,128)(2,1)S(1)}, bf16[176,512]{1,0:T(8,128)(2,1)S(1)}, u32[]{:S(2)}, u32[]{:S(2)}) collective-permute-start(bf16[176,512]{1,0:T(8,128)(2,1)S(1)} %get-tuple-element.114), channel_id=1, source_target_pairs={{0,2},{1,3},{2,0},{3,1},{4,6},{5,7},{6,4},{7,5},{8,10},{9,11},{10,... | collective-permute-start | bytes 540680 | tf_op jit(solution)/shard_map/ppermute | solution.py:296
  5.3 8.7 %collective-permute-start.4 = (bf16[176,512]{1,0:T(8,128)(2,1)S(1)}, bf16[176,512]{1,0:T(8,128)(2,1)S(1)}, u32[]{:S(2)}, u32[]{:S(2)}) collective-permute-start(bf16[176,512]{1,0:T(8,128)(2,1)S(1)} %get-tuple-element.115), channel_id=1, source_target_pairs={{0,3},{1,2},{2,1},{3,0},{4,7},{5,6},{6,5},{7,4},{8,11},{9,10},{10,... | collective-permute-start | bytes 540680 | tf_op jit(solution)/shard_map/ppermute | solution.py:296
  5.4 6.2 %collective-permute-start.1 = (bf16[64,512]{1,0:T(8,128)(2,1)S(1)}, bf16[64,512]{1,0:T(8,128)(2,1)S(1)}, u32[]{:S(2)}, u32[]{:S(2)}) collective-permute-start(bf16[64,512]{1,0:T(8,128)(2,1)S(1)} %get-tuple-element.102.refs_0_.nodes_ref), channel_id=1, source_target_pairs={{0,4},{1,5},{2,6},{3,7},{4,0},{5,1},{6,2},{7,3},{8,12},{9,13},{10,... | collective-permute-start | bytes 196616 | tf_op jit(solution)/shard_map/ppermute | solution.py:296
  7.2 6.3 %collective-permute-start = (bf16[64,512]{1,0:T(8,128)(2,1)S(1)}, bf16[64,512]{1,0:T(8,128)(2,1)S(1)}, u32[]{:S(2)}, u32[]{:S(2)}) collective-permute-start(bf16[64,512]{1,0:T(8,128)(2,1)S(1)} %get-tuple-element.102.refs_0_.nodes_ref), channel_id=1, source_target_pairs={{0,12},{1,13},{2,14},{3,15},{4,8},{5,9},{6,10},{7,11},{8,4},{9,5},... | collective-permute-start | bytes 196616 | tf_op jit(solution)/shard_map/ppermute | solution.py:296
  14.0 5.9 %collective-permute-start.5 = (bf16[64,512]{1,0:T(8,128)(2,1)S(1)}, bf16[64,512]{1,0:T(8,128)(2,1)S(1)}, u32[]{:S(2)}, u32[]{:S(2)}) collective-permute-start(bf16[64,512]{1,0:T(8,128)(2,1)S(1)} %collective-permute-done), channel_id=1, source_target_pairs={{0,4},{1,5},{2,6},{3,7},{4,0},{5,1},{6,2},{7,3},{8,12},{9,13},{10,... | collective-permute-start | bytes 196616 | tf_op jit(solution)/shard_map/ppermute | solution.py:296
  15.7 6.9 %collective-permute-start.8 = (bf16[192,512]{1,0:T(8,128)(2,1)S(1)}, bf16[192,512]{1,0:T(8,128)(2,1)S(1)}, u32[]{:S(2)}, u32[]{:S(2)}) collective-permute-start(bf16[192,512]{1,0:T(8,128)(2,1)S(1)} %pad_maximum_fusion.2), channel_id=1, source_target_pairs={{0,2},{1,3},{2,0},{3,1},{4,6},{5,7},{6,4},{7,5},{8,10},{9,11},{10,... | collective-permute-start | bytes 589832 | tf_op jit(solution)/shard_map/ppermute | solution.py:296
  20.0 2.6 %collective-permute-start.7 = (bf16[256,512]{1,0:T(8,128)(2,1)S(1)}, bf16[256,512]{1,0:T(8,128)(2,1)S(1)}, u32[]{:S(2)}, u32[]{:S(2)}) collective-permute-start(bf16[256,512]{1,0:T(8,128)(2,1)S(1)} %constant_dynamic-update-slice_fusion.refs_4_), channel_id=1, source_target_pairs={{0,1},{1,0},{2,3},{3,2},{4,5},{5,4},{6,7},{7,6},{8,9},{9,8},{10,11... | collective-permute-start | bytes 786440 | tf_op jit(solution)/shard_map/ppermute | solution.py:296
  20.1 4.7 %collective-permute-start.6 = (bf16[64,512]{1,0:T(8,128)(2,1)S(1)}, bf16[64,512]{1,0:T(8,128)(2,1)S(1)}, u32[]{:S(2)}, u32[]{:S(2)}) collective-permute-start(bf16[64,512]{1,0:T(8,128)(2,1)S(1)} %collective-permute-done.5), channel_id=1, source_target_pairs={{0,2},{1,3},{2,0},{3,1},{4,6},{5,7},{6,4},{7,5},{8,10},{9,11},{10,... | collective-permute-start | bytes 196616 | tf_op jit(solution)/shard_map/ppermute | solution.py:296
  24.8 1.6 %collective-permute-start.9 = (bf16[256,512]{1,0:T(8,128)(2,1)S(1)}, bf16[256,512]{1,0:T(8,128)(2,1)S(1)}, u32[]{:S(2)}, u32[]{:S(2)}) collective-permute-start(bf16[256,512]{1,0:T(8,128)(2,1)S(1)} %constant_dynamic-update-slice_fusion.4.refs_4_), channel_id=1, source_target_pairs={{0,1},{1,0},{2,3},{3,2},{4,5},{5,4},{6,7},{7,6},{8,9},{9,8},{10,11... | collective-permute-start | bytes 786440 | tf_op jit(solution)/shard_map/ppermute | solution.py:296
  28.8 6.9 %collective-permute-start.10 = (bf16[64,512]{1,0:T(8,128)(2,1)S(1)}, bf16[64,512]{1,0:T(8,128)(2,1)S(1)}, u32[]{:S(2)}, u32[]{:S(2)}) collective-permute-start(bf16[64,512]{1,0:T(8,128)(2,1)S(1)} %get-tuple-element.161), channel_id=1, source_target_pairs={{0,8},{1,9},{2,10},{3,11},{4,12},{5,13},{6,14},{7,15},{8,0},{9,1},... | collective-permute-start | bytes 196616 | tf_op jit(solution)/shard_map/ppermute | solution.py:296
  31.5 6.4 %collective-permute-start.11 = (bf16[64,512]{1,0:T(8,128)(2,1)S(1)}, bf16[64,512]{1,0:T(8,128)(2,1)S(1)}, u32[]{:S(2)}, u32[]{:S(2)}) collective-permute-start(bf16[64,512]{1,0:T(8,128)(2,1)S(1)} %get-tuple-element.162), channel_id=1, source_target_pairs={{0,12},{1,13},{2,14},{3,15},{4,8},{5,9},{6,10},{7,11},{8,4},{9,5},... | collective-permute-start | bytes 196616 | tf_op jit(solution)/shard_map/ppermute | solution.py:296
  31.9 6.2 %collective-permute-start.12 = (bf16[64,512]{1,0:T(8,128)(2,1)S(1)}, bf16[64,512]{1,0:T(8,128)(2,1)S(1)}, u32[]{:S(2)}, u32[]{:S(2)}) collective-permute-start(bf16[64,512]{1,0:T(8,128)(2,1)S(1)} %get-tuple-element.163), channel_id=1, source_target_pairs={{0,4},{1,5},{2,6},{3,7},{4,0},{5,1},{6,2},{7,3},{8,12},{9,13},{10,... | collective-permute-start | bytes 196616 | tf_op jit(solution)/shard_map/ppermute | solution.py:296
  38.8 6.0 %collective-permute-start.14 = (bf16[64,512]{1,0:T(8,128)(2,1)S(1)}, bf16[64,512]{1,0:T(8,128)(2,1)S(1)}, u32[]{:S(2)}, u32[]{:S(2)}) collective-permute-start(bf16[64,512]{1,0:T(8,128)(2,1)S(1)} %shard_map.192.refs_0_.nodes_ref), channel_id=1, source_target_pairs={{0,4},{1,5},{2,6},{3,7},{4,0},{5,1},{6,2},{7,3},{8,12},{9,13},{10,... | collective-permute-start | bytes 196616 | tf_op jit(solution)/shard_map/ppermute | solution.py:296
  39.5 6.2 %collective-permute-start.13 = (bf16[64,512]{1,0:T(8,128)(2,1)S(1)}, bf16[64,512]{1,0:T(8,128)(2,1)S(1)}, u32[]{:S(2)}, u32[]{:S(2)}) collective-permute-start(bf16[64,512]{1,0:T(8,128)(2,1)S(1)} %shard_map.192.refs_0_.nodes_ref), channel_id=1, source_target_pairs={{0,12},{1,13},{2,14},{3,15},{4,8},{5,9},{6,10},{7,11},{8,4},{9,5},... | collective-permute-start | bytes 196616 | tf_op jit(solution)/shard_map/ppermute | solution.py:296
  45.7 4.3 %collective-permute-start.15 = (bf16[64,512]{1,0:T(8,128)(2,1)S(1)}, bf16[64,512]{1,0:T(8,128)(2,1)S(1)}, u32[]{:S(2)}, u32[]{:S(2)}) collective-permute-start(bf16[64,512]{1,0:T(8,128)(2,1)S(1)} %collective-permute-done.13), channel_id=1, source_target_pairs={{0,4},{1,5},{2,6},{3,7},{4,0},{5,1},{6,2},{7,3},{8,12},{9,13},{10,... | collective-permute-start | bytes 196616 | tf_op jit(solution)/shard_map/ppermute | solution.py:296
  45.7 5.8 %collective-permute-start.18 = (bf16[192,512]{1,0:T(8,128)(2,1)S(1)}, bf16[192,512]{1,0:T(8,128)(2,1)S(1)}, u32[]{:S(2)}, u32[]{:S(2)}) collective-permute-start(bf16[192,512]{1,0:T(8,128)(2,1)S(1)} %pad_maximum_fusion.3), channel_id=1, source_target_pairs={{0,2},{1,3},{2,0},{3,1},{4,6},{5,7},{6,4},{7,5},{8,10},{9,11},{10,... | collective-permute-start | bytes 589832 | tf_op jit(solution)/shard_map/ppermute | solution.py:296
  49.9 1.6 %collective-permute-start.17 = (bf16[256,512]{1,0:T(8,128)(2,1)S(1)}, bf16[256,512]{1,0:T(8,128)(2,1)S(1)}, u32[]{:S(2)}, u32[]{:S(2)}) collective-permute-start(bf16[256,512]{1,0:T(8,128)(2,1)S(1)} %pad_maximum_fusion.1.refs_4_), channel_id=1, source_target_pairs={{0,1},{1,0},{2,3},{3,2},{4,5},{5,4},{6,7},{7,6},{8,9},{9,8},{10,11... | collective-permute-start | bytes 786440 | tf_op jit(solution)/shard_map/ppermute | solution.py:296
  50.0 4.5 %collective-permute-start.16 = (bf16[64,512]{1,0:T(8,128)(2,1)S(1)}, bf16[64,512]{1,0:T(8,128)(2,1)S(1)}, u32[]{:S(2)}, u32[]{:S(2)}) collective-permute-start(bf16[64,512]{1,0:T(8,128)(2,1)S(1)} %collective-permute-done.15), channel_id=1, source_target_pairs={{0,2},{1,3},{2,0},{3,1},{4,6},{5,7},{6,4},{7,5},{8,10},{9,11},{10,... | collective-permute-start | bytes 196616 | tf_op jit(solution)/shard_map/ppermute | solution.py:296
  58.5 1.7 %collective-permute-start.23 = (bf16[320,512]{1,0:T(8,128)(2,1)S(1)}, bf16[320,512]{1,0:T(8,128)(2,1)S(1)}, u32[]{:S(2)}, u32[]{:S(2)}) collective-permute-start(bf16[320,512]{1,0:T(8,128)(2,1)S(1)} %get-tuple-element.199), channel_id=1, source_target_pairs={{0,1},{1,0},{2,3},{3,2},{4,5},{5,4},{6,7},{7,6},{8,9},{9,8},{10,11... | collective-permute-start | bytes 983048 | tf_op jit(solution)/shard_map/ppermute | solution.py:296
  60.3 11.7 %collective-permute-start.24 = (bf16[320,512]{1,0:T(8,128)(2,1)S(1)}, bf16[320,512]{1,0:T(8,128)(2,1)S(1)}, u32[]{:S(2)}, u32[]{:S(2)}) collective-permute-start(bf16[320,512]{1,0:T(8,128)(2,1)S(1)} %pad_maximum_fusion), channel_id=1, source_target_pairs={{0,2},{1,3},{2,0},{3,1},{4,6},{5,7},{6,4},{7,5},{8,10},{9,11},{10,... | collective-permute-start | bytes 983048 | tf_op jit(solution)/shard_map/ppermute | solution.py:296
  61.7 7.6 %collective-permute-start.20 = (bf16[64,512]{1,0:T(8,128)(2,1)S(1)}, bf16[64,512]{1,0:T(8,128)(2,1)S(1)}, u32[]{:S(2)}, u32[]{:S(2)}) collective-permute-start(bf16[64,512]{1,0:T(8,128)(2,1)S(1)} %get-tuple-element.193), channel_id=1, source_target_pairs={{0,8},{1,9},{2,10},{3,11},{4,12},{5,13},{6,14},{7,15},{8,0},{9,1},... | collective-permute-start | bytes 196616 | tf_op jit(solution)/shard_map/ppermute | solution.py:296
  63.9 6.2 %collective-permute-start.21 = (bf16[64,512]{1,0:T(8,128)(2,1)S(1)}, bf16[64,512]{1,0:T(8,128)(2,1)S(1)}, u32[]{:S(2)}, u32[]{:S(2)}) collective-permute-start(bf16[64,512]{1,0:T(8,128)(2,1)S(1)} %get-tuple-element.194), channel_id=1, source_target_pairs={{0,12},{1,13},{2,14},{3,15},{4,8},{5,9},{6,10},{7,11},{8,4},{9,5},... | collective-permute-start | bytes 196616 | tf_op jit(solution)/shard_map/ppermute | solution.py:296
  65.4 5.2 %collective-permute-start.22 = (bf16[64,512]{1,0:T(8,128)(2,1)S(1)}, bf16[64,512]{1,0:T(8,128)(2,1)S(1)}, u32[]{:S(2)}, u32[]{:S(2)}) collective-permute-start(bf16[64,512]{1,0:T(8,128)(2,1)S(1)} %get-tuple-element.195), channel_id=1, source_target_pairs={{0,4},{1,5},{2,6},{3,7},{4,0},{5,1},{6,2},{7,3},{8,12},{9,13},{10,... | collective-permute-start | bytes 196616 | tf_op jit(solution)/shard_map/ppermute | solution.py:296
  (1 other events, 1.5 us)

commit v4 on v3

--- a/solution.py
+++ b/solution.py
@@ -172,36 +172,34 @@
         scatter_refs[pair // 2][...] = match_columns(jnp.concatenate(rows_r, axis=1), span)
 
 
-def far_second_kernel(layer, lines, slot, keep, *refs):
-    slots, refs = refs[0:PLANE], refs[PLANE:]
+def far_second_kernel(layer, lines, slot, pairs, chained, keep, *refs):
+    count = 2 * len(pairs)
+    slots, refs = refs[0:count], refs[count:]
     straight_ref, across_ref, pre_ref, late_ref, *scatter_refs = refs[0:6]
-    sum_ref, win_ref, wout_ref = refs[6:9]
-    vecs, refs = [v[layer : layer + 1, :] for v in refs[9:12]], refs[12:]
-    count = PLANE if keep else 3
-    new_refs, own_ref, part_refs = refs[0:count], refs[count], refs[count + 1 :]
+    total, refs = (refs[6][...], refs[7:]) if chained else (None, refs[6:])
+    win_ref, wout_ref = refs[0:2]
+    vecs, refs = [v[layer : layer + 1, :] for v in refs[2:5]], refs[5:]
+    new_refs, sum_refs = refs[0:count], refs[count:]
     width = pre_ref.shape[1]
     table = jnp.concatenate([straight_ref[...], across_ref[...]], axis=0)
-    total = None
-    for pair in range(0, PLANE, 2):
-        rows = slice(pair * slot, (pair + 2) * slot)
+    for i, pair in enumerate(pairs):
+        rows, own = slice(pair * slot, (pair + 2) * slot), slots[2 * i : 2 * i + 2]
         senders = mm(late_ref[rows, :], table).astype(BF)
         pre_act = pre_ref[rows, :] + mm(senders, win_ref[width : 2 * width, :])
         normed = edge_tail(pre_act, wout_ref[...], *vecs)
-        edges = jnp.concatenate([ref[0:slot, :] for ref in slots[pair : pair + 2]], axis=0)
+        edges = jnp.concatenate([ref[0:slot, :] for ref in own], axis=0)
         new = (edges.astype(F32) + normed).astype(BF)
         for j in range(2):
-            piece = new[j * slot : (j + 1) * slot, :]
+            new_refs[2 * i + j][0:slot, :] = new[j * slot : (j + 1) * slot, :]
             if keep:
-                new_refs[pair + j][0:slot, :] = piece
-                new_refs[pair + j][slot:, :] = slots[pair + j][slot:, :]
-            elif j == 0:
-                new_refs[pair][...] = piece
-            else:
-                new_refs[1][pair // 2 * slot : (pair // 2 + 1) * slot, :] = piece
+                new_refs[2 * i + j][slot:, :] = own[j][slot:, :]
         part = mm(scatter_refs[pair // 2][...], normed.astype(BF))
         total = part if total is None else total + part
-    own_ref[...] = total[0:COARSE, :] + sum_ref[0:COARSE, :]
-    for i, ref in enumerate(part_refs):
+    if len(sum_refs) == 1:
+        sum_refs[0][...] = total
+        return
+    sum_refs[0][...] = total[0:COARSE, :]
+    for i, ref in enumerate(sum_refs[1:]):
         ref[...] = total[(i + 1) * COARSE : (i + 2) * COARSE, :].astype(BF)
 
 
@@ -214,33 +212,33 @@
 
 def rest_kernel(layer, nodes_ref, sum_ref, win_ref, wout_ref, *refs):
     sums = sum_ref[COARSE:, :]
-    refs[-1][...] = node_update(layer, nodes_ref[...], sums, win_ref, wout_ref, refs[0:3])
-
-
-def coarse_kernel(layer, nodes_ref, rest_ref, own_ref, *refs):
-    part_refs, (win_ref, wout_ref), vec_refs, out_ref = refs[:-6], refs[-6:-4], refs[-4:-1], refs[-1]
-    sums = own_ref[...]
-    for ref in part_refs:
+    new = node_update(layer, nodes_ref[...], sums, win_ref, wout_ref, refs[0:3])
+    if len(refs) == 4:
+        refs[3][...] = new
+        return
+    pos_ref, out_ref, back_ref = refs[3:]
+    out_ref[...] = new
+    back_ref[...] = match_rows(as_column(pos_ref[...]), back_ref.shape[1])
+
+
+def coarse_kernel(layer, lines, nodes_ref, sum_ref, *refs):
+    part_refs, refs = refs[0:lines], refs[lines:]
+    (win_ref, wout_ref), vec_refs, refs = refs[0:2], refs[2:5], refs[5:]
+    if len(refs) > 1:
+        rest_ref, back_ref, *slot_refs, out_ref, far_ref = refs
+        slots = jnp.concatenate([ref[...] for ref in slot_refs], axis=0)
+        far_ref[...] = mm(back_ref[...], slots).astype(BF)
+        out_ref[COARSE:, :] = rest_ref[...]
+    else:
+        out_ref = refs[0]
+    sums = sum_ref[0:COARSE, :] + part_refs[0][...]
+    for ref in part_refs[1:]:
         sums = sums + ref[...].astype(F32)
     out_ref[0:COARSE, :] = node_update(layer, nodes_ref[...], sums, win_ref, wout_ref, vec_refs)
-    if out_ref.shape[0] > COARSE:
-        out_ref[COARSE:, :] = rest_ref[...]
-
-
-def restore_kernel(slot, pos_ref, *refs):
-    slots, out_ref = refs[:-1], refs[-1]
-    column = as_column(pos_ref[...])
-    total = None
-    pieces = [slots[0][...], slots[1][0:slot, :], slots[2][0:slot, :], slots[2][slot:, :]]
-    for m, rows in enumerate(pieces):
-        piece = mm(match_rows(column - m * slot, slot), rows)
-        total = piece if total is None else total + piece
-    out_ref[...] = total.astype(BF)
 
 
 def call(kernel, outs, args, flops, limit, first=None, scratch=()):
-    bytes_accessed = sum(a.size * a.dtype.itemsize for a in args)
-    bytes_accessed += sum(o.size * o.dtype.itemsize for o in outs)
+    bytes_accessed = sum(a.size * a.dtype.itemsize for a in [*args, *outs]) if flops or first == 0 else 0
     whole = pl.BlockSpec(memory_space=pltpu.VMEM)
     specs = [whole] * len(args)
     if first is not None:
@@ -334,29 +332,27 @@
     far_rows, span = PLANE * slot, lines * COARSE
     cut = local_count // 3 * 2 // 256 * 256
     pieces = [slice(0, cut), slice(cut, local_count)] if cut else [slice(0, local_count)]
-    hop = None
-    if lines == 4:
-        hop = [swap(coarse, 12), swap(coarse, 4)]
-        hop, first, slots = tied((hop, first, slots))
     local, local_send, local_recv = first[0:3]
     edge_vecs, weights = first[3:6], [first[6:8]]
     for l in range(layers):
         last = l == layers - 1
 
-        def local_part(rows, before=()):
+        def local_part(rows, before=(), share=1):
             return call(
                 functools.partial(local_kernel, l, rows),
                 [shape((rows.stop, width), BF), shape((node_count, width), F32)],
                 [coarse, rest, local, local_send, local_recv, *weights[l], *edge_vecs, *before],
-                2 * (rows.stop - rows.start) * width * (3 * node_count + 4 * width),
+                2 * (rows.stop - rows.start) * width * (3 * node_count + 4 * width) * share,
                 limit,
             )
 
-        done = local_part(pieces[0])
+        done = local_part(pieces[0], share=min(l, 1))
         if lines == 4:
-            z3, z1 = hop if l == 0 else (swap(coarse, 12), swap(coarse, 4))
+            z3, z1 = swap(coarse, 12), swap(coarse, 4)
             if l:
                 z3, z1, done = tied((z3, z1, done))
+            else:
+                z3, z1, done, slots = tied((z3, z1, done, slots))
             near = jnp.concatenate([coarse, z1, z3], axis=0)
             z2 = swap(z3, 4)
             across = swap(near, 2)
@@ -364,12 +360,10 @@
             near = [coarse if z == 0 else swap(coarse, PLANE * z) for z in place]
             near, z2 = jnp.concatenate(near[:-1], axis=0), near[-1]
             across = swap(near, 2)
-        if l == 0:
+        if not last:
             z2, done = tied((z2, done))
-        for rows in pieces[1:]:
-            done = local_part(rows, done)
-        if l:
-            z2, done = tied((z2, done))
+            for rows in pieces[1:]:
+                done = local_part(rows, done)
         late = swap(z2, 2)
         table = jnp.concatenate([near, z2], axis=0)
         tables = [table, swap(table, 1)]
@@ -382,27 +376,34 @@
             limit,
         )
         late, found, done = tied((late, found, done))
-        local, sums = done
         late = jnp.concatenate([across, late], axis=0)
         late = [late, swap(late, 1)]
-        moved = [shape((padded, width), BF)] * PLANE
+        moved = shape((slot if last else padded, width), BF)
+        parts_shape = [shape((COARSE, width), F32)] + [shape((COARSE, width), BF)] * (lines - 1)
+
+        def far_part(pairs, before, outs):
+            return call(
+                functools.partial(far_second_kernel, l, lines, slot, pairs, len(before) > 0, not last),
+                [moved] * (2 * len(pairs)) + outs,
+                [*[v for i in pairs for v in slots[i : i + 2]], *late, *found, *before]
+                + [*weights[l], *edge_vecs],
+                4 * len(pairs) * slot * width * (3 * span + 2 * width),
+                limit,
+            )
+
         if last:
-            moved = [shape((rows * slot, width), BF) for rows in (1, 2, 1)]
-        far = call(
-            functools.partial(far_second_kernel, l, lines, slot, not last),
-            moved
-            + [shape((COARSE, width), F32)]
-            + [shape((COARSE, width), BF)] * (lines - 1),
-            [*slots, *late, *found, sums, *weights[l], *edge_vecs],
-            2 * far_rows * width * (3 * span + 2 * width),
-            limit,
-        )
-        slots, parts = [*far[: len(moved)]], far[len(moved) :]
-        if last:
-            kept, paired, crossing = slots
-            paired = swap(paired, 1)
-            crossing = jnp.concatenate([crossing, paired[slot:]], axis=0)
-            slots = [kept, paired, swap(crossing, 2)]
+            ahead = far_part((2,), [], [shape((span, width), F32)])
+            passed = swap(ahead[1], 1)
+            passed, far = tied((passed, far_part((0,), [ahead[2]], parts_shape)))
+            crossing = jnp.concatenate([ahead[0], passed], axis=0)
+            slots, parts = [far[0], swap(far[1], 1), swap(crossing, 2)], far[2:]
+            parts, done = tied((parts, done))
+            for rows in pieces[1:]:
+                done = local_part(rows, done)
+        else:
+            far = far_part((0, 2), [], parts_shape)
+            slots, parts = [*far[:PLANE]], far[PLANE:]
+        local, sums = done
         far_parts = [swap(parts[i], PLANE * place[i]) for i in range(lines - 1, 0, -1)]
         parts = [parts[0], *far_parts]
         if l == 0:
@@ -417,26 +418,25 @@
         ends = [node_in, node_out, *node_vecs]
         rest = call(
             functools.partial(rest_kernel, l),
-            [shape((node_count - COARSE, width), BF)],
-            [rest, sums, *ends],
+            [shape((node_count - COARSE, width), BF)]
+            + [shape((far_count, far_rows), BF)] * last,
+            [rest, sums, *ends] + [pos] * last,
             6 * (node_count - COARSE) * width * width,
             limit,
-        )[0]
-        coarse = call(
-            functools.partial(coarse_kernel, l),
-            [shape((node_count if last else COARSE, width), BF)],
-            [coarse, rest, *parts, *ends],
+        )
+        if last:
+            return_shapes = [shape((node_count, width), BF), shape((far_count, width), BF)]
+            extra = [*rest, *slots]
+        else:
+            return_shapes, extra, rest = [shape((COARSE, width), BF)], [], rest[0]
+        coarse, *far_out = call(
+            functools.partial(coarse_kernel, l, lines),
+            return_shapes,
+            [coarse, sums, *parts, *ends, *extra],
             6 * COARSE * width * width,
             limit,
-        )[0]
-    far_out = call(
-        functools.partial(restore_kernel, slot),
-        [shape((far_count, width), BF)],
-        [pos, *slots],
-        2 * PLANE * slot * far_count * width,
-        limit,
-    )[0]
-    return (coarse, local, far_out)
+        )
+    return (coarse, local, far_out[0])
 
 
 def solution(mesh):

time: 73.4 us -> 72.4 us (0.986)
  waiting for transfers between devices: 15.9 us -> 14.5 us
  starting transfers between devices: 26.6 us -> 27.5 us
    ppermute x25 -> x26, waiting for transfers between devices: 15.9 us -> 14.5 us  [swap(): lax.ppermute(values, 'patch', [(i, i ^ distance) for i in range(devices)])]
    ppermute x25 -> x26, starting transfers between devices: 26.6 us -> 27.5 us  [swap(): lax.ppermute(values, 'patch', [(i, i ^ distance) for i in range(devices)])]
  transfers between devices with their start and end apart: 25 -> 26, of which waited for: 14 -> 11; matrix products, arithmetic and copies ran while one was open for 0% -> 0% of each run, Pallas kernels for 29% -> 30%
where the time goes in v4:
time: 72.4 us; the launch traced here: 72.2 us
  Pallas kernels  29.2 us (40%)
  starting transfers between devices  27.5 us (38%)
  waiting for transfers between devices  14.5 us (20%)
  between operations  0.93 us (1%)
    pallas_call x16, Pallas kernels, call(): pl.pallas_call(kernel, out_shape=outs, in_specs=specs, out_specs=[whole]...  29.2 us
    ppermute x26, starting transfers between devices, swap(): lax.ppermute(values, 'patch', [(i, i ^ distance) for i in range(devices)])  27.5 us
    ppermute x26, waiting for transfers between devices, swap(): lax.ppermute(values, 'patch', [(i, i ^ distance) for i in range(devices)])  14.5 us
  transfers between devices with their start and end apart: 26, of which 11 were waited for; matrix products, arithmetic and copies ran while one was open for 0% of the time, Pallas kernels for 30%

profile of v4, /device:TPU:0, one launch (start us, length us, event | category | flops | bytes accessed | tf_op | source)
XLA Modules:
  0.0 72.2 jit_solution(11978670500284275306)
XLA Ops:
  0.6 1.6 %shard_map.184 = (s32[1,256]{1,0:T(1,128)S(1)}, bf16[64,512]{1,0:T(8,128)(2,1)S(1)}, bf16[192,512]{1,0:T(8,128)(2,1)S(1)}, bf16[176,512]{1,0:T(8,128)(2,1)S(1)},...) custom-call(s32[1]{0:T(128)} %bitcast.own_ref, s32[1,256]{1,0:T(1,128)} %bitcast.3, ...), custom_call_target="tpu_custom_call" | custom-call | flops 167772160 | bytes 1510404 | tf_op jit(solution)/shard_map/pallas_call | solution.py:250
  2.7 2.6 %collective-permute-start.3 = (bf16[176,512]{1,0:T(8,128)(2,1)S(1)}, bf16[176,512]{1,0:T(8,128)(2,1)S(1)}, u32[]{:S(2)}, u32[]{:S(2)}) collective-permute-start(bf16[176,512]{1,0:T(8,128)(2,1)S(1)} %get-tuple-element.126), channel_id=1, source_target_pairs={{0,2},{1,3},{2,0},{3,1},{4,6},{5,7},{6,4},{7,5},{8,10},{9,11},{10,... | collective-permute-start | bytes 540680 | tf_op jit(solution)/shard_map/ppermute | solution.py:294
  5.4 1.8 %collective-permute-start.1 = (bf16[64,512]{1,0:T(8,128)(2,1)S(1)}, bf16[64,512]{1,0:T(8,128)(2,1)S(1)}, u32[]{:S(2)}, u32[]{:S(2)}) collective-permute-start(bf16[64,512]{1,0:T(8,128)(2,1)S(1)} %get-tuple-element.112.refs_0_.nodes_ref), channel_id=1, source_target_pairs={{0,4},{1,5},{2,6},{3,7},{4,0},{5,1},{6,2},{7,3},{8,12},{9,13},{10,... | collective-permute-start | bytes 196616 | tf_op jit(solution)/shard_map/ppermute | solution.py:294
  7.2 2.5 %collective-permute-start = (bf16[64,512]{1,0:T(8,128)(2,1)S(1)}, bf16[64,512]{1,0:T(8,128)(2,1)S(1)}, u32[]{:S(2)}, u32[]{:S(2)}) collective-permute-start(bf16[64,512]{1,0:T(8,128)(2,1)S(1)} %get-tuple-element.112.refs_0_.nodes_ref), channel_id=1, source_target_pairs={{0,12},{1,13},{2,14},{3,15},{4,8},{5,9},{6,10},{7,11},{8,4},{9,5},... | collective-permute-start | bytes 196616 | tf_op jit(solution)/shard_map/ppermute | solution.py:294
  9.7 1.9 %shard_map.185 = (bf16[768,512]{1,0:T(8,128)(2,1)S(1)}, s32[768]{0:T(1024)S(1)}, s32[768]{0:T(1024)S(1)}, f32[2,512]{1,0:T(2,128)S(1)}, f32[2,512]{1,0:T(2,128)S...) custom-call(bf16[768,512]{1,0:T(8,128)(2,1)} %refs_0_.1, s32[768]{0:T(1024)} %refs_1_.1, ...), custom_call_target="tpu_custom_call" | custom-call | bytes 7901184 | tf_op jit(solution)/shard_map/pallas_call | solution.py:250
  11.6 2.7 %shard_map.186 = (bf16[512,512]{1,0:T(8,128)(2,1)S(1)}, f32[256,512]{1,0:T(8,128)S(1)}) custom-call(bf16[64,512]{1,0:T(8,128)(2,1)S(1)} %get-tuple-element.112.refs_0_.nodes_ref, bf16[192,512]{1,0:T(8,128)(2,1)S(1)} %get-tuple-element.113.refs_1_.nodes_ref, bf16[768,512]{1,0:T(8,128)(2,1)S(1)} %get-tuple-element.114.refs_2_, ...), custom_call_target="tpu_custom_call" | custom-call | tf_op jit(solution)/shard_map/pallas_call | solution.py:250
  15.7 1.6 %collective-permute-start.8 = (bf16[192,512]{1,0:T(8,128)(2,1)S(1)}, bf16[192,512]{1,0:T(8,128)(2,1)S(1)}, u32[]{:S(2)}, u32[]{:S(2)}) collective-permute-start(bf16[192,512]{1,0:T(8,128)(2,1)S(1)} %pad_maximum_fusion.2), channel_id=1, source_target_pairs={{0,2},{1,3},{2,0},{3,1},{4,6},{5,7},{6,4},{7,5},{8,10},{9,11},{10,... | collective-permute-start | bytes 589832 | tf_op jit(solution)/shard_map/ppermute | solution.py:294
  20.2 1.7 %shard_map.188 = (bf16[768,512]{1,0:T(8,128)(2,1)S(1)}, f32[256,512]{1,0:T(8,128)S(1)}) custom-call(bf16[64,512]{1,0:T(8,128)(2,1)S(1)} %get-tuple-element.112.refs_0_.nodes_ref, bf16[192,512]{1,0:T(8,128)(2,1)S(1)} %get-tuple-element.113.refs_1_.nodes_ref, bf16[768,512]{1,0:T(8,128)(2,1)S(1)} %get-tuple-element.114.refs_2_, ...), custom_call_target="tpu_custom_call" | custom-call | flops 738197504 | bytes 5523456 | tf_op jit(solution)/shard_map/pallas_call | solution.py:250
  23.3 2.1 %shard_map.187 = (f32[640,512]{1,0:T(8,128)S(1)}, bf16[640,512]{1,0:T(8,128)(2,1)S(1)}, bf16[256,320]{1,0:T(8,128)(2,1)S(1)}, bf16[256,320]{1,0:T(8,128)(2,1)S(1)}) custom-call(bf16[176,512]{1,0:T(8,128)(2,1)S(1)} %get-tuple-element.132.refs_0_, bf16[176,512]{1,0:T(8,128)(2,1)S(1)} %collective-permute-done.2.refs_1_, ...), custom_call_target="tpu_custom_call" | custom-call | flops 1509949440 | bytes 5111808 | tf_op jit(solution)/shard_map/pallas_call | solution.py:250
  27.1 2.4 %shard_map.189 = (bf16[176,512]{1,0:T(8,128)(2,1)S(1)}, bf16[176,512]{1,0:T(8,128)(2,1)S(1)}, bf16[176,512]{1,0:T(8,128)(2,1)S(1)}, bf16[176,512]{1,0:T(8,128)(2...) custom-call(bf16[176,512]{1,0:T(8,128)(2,1)S(1)} %get-tuple-element., ...), custom_call_target="tpu_custom_call" | custom-call | flops 1174405120 | bytes 6696960 | tf_op jit(solution)/shard_map/pallas_call | solution.py:250
  29.5 2.7 %collective-permute-start.10 = (bf16[64,512]{1,0:T(8,128)(2,1)S(1)}, bf16[64,512]{1,0:T(8,128)(2,1)S(1)}, u32[]{:S(2)}, u32[]{:S(2)}) collective-permute-start(bf16[64,512]{1,0:T(8,128)(2,1)S(1)} %get-tuple-element.153), channel_id=1, source_target_pairs={{0,8},{1,9},{2,10},{3,11},{4,12},{5,13},{6,14},{7,15},{8,0},{9,1},... | collective-permute-start | bytes 196616 | tf_op jit(solution)/shard_map/ppermute | solution.py:294
  33.1 2.6 %shard_map.190 = (bf16[2,1024,512]{2,1,0:T(8,128)(2,1)S(1)}, bf16[2,512,512]{2,1,0:T(8,128)(2,1)S(1)}, f32[2,512]{1,0:T(2,128)S(1)}, f32[2,512]{1,0:T(2,128)S(1)...) custom-call(bf16[2,1024,512]{2,1,0:T(8,128)(2,1)} %refs_0_.2, ...), custom_call_target="tpu_custom_call" | custom-call | bytes 12607488 | tf_op jit(solution)/shard_map/pallas_call | solution.py:250
  36.5 2.0 %collective-permute-done.11.refs_2_ = bf16[64,512]{1,0:T(8,128)(2,1)S(1)} collective-permute-done((bf16[64,512]{1,0:T(8,128)(2,1)S(1)}, bf16[64,512]{1,0:T(8,128)(2,1)S(1)}, u32[]{:S(2)}, u32[]{:S(2)}) %collective-permute-start.11) | collective-permute-done | bytes 65568 | tf_op jit(solution)/shard_map/ppermute | solution.py:294
  39.9 2.3 %collective-permute-start.13 = (bf16[64,512]{1,0:T(8,128)(2,1)S(1)}, bf16[64,512]{1,0:T(8,128)(2,1)S(1)}, u32[]{:S(2)}, u32[]{:S(2)}) collective-permute-start(bf16[64,512]{1,0:T(8,128)(2,1)S(1)} %shard_map.191.refs_0_.nodes_ref), channel_id=1, source_target_pairs={{0,12},{1,13},{2,14},{3,15},{4,8},{5,9},{6,10},{7,11},{8,4},{9,5},... | collective-permute-start | bytes 196616 | tf_op jit(solution)/shard_map/ppermute | solution.py:294
  42.2 2.7 %shard_map.193 = (bf16[512,512]{1,0:T(8,128)(2,1)S(1)}, f32[256,512]{1,0:T(8,128)S(1)}) custom-call(bf16[64,512]{1,0:T(8,128)(2,1)S(1)} %shard_map.191.refs_0_.nodes_ref, bf16[192,512]{1,0:T(8,128)(2,1)S(1)} %shard_map.192.refs_1_.nodes_ref, bf16[768,512]{1,0:T(8,128)(2,1)S(1)} %get-tuple-element.168.refs_2_, s32[768]{0:T(1024)S(1)} %get-tuple-element.115.refs_3_, ...), custom_call_target="tpu_custom_call" | custom-call | flops 1476395008 | bytes 4212736 | tf_op jit(solution)/shard_map/pallas_call | solution.py:250
  46.0 1.6 %collective-permute-start.15 = (bf16[192,512]{1,0:T(8,128)(2,1)S(1)}, bf16[192,512]{1,0:T(8,128)(2,1)S(1)}, u32[]{:S(2)}, u32[]{:S(2)}) collective-permute-start(bf16[192,512]{1,0:T(8,128)(2,1)S(1)} %pad_maximum_fusion.3), channel_id=1, source_target_pairs={{0,2},{1,3},{2,0},{3,1},{4,6},{5,7},{6,4},{7,5},{8,10},{9,11},{10,... | collective-permute-start | bytes 589832 | tf_op jit(solution)/shard_map/ppermute | solution.py:294
  47.5 2.7 %collective-permute-done.16 = bf16[64,512]{1,0:T(8,128)(2,1)S(1)} collective-permute-done((bf16[64,512]{1,0:T(8,128)(2,1)S(1)}, bf16[64,512]{1,0:T(8,128)(2,1)S(1)}, u32[]{:S(2)}, u32[]{:S(2)}) %collective-permute-start.16) | collective-permute-done | bytes 65568 | tf_op jit(solution)/shard_map/ppermute | solution.py:294
  50.3 1.6 %collective-permute-start.17 = (bf16[64,512]{1,0:T(8,128)(2,1)S(1)}, bf16[64,512]{1,0:T(8,128)(2,1)S(1)}, u32[]{:S(2)}, u32[]{:S(2)}) collective-permute-start(bf16[64,512]{1,0:T(8,128)(2,1)S(1)} %collective-permute-done.16), channel_id=1, source_target_pairs={{0,2},{1,3},{2,0},{3,1},{4,6},{5,7},{6,4},{7,5},{8,10},{9,11},{10,... | collective-permute-start | bytes 196616 | tf_op jit(solution)/shard_map/ppermute | solution.py:294
  51.9 2.3 %shard_map.194 = (f32[640,512]{1,0:T(8,128)S(1)}, bf16[640,512]{1,0:T(8,128)(2,1)S(1)}, bf16[256,320]{1,0:T(8,128)(2,1)S(1)}, bf16[256,320]{1,0:T(8,128)(2,1)S(1)}) custom-call(bf16[176,512]{1,0:T(8,128)(2,1)S(1)} %get-tuple-element.177.refs_0_, bf16[176,512]{1,0:T(8,128)(2,1)S(1)} %get-tuple-element.178.refs_1_, ...), custom_call_target="tpu_custom_call" | custom-call | flops 1509949440 | bytes 5111808 | tf_op jit(solution)/shard_map/pallas_call | solution.py:250
  59.5 1.6 %collective-permute-start.25 = (bf16[320,512]{1,0:T(8,128)(2,1)S(1)}, bf16[320,512]{1,0:T(8,128)(2,1)S(1)}, u32[]{:S(2)}, u32[]{:S(2)}) collective-permute-start(bf16[320,512]{1,0:T(8,128)(2,1)S(1)} %pad_maximum_fusion), channel_id=1, source_target_pairs={{0,2},{1,3},{2,0},{3,1},{4,6},{5,7},{6,4},{7,5},{8,10},{9,11},{10,... | collective-permute-start | bytes 983048 | tf_op jit(solution)/shard_map/ppermute | solution.py:294
  61.1 2.4 %collective-permute-start.21 = (bf16[64,512]{1,0:T(8,128)(2,1)S(1)}, bf16[64,512]{1,0:T(8,128)(2,1)S(1)}, u32[]{:S(2)}, u32[]{:S(2)}) collective-permute-start(bf16[64,512]{1,0:T(8,128)(2,1)S(1)} %get-tuple-element.208), channel_id=1, source_target_pairs={{0,8},{1,9},{2,10},{3,11},{4,12},{5,13},{6,14},{7,15},{8,0},{9,1},... | collective-permute-start | bytes 196616 | tf_op jit(solution)/shard_map/ppermute | solution.py:294
  63.5 1.5 %collective-permute-start.22 = (bf16[64,512]{1,0:T(8,128)(2,1)S(1)}, bf16[64,512]{1,0:T(8,128)(2,1)S(1)}, u32[]{:S(2)}, u32[]{:S(2)}) collective-permute-start(bf16[64,512]{1,0:T(8,128)(2,1)S(1)} %get-tuple-element.209), channel_id=1, source_target_pairs={{0,12},{1,13},{2,14},{3,15},{4,8},{5,9},{6,10},{7,11},{8,4},{9,5},... | collective-permute-start | bytes 196616 | tf_op jit(solution)/shard_map/ppermute | solution.py:294
  65.1 2.5 %shard_map.197 = (bf16[768,512]{1,0:T(8,128)(2,1)}, f32[256,512]{1,0:T(8,128)S(1)}) custom-call(bf16[64,512]{1,0:T(8,128)(2,1)S(1)} %shard_map.191.refs_0_.nodes_ref, bf16[192,512]{1,0:T(8,128)(2,1)S(1)} %shard_map.192.refs_1_.nodes_ref, bf16[768,512]{1,0:T(8,128)(2,1)S(1)} %get-tuple-element.168.refs_2_, s32[768]{0:T(1024)S(1)} %get-tuple-element.115.refs_3_, ...), custom_call_target="tpu_custom_call" | custom-call | flops 738197504 | bytes 5523456 | tf_op jit(solution)/shard_map/pallas_call | solution.py:250
  70.7 1.6 %shard_map.199 = (bf16[256,512]{1,0:T(8,128)(2,1)}, bf16[256,512]{1,0:T(8,128)(2,1)}) custom-call(bf16[64,512]{1,0:T(8,128)(2,1)S(1)} %shard_map.191.refs_0_.nodes_ref, f32[256,512]{1,0:T(8,128)S(1)} %get-tuple-element.206.sum_ref, f32[64,512]{1,0:T(8,128)S(1)} %get-tuple-element.207.refs_0_, bf16[64,512]{1,0:T(8,128)(2,1)S(1)} %collective-permute-done.21.refs_1_, ...), custom_call_target="tpu_custom_call" | custom-call | flops 100663296 | bytes 5779456 | tf_op jit(solution)/shard_map/pallas_call | solution.py:250
  (56 shorter events, 20.6 us)
Async XLA Ops:
  2.2 12.1 %collective-permute-start.2 = (bf16[176,512]{1,0:T(8,128)(2,1)S(1)}, bf16[176,512]{1,0:T(8,128)(2,1)S(1)}, u32[]{:S(2)}, u32[]{:S(2)}) collective-permute-start(bf16[176,512]{1,0:T(8,128)(2,1)S(1)} %get-tuple-element.125), channel_id=1, source_target_pairs={{0,1},{1,0},{2,3},{3,2},{4,5},{5,4},{6,7},{7,6},{8,9},{9,8},{10,11... | collective-permute-start | bytes 540680 | tf_op jit(solution)/shard_map/ppermute | solution.py:294
  2.7 11.6 %collective-permute-start.3 = (bf16[176,512]{1,0:T(8,128)(2,1)S(1)}, bf16[176,512]{1,0:T(8,128)(2,1)S(1)}, u32[]{:S(2)}, u32[]{:S(2)}) collective-permute-start(bf16[176,512]{1,0:T(8,128)(2,1)S(1)} %get-tuple-element.126), channel_id=1, source_target_pairs={{0,2},{1,3},{2,0},{3,1},{4,6},{5,7},{6,4},{7,5},{8,10},{9,11},{10,... | collective-permute-start | bytes 540680 | tf_op jit(solution)/shard_map/ppermute | solution.py:294
  5.3 9.0 %collective-permute-start.4 = (bf16[176,512]{1,0:T(8,128)(2,1)S(1)}, bf16[176,512]{1,0:T(8,128)(2,1)S(1)}, u32[]{:S(2)}, u32[]{:S(2)}) collective-permute-start(bf16[176,512]{1,0:T(8,128)(2,1)S(1)} %get-tuple-element.127), channel_id=1, source_target_pairs={{0,3},{1,2},{2,1},{3,0},{4,7},{5,6},{6,5},{7,4},{8,11},{9,10},{10,... | collective-permute-start | bytes 540680 | tf_op jit(solution)/shard_map/ppermute | solution.py:294
  5.4 8.9 %collective-permute-start.1 = (bf16[64,512]{1,0:T(8,128)(2,1)S(1)}, bf16[64,512]{1,0:T(8,128)(2,1)S(1)}, u32[]{:S(2)}, u32[]{:S(2)}) collective-permute-start(bf16[64,512]{1,0:T(8,128)(2,1)S(1)} %get-tuple-element.112.refs_0_.nodes_ref), channel_id=1, source_target_pairs={{0,4},{1,5},{2,6},{3,7},{4,0},{5,1},{6,2},{7,3},{8,12},{9,13},{10,... | collective-permute-start | bytes 196616 | tf_op jit(solution)/shard_map/ppermute | solution.py:294
  7.2 7.1 %collective-permute-start = (bf16[64,512]{1,0:T(8,128)(2,1)S(1)}, bf16[64,512]{1,0:T(8,128)(2,1)S(1)}, u32[]{:S(2)}, u32[]{:S(2)}) collective-permute-start(bf16[64,512]{1,0:T(8,128)(2,1)S(1)} %get-tuple-element.112.refs_0_.nodes_ref), channel_id=1, source_target_pairs={{0,12},{1,13},{2,14},{3,15},{4,8},{5,9},{6,10},{7,11},{8,4},{9,5},... | collective-permute-start | bytes 196616 | tf_op jit(solution)/shard_map/ppermute | solution.py:294
  14.3 4.3 %collective-permute-start.5 = (bf16[64,512]{1,0:T(8,128)(2,1)S(1)}, bf16[64,512]{1,0:T(8,128)(2,1)S(1)}, u32[]{:S(2)}, u32[]{:S(2)}) collective-permute-start(bf16[64,512]{1,0:T(8,128)(2,1)S(1)} %collective-permute-done), channel_id=1, source_target_pairs={{0,4},{1,5},{2,6},{3,7},{4,0},{5,1},{6,2},{7,3},{8,12},{9,13},{10,... | collective-permute-start | bytes 196616 | tf_op jit(solution)/shard_map/ppermute | solution.py:294
  15.7 7.6 %collective-permute-start.8 = (bf16[192,512]{1,0:T(8,128)(2,1)S(1)}, bf16[192,512]{1,0:T(8,128)(2,1)S(1)}, u32[]{:S(2)}, u32[]{:S(2)}) collective-permute-start(bf16[192,512]{1,0:T(8,128)(2,1)S(1)} %pad_maximum_fusion.2), channel_id=1, source_target_pairs={{0,2},{1,3},{2,0},{3,1},{4,6},{5,7},{6,4},{7,5},{8,10},{9,11},{10,... | collective-permute-start | bytes 589832 | tf_op jit(solution)/shard_map/ppermute | solution.py:294
  18.7 4.7 %collective-permute-start.7 = (bf16[256,512]{1,0:T(8,128)(2,1)S(1)}, bf16[256,512]{1,0:T(8,128)(2,1)S(1)}, u32[]{:S(2)}, u32[]{:S(2)}) collective-permute-start(bf16[256,512]{1,0:T(8,128)(2,1)S(1)} %constant_dynamic-update-slice_fusion.refs_4_), channel_id=1, source_target_pairs={{0,1},{1,0},{2,3},{3,2},{4,5},{5,4},{6,7},{7,6},{8,9},{9,8},{10,11... | collective-permute-start | bytes 786440 | tf_op jit(solution)/shard_map/ppermute | solution.py:294
  18.7 6.8 %collective-permute-start.6 = (bf16[64,512]{1,0:T(8,128)(2,1)S(1)}, bf16[64,512]{1,0:T(8,128)(2,1)S(1)}, u32[]{:S(2)}, u32[]{:S(2)}) collective-permute-start(bf16[64,512]{1,0:T(8,128)(2,1)S(1)} %collective-permute-done.5), channel_id=1, source_target_pairs={{0,2},{1,3},{2,0},{3,1},{4,6},{5,7},{6,4},{7,5},{8,10},{9,11},{10,... | collective-permute-start | bytes 196616 | tf_op jit(solution)/shard_map/ppermute | solution.py:294
  29.5 6.9 %collective-permute-start.10 = (bf16[64,512]{1,0:T(8,128)(2,1)S(1)}, bf16[64,512]{1,0:T(8,128)(2,1)S(1)}, u32[]{:S(2)}, u32[]{:S(2)}) collective-permute-start(bf16[64,512]{1,0:T(8,128)(2,1)S(1)} %get-tuple-element.153), channel_id=1, source_target_pairs={{0,8},{1,9},{2,10},{3,11},{4,12},{5,13},{6,14},{7,15},{8,0},{9,1},... | collective-permute-start | bytes 196616 | tf_op jit(solution)/shard_map/ppermute | solution.py:294
  32.2 6.4 %collective-permute-start.11 = (bf16[64,512]{1,0:T(8,128)(2,1)S(1)}, bf16[64,512]{1,0:T(8,128)(2,1)S(1)}, u32[]{:S(2)}, u32[]{:S(2)}) collective-permute-start(bf16[64,512]{1,0:T(8,128)(2,1)S(1)} %get-tuple-element.154), channel_id=1, source_target_pairs={{0,12},{1,13},{2,14},{3,15},{4,8},{5,9},{6,10},{7,11},{8,4},{9,5},... | collective-permute-start | bytes 196616 | tf_op jit(solution)/shard_map/ppermute | solution.py:294
  32.2 6.4 %collective-permute-start.12 = (bf16[64,512]{1,0:T(8,128)(2,1)S(1)}, bf16[64,512]{1,0:T(8,128)(2,1)S(1)}, u32[]{:S(2)}, u32[]{:S(2)}) collective-permute-start(bf16[64,512]{1,0:T(8,128)(2,1)S(1)} %get-tuple-element.155), channel_id=1, source_target_pairs={{0,4},{1,5},{2,6},{3,7},{4,0},{5,1},{6,2},{7,3},{8,12},{9,13},{10,... | collective-permute-start | bytes 196616 | tf_op jit(solution)/shard_map/ppermute | solution.py:294
  39.2 5.7 %collective-permute-start.14 = (bf16[64,512]{1,0:T(8,128)(2,1)S(1)}, bf16[64,512]{1,0:T(8,128)(2,1)S(1)}, u32[]{:S(2)}, u32[]{:S(2)}) collective-permute-start(bf16[64,512]{1,0:T(8,128)(2,1)S(1)} %shard_map.191.refs_0_.nodes_ref), channel_id=1, source_target_pairs={{0,4},{1,5},{2,6},{3,7},{4,0},{5,1},{6,2},{7,3},{8,12},{9,13},{10,... | collective-permute-start | bytes 196616 | tf_op jit(solution)/shard_map/ppermute | solution.py:294
  39.9 6.1 %collective-permute-start.13 = (bf16[64,512]{1,0:T(8,128)(2,1)S(1)}, bf16[64,512]{1,0:T(8,128)(2,1)S(1)}, u32[]{:S(2)}, u32[]{:S(2)}) collective-permute-start(bf16[64,512]{1,0:T(8,128)(2,1)S(1)} %shard_map.191.refs_0_.nodes_ref), channel_id=1, source_target_pairs={{0,12},{1,13},{2,14},{3,15},{4,8},{5,9},{6,10},{7,11},{8,4},{9,5},... | collective-permute-start | bytes 196616 | tf_op jit(solution)/shard_map/ppermute | solution.py:294
  46.0 4.3 %collective-permute-start.16 = (bf16[64,512]{1,0:T(8,128)(2,1)S(1)}, bf16[64,512]{1,0:T(8,128)(2,1)S(1)}, u32[]{:S(2)}, u32[]{:S(2)}) collective-permute-start(bf16[64,512]{1,0:T(8,128)(2,1)S(1)} %collective-permute-done.13), channel_id=1, source_target_pairs={{0,4},{1,5},{2,6},{3,7},{4,0},{5,1},{6,2},{7,3},{8,12},{9,13},{10,... | collective-permute-start | bytes 196616 | tf_op jit(solution)/shard_map/ppermute | solution.py:294
  46.0 5.9 %collective-permute-start.15 = (bf16[192,512]{1,0:T(8,128)(2,1)S(1)}, bf16[192,512]{1,0:T(8,128)(2,1)S(1)}, u32[]{:S(2)}, u32[]{:S(2)}) collective-permute-start(bf16[192,512]{1,0:T(8,128)(2,1)S(1)} %pad_maximum_fusion.3), channel_id=1, source_target_pairs={{0,2},{1,3},{2,0},{3,1},{4,6},{5,7},{6,4},{7,5},{8,10},{9,11},{10,... | collective-permute-start | bytes 589832 | tf_op jit(solution)/shard_map/ppermute | solution.py:294
  50.3 1.7 %collective-permute-start.18 = (bf16[256,512]{1,0:T(8,128)(2,1)S(1)}, bf16[256,512]{1,0:T(8,128)(2,1)S(1)}, u32[]{:S(2)}, u32[]{:S(2)}) collective-permute-start(bf16[256,512]{1,0:T(8,128)(2,1)S(1)} %pad_maximum_fusion.1.refs_4_), channel_id=1, source_target_pairs={{0,1},{1,0},{2,3},{3,2},{4,5},{5,4},{6,7},{7,6},{8,9},{9,8},{10,11... | collective-permute-start | bytes 786440 | tf_op jit(solution)/shard_map/ppermute | solution.py:294
  50.3 4.5 %collective-permute-start.17 = (bf16[64,512]{1,0:T(8,128)(2,1)S(1)}, bf16[64,512]{1,0:T(8,128)(2,1)S(1)}, u32[]{:S(2)}, u32[]{:S(2)}) collective-permute-start(bf16[64,512]{1,0:T(8,128)(2,1)S(1)} %collective-permute-done.16), channel_id=1, source_target_pairs={{0,2},{1,3},{2,0},{3,1},{4,6},{5,7},{6,4},{7,5},{8,10},{9,11},{10,... | collective-permute-start | bytes 196616 | tf_op jit(solution)/shard_map/ppermute | solution.py:294
  57.8 1.6 %collective-permute-start.20 = (bf16[160,512]{1,0:T(8,128)(2,1)S(1)}, bf16[160,512]{1,0:T(8,128)(2,1)S(1)}, u32[]{:S(2)}, u32[]{:S(2)}) collective-permute-start(bf16[160,512]{1,0:T(8,128)(2,1)S(1)} %get-tuple-element.190), channel_id=1, source_target_pairs={{0,1},{1,0},{2,3},{3,2},{4,5},{5,4},{6,7},{7,6},{8,9},{9,8},{10,11... | collective-permute-start | bytes 491528 | tf_op jit(solution)/shard_map/ppermute | solution.py:294
  59.5 11.2 %collective-permute-start.25 = (bf16[320,512]{1,0:T(8,128)(2,1)S(1)}, bf16[320,512]{1,0:T(8,128)(2,1)S(1)}, u32[]{:S(2)}, u32[]{:S(2)}) collective-permute-start(bf16[320,512]{1,0:T(8,128)(2,1)S(1)} %pad_maximum_fusion), channel_id=1, source_target_pairs={{0,2},{1,3},{2,0},{3,1},{4,6},{5,7},{6,4},{7,5},{8,10},{9,11},{10,... | collective-permute-start | bytes 983048 | tf_op jit(solution)/shard_map/ppermute | solution.py:294
  61.1 9.6 %collective-permute-start.24 = (bf16[160,512]{1,0:T(8,128)(2,1)S(1)}, bf16[160,512]{1,0:T(8,128)(2,1)S(1)}, u32[]{:S(2)}, u32[]{:S(2)}) collective-permute-start(bf16[160,512]{1,0:T(8,128)(2,1)S(1)} %get-tuple-element.215), channel_id=1, source_target_pairs={{0,1},{1,0},{2,3},{3,2},{4,5},{5,4},{6,7},{7,6},{8,9},{9,8},{10,11... | collective-permute-start | bytes 491528 | tf_op jit(solution)/shard_map/ppermute | solution.py:294
  61.1 7.9 %collective-permute-start.21 = (bf16[64,512]{1,0:T(8,128)(2,1)S(1)}, bf16[64,512]{1,0:T(8,128)(2,1)S(1)}, u32[]{:S(2)}, u32[]{:S(2)}) collective-permute-start(bf16[64,512]{1,0:T(8,128)(2,1)S(1)} %get-tuple-element.208), channel_id=1, source_target_pairs={{0,8},{1,9},{2,10},{3,11},{4,12},{5,13},{6,14},{7,15},{8,0},{9,1},... | collective-permute-start | bytes 196616 | tf_op jit(solution)/shard_map/ppermute | solution.py:294
  63.5 6.7 %collective-permute-start.22 = (bf16[64,512]{1,0:T(8,128)(2,1)S(1)}, bf16[64,512]{1,0:T(8,128)(2,1)S(1)}, u32[]{:S(2)}, u32[]{:S(2)}) collective-permute-start(bf16[64,512]{1,0:T(8,128)(2,1)S(1)} %get-tuple-element.209), channel_id=1, source_target_pairs={{0,12},{1,13},{2,14},{3,15},{4,8},{5,9},{6,10},{7,11},{8,4},{9,5},... | collective-permute-start | bytes 196616 | tf_op jit(solution)/shard_map/ppermute | solution.py:294
  65.1 5.6 %collective-permute-start.23 = (bf16[64,512]{1,0:T(8,128)(2,1)S(1)}, bf16[64,512]{1,0:T(8,128)(2,1)S(1)}, u32[]{:S(2)}, u32[]{:S(2)}) collective-permute-start(bf16[64,512]{1,0:T(8,128)(2,1)S(1)} %get-tuple-element.210), channel_id=1, source_target_pairs={{0,4},{1,5},{2,6},{3,7},{4,0},{5,1},{6,2},{7,3},{8,12},{9,13},{10,... | collective-permute-start | bytes 196616 | tf_op jit(solution)/shard_map/ppermute | solution.py:294
  (2 other events, 3.1 us)

commit v5 on v4

--- a/solution.py
+++ b/solution.py
@@ -149,52 +149,48 @@
 def far_first_kernel(lines, slot, *refs):
     slots, tables, win_ref = refs[0:PLANE], refs[PLANE : PLANE + 2], refs[PLANE + 2]
     out_ref, late_ref, *scatter_refs = refs[PLANE + 3 :]
-    span = lines * COARSE
-    for pair in range(0, PLANE, 2):
-        columns_s, columns_r, rows_r = [], [], []
-        for ref in slots[pair : pair + 2]:
-            meta = ref[slot : slot + 16, :].astype(F32)[0:8, 0 : -(-slot // 128) * 128]
-            tall = jnp.transpose(meta)[0:slot, :]
-            columns_s.append((tall[:, 0:1] * COARSE + tall[:, 1:2]).astype(I32))
-            columns_r.append((tall[:, 2:3] * COARSE + tall[:, 3:4]).astype(I32) - COARSE)
-            rows_r.append((meta[2:3, 0:slot] * COARSE + meta[3:4, 0:slot]).astype(I32) - COARSE)
-        column_s, column_r = jnp.concatenate(columns_s, axis=0), jnp.concatenate(columns_r, axis=0)
-        senders = None
-        for q, table in enumerate(tables):
-            piece = mm(match_rows(column_s, table.shape[0], q * span), table[...])
-            senders = piece if senders is None else senders + piece
-        receivers = mm(match_rows(column_r, span), tables[0][...])
-        edges = jnp.concatenate([ref[0:slot, :] for ref in slots[pair : pair + 2]], axis=0)
-        stacked = jnp.concatenate([edges, senders.astype(BF), receivers.astype(BF)], axis=1)
-        rows = slice(pair * slot, (pair + 2) * slot)
-        out_ref[rows, :] = mm(stacked, win_ref[...])
-        late_ref[rows, :] = match_rows(column_s, 2 * span, 2 * span)
-        scatter_refs[pair // 2][...] = match_columns(jnp.concatenate(rows_r, axis=1), span)
-
-
-def far_second_kernel(layer, lines, slot, pairs, chained, keep, *refs):
-    count = 2 * len(pairs)
-    slots, refs = refs[0:count], refs[count:]
-    straight_ref, across_ref, pre_ref, late_ref, *scatter_refs = refs[0:6]
-    total, refs = (refs[6][...], refs[7:]) if chained else (None, refs[6:])
+    span, size = lines * COARSE, PLANE // len(scatter_refs)
+    columns_s, columns_r, rows_r = [], [], []
+    for ref in slots:
+        meta = ref[slot : slot + 16, :].astype(F32)[0:8, 0 : -(-slot // 128) * 128]
+        tall = jnp.transpose(meta)[0:slot, :]
+        columns_s.append((tall[:, 0:1] * COARSE + tall[:, 1:2]).astype(I32))
+        columns_r.append((tall[:, 2:3] * COARSE + tall[:, 3:4]).astype(I32) - COARSE)
+        rows_r.append((meta[2:3, 0:slot] * COARSE + meta[3:4, 0:slot]).astype(I32) - COARSE)
+    column_s, column_r = jnp.concatenate(columns_s, axis=0), jnp.concatenate(columns_r, axis=0)
+    senders = None
+    for q, table in enumerate(tables):
+        piece = mm(match_rows(column_s, span, q * span), table[...])
+        senders = piece if senders is None else senders + piece
+    receivers = mm(match_rows(column_r, span), tables[0][...])
+    edges = jnp.concatenate([ref[0:slot, :] for ref in slots], axis=0)
+    stacked = jnp.concatenate([edges, senders.astype(BF), receivers.astype(BF)], axis=1)
+    out_ref[...] = mm(stacked, win_ref[...])
+    late_ref[...] = match_rows(column_s, 2 * span, 2 * span)
+    for i, ref in enumerate(scatter_refs):
+        ref[...] = match_columns(jnp.concatenate(rows_r[i * size : (i + 1) * size], axis=1), span)
+
+
+def far_second_kernel(layer, lines, slot, start, chained, keep, *refs):
+    straight_ref, across_ref, pre_ref, late_ref, scatter_ref, *refs = refs
+    total, refs = (refs[0][...], refs[1:]) if chained else (None, refs)
     win_ref, wout_ref = refs[0:2]
     vecs, refs = [v[layer : layer + 1, :] for v in refs[2:5]], refs[5:]
-    new_refs, sum_refs = refs[0:count], refs[count:]
-    width = pre_ref.shape[1]
+    count = scatter_ref.shape[1] // slot
+    slots, new_refs, sum_refs = refs[0:count], refs[count : 2 * count], refs[2 * count :]
+    rows, width = slice(start * slot, (start + count) * slot), pre_ref.shape[1]
     table = jnp.concatenate([straight_ref[...], across_ref[...]], axis=0)
-    for i, pair in enumerate(pairs):
-        rows, own = slice(pair * slot, (pair + 2) * slot), slots[2 * i : 2 * i + 2]
-        senders = mm(late_ref[rows, :], table).astype(BF)
-        pre_act = pre_ref[rows, :] + mm(senders, win_ref[width : 2 * width, :])
-        normed = edge_tail(pre_act, wout_ref[...], *vecs)
-        edges = jnp.concatenate([ref[0:slot, :] for ref in own], axis=0)
-        new = (edges.astype(F32) + normed).astype(BF)
-        for j in range(2):
-            new_refs[2 * i + j][0:slot, :] = new[j * slot : (j + 1) * slot, :]
-            if keep:
-                new_refs[2 * i + j][slot:, :] = own[j][slot:, :]
-        part = mm(scatter_refs[pair // 2][...], normed.astype(BF))
-        total = part if total is None else total + part
+    senders = mm(late_ref[rows, :], table).astype(BF)
+    pre_act = pre_ref[rows, :] + mm(senders, win_ref[width : 2 * width, :])
+    normed = edge_tail(pre_act, wout_ref[...], *vecs)
+    edges = jnp.concatenate([ref[0:slot, :] for ref in slots], axis=0)
+    new = (edges.astype(F32) + normed).astype(BF)
+    for j in range(count):
+        new_refs[j][0:slot, :] = new[j * slot : (j + 1) * slot, :]
+        if keep:
+            new_refs[j][slot:, :] = slots[j][slot:, :]
+    part = mm(scatter_ref[...], normed.astype(BF))
+    total = part if total is None else total + part
     if len(sum_refs) == 1:
         sum_refs[0][...] = total
         return
@@ -216,28 +212,40 @@
     if len(refs) == 4:
         refs[3][...] = new
         return
-    pos_ref, out_ref, back_ref = refs[3:]
+    pos_ref, *slot_refs, out_ref, half_ref, back_ref = refs[3:]
     out_ref[...] = new
-    back_ref[...] = match_rows(as_column(pos_ref[...]), back_ref.shape[1])
+    column, count = as_column(pos_ref[...]), back_ref.shape[1]
+    slots = jnp.concatenate([ref[...] for ref in slot_refs], axis=0)
+    half_ref[...] = mm(match_rows(column, count), slots).astype(BF)
+    back_ref[...] = match_rows(column, count, count)
 
 
 def coarse_kernel(layer, lines, nodes_ref, sum_ref, *refs):
     part_refs, refs = refs[0:lines], refs[lines:]
     (win_ref, wout_ref), vec_refs, refs = refs[0:2], refs[2:5], refs[5:]
+    copies = []
     if len(refs) > 1:
-        rest_ref, back_ref, *slot_refs, out_ref, far_ref = refs
+        rest_ref, half_ref, back_ref, *slot_refs, out_hbm, far_hbm, out_ref, far_ref, sems = refs
+        copies.append(pltpu.make_async_copy(rest_ref, out_hbm.at[COARSE:, :], sems.at[0]))
+        copies[0].start()
         slots = jnp.concatenate([ref[...] for ref in slot_refs], axis=0)
-        far_ref[...] = mm(back_ref[...], slots).astype(BF)
-        out_ref[COARSE:, :] = rest_ref[...]
+        far_ref[...] = (half_ref[...].astype(F32) + mm(back_ref[...], slots)).astype(BF)
+        copies.append(pltpu.make_async_copy(far_ref, far_hbm, sems.at[1]))
+        copies[1].start()
     else:
         out_ref = refs[0]
     sums = sum_ref[0:COARSE, :] + part_refs[0][...]
     for ref in part_refs[1:]:
         sums = sums + ref[...].astype(F32)
-    out_ref[0:COARSE, :] = node_update(layer, nodes_ref[...], sums, win_ref, wout_ref, vec_refs)
-
-
-def call(kernel, outs, args, flops, limit, first=None, scratch=()):
+    out_ref[...] = node_update(layer, nodes_ref[...], sums, win_ref, wout_ref, vec_refs)
+    if copies:
+        copies.append(pltpu.make_async_copy(out_ref, out_hbm.at[0:COARSE, :], sems.at[2]))
+        copies[2].start()
+        for copy in copies:
+            copy.wait()
+
+
+def call(kernel, outs, args, flops, limit, first=None, scratch=(), placed=pltpu.VMEM):
     bytes_accessed = sum(a.size * a.dtype.itemsize for a in [*args, *outs]) if flops or first == 0 else 0
     whole = pl.BlockSpec(memory_space=pltpu.VMEM)
     specs = [whole] * len(args)
@@ -251,7 +259,7 @@
         kernel,
         out_shape=outs,
         in_specs=specs,
-        out_specs=[whole] * len(outs),
+        out_specs=[pl.BlockSpec(memory_space=placed)] * len(outs),
         scratch_shapes=scratch,
         compiler_params=pltpu.CompilerParams(vmem_limit_bytes=limit),
         cost_estimate=pl.CostEstimate(flops=flops, bytes_accessed=bytes_accessed, transcendentals=0),
@@ -370,7 +378,7 @@
         found = call(
             functools.partial(far_first_kernel, lines, slot),
             [shape((far_rows, width), F32), shape((far_rows, 2 * span), BF)]
-            + [shape((span, 2 * slot), BF)] * 2,
+            + [shape((span, far_rows), BF)],
             [*slots, *tables, weights[l][0]],
             2 * far_rows * width * (3 * span + 3 * width),
             limit,
@@ -381,28 +389,23 @@
         moved = shape((slot if last else padded, width), BF)
         parts_shape = [shape((COARSE, width), F32)] + [shape((COARSE, width), BF)] * (lines - 1)
 
-        def far_part(pairs, before, outs):
+        def far_part(start, size, before, outs):
             return call(
-                functools.partial(far_second_kernel, l, lines, slot, pairs, len(before) > 0, not last),
-                [moved] * (2 * len(pairs)) + outs,
-                [*[v for i in pairs for v in slots[i : i + 2]], *late, *found, *before]
-                + [*weights[l], *edge_vecs],
-                4 * len(pairs) * slot * width * (3 * span + 2 * width),
+                functools.partial(far_second_kernel, l, lines, slot, start, len(before) > 0, not last),
+                [moved] * size + outs,
+                [*late, *found[0:2], found[2 + start // size], *before]
+                + [*weights[l], *edge_vecs, *slots[start : start + size]],
+                2 * size * slot * width * (3 * span + 2 * width),
                 limit,
             )
 
+        far = far_part(0, PLANE, [], parts_shape)
+        slots, parts = [*far[:PLANE]], far[PLANE:]
         if last:
-            ahead = far_part((2,), [], [shape((span, width), F32)])
-            passed = swap(ahead[1], 1)
-            passed, far = tied((passed, far_part((0,), [ahead[2]], parts_shape)))
-            crossing = jnp.concatenate([ahead[0], passed], axis=0)
-            slots, parts = [far[0], swap(far[1], 1), swap(crossing, 2)], far[2:]
+            slots = [slots[0]] + [swap(slots[m], m) for m in range(1, PLANE)]
             parts, done = tied((parts, done))
             for rows in pieces[1:]:
                 done = local_part(rows, done)
-        else:
-            far = far_part((0, 2), [], parts_shape)
-            slots, parts = [*far[:PLANE]], far[PLANE:]
         local, sums = done
         far_parts = [swap(parts[i], PLANE * place[i]) for i in range(lines - 1, 0, -1)]
         parts = [parts[0], *far_parts]
@@ -419,14 +422,16 @@
         rest = call(
             functools.partial(rest_kernel, l),
             [shape((node_count - COARSE, width), BF)]
-            + [shape((far_count, far_rows), BF)] * last,
-            [rest, sums, *ends] + [pos] * last,
+            + [shape((far_count, width), BF), shape((far_count, 2 * slot), BF)] * last,
+            [rest, sums, *ends] + [pos, *slots[0:2]] * last,
             6 * (node_count - COARSE) * width * width,
             limit,
         )
         if last:
             return_shapes = [shape((node_count, width), BF), shape((far_count, width), BF)]
-            extra = [*rest, *slots]
+            extra = [*rest, *slots[2:]]
+            scratch = [pltpu.VMEM((COARSE, width), BF), pltpu.VMEM((far_count, width), BF)]
+            scratch += [pltpu.SemaphoreType.DMA((3,))]
         else:
             return_shapes, extra, rest = [shape((COARSE, width), BF)], [], rest[0]
         coarse, *far_out = call(
@@ -435,6 +440,8 @@
             [coarse, sums, *parts, *ends, *extra],
             6 * COARSE * width * width,
             limit,
+            scratch=scratch if last else (),
+            placed=pltpu.HBM if last else pltpu.VMEM,
         )
     return (coarse, local, far_out[0])
 

time: 72.4 us -> 71.5 us (0.988)
  Pallas kernels: 29.2 us -> 28 us
    pallas_call x16 -> x15, Pallas kernels: 29.2 us -> 28 us  [call(): pl.pallas_call(kernel, out_shape=outs, in_specs=specs, out_specs=[pl.Bloc...]
  transfers between devices with their start and end apart: 26 -> 26, of which waited for: 11 -> 10; matrix products, arithmetic and copies ran while one was open for 0% -> 0% of each run, Pallas kernels for 30% -> 28%
where the time goes in v5:
time: 71.5 us; the launch traced here: 71.3 us
  Pallas kernels  28 us (39%)
  starting transfers between devices  27.6 us (39%)
  waiting for transfers between devices  14.4 us (20%)
  between operations  1.07 us (1%)
    pallas_call x15, Pallas kernels, call(): pl.pallas_call(kernel, out_shape=outs, in_specs=specs, out_specs=[pl.Bloc...  28 us
    ppermute x26, starting transfers between devices, swap(): lax.ppermute(values, 'patch', [(i, i ^ distance) for i in range(devices)])  27.6 us
    ppermute x26, waiting for transfers between devices, swap(): lax.ppermute(values, 'patch', [(i, i ^ distance) for i in range(devices)])  14.4 us
  transfers between devices with their start and end apart: 26, of which 10 were waited for; matrix products, arithmetic and copies ran while one was open for 0% of the time, Pallas kernels for 28%

profile of v5, /device:TPU:0, one launch (start us, length us, event | category | flops | bytes accessed | tf_op | source)
XLA Modules:
  0.0 71.3 jit_solution(16278752606695324034)
XLA Ops:
  0.6 1.6 %shard_map.184 = (s32[1,256]{1,0:T(1,128)S(1)}, bf16[64,512]{1,0:T(8,128)(2,1)S(1)}, bf16[192,512]{1,0:T(8,128)(2,1)S(1)}, bf16[176,512]{1,0:T(8,128)(2,1)S(1)},...) custom-call(s32[1]{0:T(128)} %bitcast.own_ref, s32[1,256]{1,0:T(1,128)} %bitcast.3, ...), custom_call_target="tpu_custom_call" | custom-call | flops 167772160 | bytes 1510404 | tf_op jit(solution)/shard_map/pallas_call | solution.py:258
  2.7 2.6 %collective-permute-start.3 = (bf16[176,512]{1,0:T(8,128)(2,1)S(1)}, bf16[176,512]{1,0:T(8,128)(2,1)S(1)}, u32[]{:S(2)}, u32[]{:S(2)}) collective-permute-start(bf16[176,512]{1,0:T(8,128)(2,1)S(1)} %get-tuple-element.115), channel_id=1, source_target_pairs={{0,2},{1,3},{2,0},{3,1},{4,6},{5,7},{6,4},{7,5},{8,10},{9,11},{10,... | collective-permute-start | bytes 540680 | tf_op jit(solution)/shard_map/ppermute | solution.py:302
  5.4 1.8 %collective-permute-start.1 = (bf16[64,512]{1,0:T(8,128)(2,1)S(1)}, bf16[64,512]{1,0:T(8,128)(2,1)S(1)}, u32[]{:S(2)}, u32[]{:S(2)}) collective-permute-start(bf16[64,512]{1,0:T(8,128)(2,1)S(1)} %get-tuple-element.101.refs_0_.nodes_ref), channel_id=1, source_target_pairs={{0,4},{1,5},{2,6},{3,7},{4,0},{5,1},{6,2},{7,3},{8,12},{9,13},{10,... | collective-permute-start | bytes 196616 | tf_op jit(solution)/shard_map/ppermute | solution.py:302
  7.2 2.5 %collective-permute-start = (bf16[64,512]{1,0:T(8,128)(2,1)S(1)}, bf16[64,512]{1,0:T(8,128)(2,1)S(1)}, u32[]{:S(2)}, u32[]{:S(2)}) collective-permute-start(bf16[64,512]{1,0:T(8,128)(2,1)S(1)} %get-tuple-element.101.refs_0_.nodes_ref), channel_id=1, source_target_pairs={{0,12},{1,13},{2,14},{3,15},{4,8},{5,9},{6,10},{7,11},{8,4},{9,5},... | collective-permute-start | bytes 196616 | tf_op jit(solution)/shard_map/ppermute | solution.py:302
  9.7 1.9 %shard_map.185 = (bf16[768,512]{1,0:T(8,128)(2,1)S(1)}, s32[768]{0:T(1024)S(1)}, s32[768]{0:T(1024)S(1)}, f32[2,512]{1,0:T(2,128)S(1)}, f32[2,512]{1,0:T(2,128)S...) custom-call(bf16[768,512]{1,0:T(8,128)(2,1)} %refs_0_.1, s32[768]{0:T(1024)} %refs_1_.1, ...), custom_call_target="tpu_custom_call" | custom-call | bytes 7901184 | tf_op jit(solution)/shard_map/pallas_call | solution.py:258
  11.6 2.7 %shard_map.186 = (bf16[512,512]{1,0:T(8,128)(2,1)S(1)}, f32[256,512]{1,0:T(8,128)S(1)}) custom-call(bf16[64,512]{1,0:T(8,128)(2,1)S(1)} %get-tuple-element.101.refs_0_.nodes_ref, bf16[192,512]{1,0:T(8,128)(2,1)S(1)} %get-tuple-element.102.refs_1_.nodes_ref, bf16[768,512]{1,0:T(8,128)(2,1)S(1)} %get-tuple-element.103.refs_2_, ...), custom_call_target="tpu_custom_call" | custom-call | tf_op jit(solution)/shard_map/pallas_call | solution.py:258
  15.7 1.6 %collective-permute-start.8 = (bf16[192,512]{1,0:T(8,128)(2,1)S(1)}, bf16[192,512]{1,0:T(8,128)(2,1)S(1)}, u32[]{:S(2)}, u32[]{:S(2)}) collective-permute-start(bf16[192,512]{1,0:T(8,128)(2,1)S(1)} %pad_maximum_fusion.1), channel_id=1, source_target_pairs={{0,2},{1,3},{2,0},{3,1},{4,6},{5,7},{6,4},{7,5},{8,10},{9,11},{10,... | collective-permute-start | bytes 589832 | tf_op jit(solution)/shard_map/ppermute | solution.py:302
  20.2 1.7 %shard_map.188 = (bf16[768,512]{1,0:T(8,128)(2,1)S(1)}, f32[256,512]{1,0:T(8,128)S(1)}) custom-call(bf16[64,512]{1,0:T(8,128)(2,1)S(1)} %get-tuple-element.101.refs_0_.nodes_ref, bf16[192,512]{1,0:T(8,128)(2,1)S(1)} %get-tuple-element.102.refs_1_.nodes_ref, bf16[768,512]{1,0:T(8,128)(2,1)S(1)} %get-tuple-element.103.refs_2_, ...), custom_call_target="tpu_custom_call" | custom-call | flops 738197504 | bytes 5523456 | tf_op jit(solution)/shard_map/pallas_call | solution.py:258
  23.3 2.2 %shard_map.187 = (f32[640,512]{1,0:T(8,128)S(1)}, bf16[640,512]{1,0:T(8,128)(2,1)S(1)}, bf16[256,640]{1,0:T(8,128)(2,1)S(1)}) custom-call(bf16[176,512]{1,0:T(8,128)(2,1)S(1)} %get-tuple-element.121.refs_0_.refs_10_, bf16[176,512]{1,0:T(8,128)(2,1)S(1)} %collective-permute-done.2.refs_1_.refs_11_, ...), custom_call_target="tpu_custom_call" | custom-call | flops 1509949440 | bytes 5111808 | tf_op jit(solution)/shard_map/pallas_call | solution.py:258
  27.2 2.0 %shard_map.189 = (bf16[176,512]{1,0:T(8,128)(2,1)S(1)}, bf16[176,512]{1,0:T(8,128)(2,1)S(1)}, bf16[176,512]{1,0:T(8,128)(2,1)S(1)}, bf16[176,512]{1,0:T(8,128)(2...) custom-call(bf16[256,512]{1,0:T(8,128)(2,1)S(1)} %constant_dynamic-u, ...), custom_call_target="tpu_custom_call" | custom-call | flops 1174405120 | bytes 6696960 | tf_op jit(solution)/shard_map/pallas_call | solution.py:258
  29.2 2.7 %collective-permute-start.10 = (bf16[64,512]{1,0:T(8,128)(2,1)S(1)}, bf16[64,512]{1,0:T(8,128)(2,1)S(1)}, u32[]{:S(2)}, u32[]{:S(2)}) collective-permute-start(bf16[64,512]{1,0:T(8,128)(2,1)S(1)} %get-tuple-element.140), channel_id=1, source_target_pairs={{0,8},{1,9},{2,10},{3,11},{4,12},{5,13},{6,14},{7,15},{8,0},{9,1},... | collective-permute-start | bytes 196616 | tf_op jit(solution)/shard_map/ppermute | solution.py:302
  32.8 2.6 %shard_map.190 = (bf16[2,1024,512]{2,1,0:T(8,128)(2,1)S(1)}, bf16[2,512,512]{2,1,0:T(8,128)(2,1)S(1)}, f32[2,512]{1,0:T(2,128)S(1)}, f32[2,512]{1,0:T(2,128)S(1)...) custom-call(bf16[2,1024,512]{2,1,0:T(8,128)(2,1)} %refs_0_.2, ...), custom_call_target="tpu_custom_call" | custom-call | bytes 12607488 | tf_op jit(solution)/shard_map/pallas_call | solution.py:258
  36.2 2.0 %collective-permute-done.11.refs_2_ = bf16[64,512]{1,0:T(8,128)(2,1)S(1)} collective-permute-done((bf16[64,512]{1,0:T(8,128)(2,1)S(1)}, bf16[64,512]{1,0:T(8,128)(2,1)S(1)}, u32[]{:S(2)}, u32[]{:S(2)}) %collective-permute-start.11) | collective-permute-done | bytes 65568 | tf_op jit(solution)/shard_map/ppermute | solution.py:302
  39.6 2.3 %collective-permute-start.13 = (bf16[64,512]{1,0:T(8,128)(2,1)S(1)}, bf16[64,512]{1,0:T(8,128)(2,1)S(1)}, u32[]{:S(2)}, u32[]{:S(2)}) collective-permute-start(bf16[64,512]{1,0:T(8,128)(2,1)S(1)} %shard_map.191.refs_0_.nodes_ref), channel_id=1, source_target_pairs={{0,12},{1,13},{2,14},{3,15},{4,8},{5,9},{6,10},{7,11},{8,4},{9,5},... | collective-permute-start | bytes 196616 | tf_op jit(solution)/shard_map/ppermute | solution.py:302
  41.9 2.7 %shard_map.193 = (bf16[512,512]{1,0:T(8,128)(2,1)S(1)}, f32[256,512]{1,0:T(8,128)S(1)}) custom-call(bf16[64,512]{1,0:T(8,128)(2,1)S(1)} %shard_map.191.refs_0_.nodes_ref, bf16[192,512]{1,0:T(8,128)(2,1)S(1)} %shard_map.192.refs_1_.nodes_ref, bf16[768,512]{1,0:T(8,128)(2,1)S(1)} %get-tuple-element.155.refs_2_, s32[768]{0:T(1024)S(1)} %get-tuple-element.104.refs_3_, ...), custom_call_target="tpu_custom_call" | custom-call | flops 1476395008 | bytes 4212736 | tf_op jit(solution)/shard_map/pallas_call | solution.py:258
  45.7 1.6 %collective-permute-start.15 = (bf16[192,512]{1,0:T(8,128)(2,1)S(1)}, bf16[192,512]{1,0:T(8,128)(2,1)S(1)}, u32[]{:S(2)}, u32[]{:S(2)}) collective-permute-start(bf16[192,512]{1,0:T(8,128)(2,1)S(1)} %pad_maximum_fusion.2), channel_id=1, source_target_pairs={{0,2},{1,3},{2,0},{3,1},{4,6},{5,7},{6,4},{7,5},{8,10},{9,11},{10,... | collective-permute-start | bytes 589832 | tf_op jit(solution)/shard_map/ppermute | solution.py:302
  47.2 2.7 %collective-permute-done.16 = bf16[64,512]{1,0:T(8,128)(2,1)S(1)} collective-permute-done((bf16[64,512]{1,0:T(8,128)(2,1)S(1)}, bf16[64,512]{1,0:T(8,128)(2,1)S(1)}, u32[]{:S(2)}, u32[]{:S(2)}) %collective-permute-start.16) | collective-permute-done | bytes 65568 | tf_op jit(solution)/shard_map/ppermute | solution.py:302
  50.0 1.6 %collective-permute-start.17 = (bf16[64,512]{1,0:T(8,128)(2,1)S(1)}, bf16[64,512]{1,0:T(8,128)(2,1)S(1)}, u32[]{:S(2)}, u32[]{:S(2)}) collective-permute-start(bf16[64,512]{1,0:T(8,128)(2,1)S(1)} %collective-permute-done.16), channel_id=1, source_target_pairs={{0,2},{1,3},{2,0},{3,1},{4,6},{5,7},{6,4},{7,5},{8,10},{9,11},{10,... | collective-permute-start | bytes 196616 | tf_op jit(solution)/shard_map/ppermute | solution.py:302
  51.6 2.4 %shard_map.194 = (f32[640,512]{1,0:T(8,128)S(1)}, bf16[640,512]{1,0:T(8,128)(2,1)S(1)}, bf16[256,640]{1,0:T(8,128)(2,1)S(1)}) custom-call(bf16[176,512]{1,0:T(8,128)(2,1)S(1)} %get-tuple-element.162.refs_0_.refs_10_, bf16[176,512]{1,0:T(8,128)(2,1)S(1)} %get-tuple-element.163.refs_1_.refs_11_, bf16[176,512]{1,0:T(8,128)(2,1)S(1)} %get-tuple-element.164.refs_2_.refs_12_, ...), custom_call_target="tpu_custom_call" | custom-call | flops 1509949440 | bytes 5111808 | tf_op jit(solution)/shard_map/pallas_call | solution.py:258
  56.1 2.0 %shard_map.195 = (bf16[160,512]{1,0:T(8,128)(2,1)S(1)}, bf16[160,512]{1,0:T(8,128)(2,1)S(1)}, bf16[160,512]{1,0:T(8,128)(2,1)S(1)}, bf16[160,512]{1,0:T(8,128)(2...) custom-call(bf16[256,512]{1,0:T(8,128)(2,1)S(1)} %constant_dynamic-u, ...), custom_call_target="tpu_custom_call" | custom-call | flops 1174405120 | bytes 6631424 | tf_op jit(solution)/shard_map/pallas_call | solution.py:258
  60.0 2.5 %collective-permute-start.20 = (bf16[64,512]{1,0:T(8,128)(2,1)S(1)}, bf16[64,512]{1,0:T(8,128)(2,1)S(1)}, u32[]{:S(2)}, u32[]{:S(2)}) collective-permute-start(bf16[64,512]{1,0:T(8,128)(2,1)S(1)} %get-tuple-element.185), channel_id=1, source_target_pairs={{0,8},{1,9},{2,10},{3,11},{4,12},{5,13},{6,14},{7,15},{8,0},{9,1},... | collective-permute-start | bytes 196616 | tf_op jit(solution)/shard_map/ppermute | solution.py:302
  62.5 1.5 %collective-permute-start.21 = (bf16[64,512]{1,0:T(8,128)(2,1)S(1)}, bf16[64,512]{1,0:T(8,128)(2,1)S(1)}, u32[]{:S(2)}, u32[]{:S(2)}) collective-permute-start(bf16[64,512]{1,0:T(8,128)(2,1)S(1)} %get-tuple-element.186), channel_id=1, source_target_pairs={{0,12},{1,13},{2,14},{3,15},{4,8},{5,9},{6,10},{7,11},{8,4},{9,5},... | collective-permute-start | bytes 196616 | tf_op jit(solution)/shard_map/ppermute | solution.py:302
  64.1 2.5 %shard_map.196 = (bf16[768,512]{1,0:T(8,128)(2,1)}, f32[256,512]{1,0:T(8,128)S(1)}) custom-call(bf16[64,512]{1,0:T(8,128)(2,1)S(1)} %shard_map.191.refs_0_.nodes_ref, bf16[192,512]{1,0:T(8,128)(2,1)S(1)} %shard_map.192.refs_1_.nodes_ref, bf16[768,512]{1,0:T(8,128)(2,1)S(1)} %get-tuple-element.155.refs_2_, s32[768]{0:T(1024)S(1)} %get-tuple-element.104.refs_3_, ...), custom_call_target="tpu_custom_call" | custom-call | flops 738197504 | bytes 5523456 | tf_op jit(solution)/shard_map/pallas_call | solution.py:258
  67.4 1.8 %collective-permute-done.21.refs_2_ = bf16[64,512]{1,0:T(8,128)(2,1)S(1)} collective-permute-done((bf16[64,512]{1,0:T(8,128)(2,1)S(1)}, bf16[64,512]{1,0:T(8,128)(2,1)S(1)}, u32[]{:S(2)}, u32[]{:S(2)}) %collective-permute-start.21) | collective-permute-done | bytes 65568 | tf_op jit(solution)/shard_map/ppermute | solution.py:302
  (54 shorter events, 19.0 us)
Async XLA Ops:
  2.2 12.1 %collective-permute-start.2 = (bf16[176,512]{1,0:T(8,128)(2,1)S(1)}, bf16[176,512]{1,0:T(8,128)(2,1)S(1)}, u32[]{:S(2)}, u32[]{:S(2)}) collective-permute-start(bf16[176,512]{1,0:T(8,128)(2,1)S(1)} %get-tuple-element.114), channel_id=1, source_target_pairs={{0,1},{1,0},{2,3},{3,2},{4,5},{5,4},{6,7},{7,6},{8,9},{9,8},{10,11... | collective-permute-start | bytes 540680 | tf_op jit(solution)/shard_map/ppermute | solution.py:302
  2.7 11.6 %collective-permute-start.3 = (bf16[176,512]{1,0:T(8,128)(2,1)S(1)}, bf16[176,512]{1,0:T(8,128)(2,1)S(1)}, u32[]{:S(2)}, u32[]{:S(2)}) collective-permute-start(bf16[176,512]{1,0:T(8,128)(2,1)S(1)} %get-tuple-element.115), channel_id=1, source_target_pairs={{0,2},{1,3},{2,0},{3,1},{4,6},{5,7},{6,4},{7,5},{8,10},{9,11},{10,... | collective-permute-start | bytes 540680 | tf_op jit(solution)/shard_map/ppermute | solution.py:302
  5.3 9.0 %collective-permute-start.4 = (bf16[176,512]{1,0:T(8,128)(2,1)S(1)}, bf16[176,512]{1,0:T(8,128)(2,1)S(1)}, u32[]{:S(2)}, u32[]{:S(2)}) collective-permute-start(bf16[176,512]{1,0:T(8,128)(2,1)S(1)} %get-tuple-element.116), channel_id=1, source_target_pairs={{0,3},{1,2},{2,1},{3,0},{4,7},{5,6},{6,5},{7,4},{8,11},{9,10},{10,... | collective-permute-start | bytes 540680 | tf_op jit(solution)/shard_map/ppermute | solution.py:302
  5.4 8.9 %collective-permute-start.1 = (bf16[64,512]{1,0:T(8,128)(2,1)S(1)}, bf16[64,512]{1,0:T(8,128)(2,1)S(1)}, u32[]{:S(2)}, u32[]{:S(2)}) collective-permute-start(bf16[64,512]{1,0:T(8,128)(2,1)S(1)} %get-tuple-element.101.refs_0_.nodes_ref), channel_id=1, source_target_pairs={{0,4},{1,5},{2,6},{3,7},{4,0},{5,1},{6,2},{7,3},{8,12},{9,13},{10,... | collective-permute-start | bytes 196616 | tf_op jit(solution)/shard_map/ppermute | solution.py:302
  7.2 7.1 %collective-permute-start = (bf16[64,512]{1,0:T(8,128)(2,1)S(1)}, bf16[64,512]{1,0:T(8,128)(2,1)S(1)}, u32[]{:S(2)}, u32[]{:S(2)}) collective-permute-start(bf16[64,512]{1,0:T(8,128)(2,1)S(1)} %get-tuple-element.101.refs_0_.nodes_ref), channel_id=1, source_target_pairs={{0,12},{1,13},{2,14},{3,15},{4,8},{5,9},{6,10},{7,11},{8,4},{9,5},... | collective-permute-start | bytes 196616 | tf_op jit(solution)/shard_map/ppermute | solution.py:302
  14.3 4.3 %collective-permute-start.5 = (bf16[64,512]{1,0:T(8,128)(2,1)S(1)}, bf16[64,512]{1,0:T(8,128)(2,1)S(1)}, u32[]{:S(2)}, u32[]{:S(2)}) collective-permute-start(bf16[64,512]{1,0:T(8,128)(2,1)S(1)} %collective-permute-done), channel_id=1, source_target_pairs={{0,4},{1,5},{2,6},{3,7},{4,0},{5,1},{6,2},{7,3},{8,12},{9,13},{10,... | collective-permute-start | bytes 196616 | tf_op jit(solution)/shard_map/ppermute | solution.py:302
  15.7 7.6 %collective-permute-start.8 = (bf16[192,512]{1,0:T(8,128)(2,1)S(1)}, bf16[192,512]{1,0:T(8,128)(2,1)S(1)}, u32[]{:S(2)}, u32[]{:S(2)}) collective-permute-start(bf16[192,512]{1,0:T(8,128)(2,1)S(1)} %pad_maximum_fusion.1), channel_id=1, source_target_pairs={{0,2},{1,3},{2,0},{3,1},{4,6},{5,7},{6,4},{7,5},{8,10},{9,11},{10,... | collective-permute-start | bytes 589832 | tf_op jit(solution)/shard_map/ppermute | solution.py:302
  18.6 4.7 %collective-permute-start.7 = (bf16[256,512]{1,0:T(8,128)(2,1)S(1)}, bf16[256,512]{1,0:T(8,128)(2,1)S(1)}, u32[]{:S(2)}, u32[]{:S(2)}) collective-permute-start(bf16[256,512]{1,0:T(8,128)(2,1)S(1)} %constant_dynamic-update-slice_fusion.refs_4_), channel_id=1, source_target_pairs={{0,1},{1,0},{2,3},{3,2},{4,5},{5,4},{6,7},{7,6},{8,9},{9,8},{10,11... | collective-permute-start | bytes 786440 | tf_op jit(solution)/shard_map/ppermute | solution.py:302
  18.7 6.9 %collective-permute-start.6 = (bf16[64,512]{1,0:T(8,128)(2,1)S(1)}, bf16[64,512]{1,0:T(8,128)(2,1)S(1)}, u32[]{:S(2)}, u32[]{:S(2)}) collective-permute-start(bf16[64,512]{1,0:T(8,128)(2,1)S(1)} %collective-permute-done.5), channel_id=1, source_target_pairs={{0,2},{1,3},{2,0},{3,1},{4,6},{5,7},{6,4},{7,5},{8,10},{9,11},{10,... | collective-permute-start | bytes 196616 | tf_op jit(solution)/shard_map/ppermute | solution.py:302
  29.2 6.9 %collective-permute-start.10 = (bf16[64,512]{1,0:T(8,128)(2,1)S(1)}, bf16[64,512]{1,0:T(8,128)(2,1)S(1)}, u32[]{:S(2)}, u32[]{:S(2)}) collective-permute-start(bf16[64,512]{1,0:T(8,128)(2,1)S(1)} %get-tuple-element.140), channel_id=1, source_target_pairs={{0,8},{1,9},{2,10},{3,11},{4,12},{5,13},{6,14},{7,15},{8,0},{9,1},... | collective-permute-start | bytes 196616 | tf_op jit(solution)/shard_map/ppermute | solution.py:302
  31.9 6.3 %collective-permute-start.11 = (bf16[64,512]{1,0:T(8,128)(2,1)S(1)}, bf16[64,512]{1,0:T(8,128)(2,1)S(1)}, u32[]{:S(2)}, u32[]{:S(2)}) collective-permute-start(bf16[64,512]{1,0:T(8,128)(2,1)S(1)} %get-tuple-element.141), channel_id=1, source_target_pairs={{0,12},{1,13},{2,14},{3,15},{4,8},{5,9},{6,10},{7,11},{8,4},{9,5},... | collective-permute-start | bytes 196616 | tf_op jit(solution)/shard_map/ppermute | solution.py:302
  31.9 6.3 %collective-permute-start.12 = (bf16[64,512]{1,0:T(8,128)(2,1)S(1)}, bf16[64,512]{1,0:T(8,128)(2,1)S(1)}, u32[]{:S(2)}, u32[]{:S(2)}) collective-permute-start(bf16[64,512]{1,0:T(8,128)(2,1)S(1)} %get-tuple-element.142), channel_id=1, source_target_pairs={{0,4},{1,5},{2,6},{3,7},{4,0},{5,1},{6,2},{7,3},{8,12},{9,13},{10,... | collective-permute-start | bytes 196616 | tf_op jit(solution)/shard_map/ppermute | solution.py:302
  38.9 5.7 %collective-permute-start.14 = (bf16[64,512]{1,0:T(8,128)(2,1)S(1)}, bf16[64,512]{1,0:T(8,128)(2,1)S(1)}, u32[]{:S(2)}, u32[]{:S(2)}) collective-permute-start(bf16[64,512]{1,0:T(8,128)(2,1)S(1)} %shard_map.191.refs_0_.nodes_ref), channel_id=1, source_target_pairs={{0,4},{1,5},{2,6},{3,7},{4,0},{5,1},{6,2},{7,3},{8,12},{9,13},{10,... | collective-permute-start | bytes 196616 | tf_op jit(solution)/shard_map/ppermute | solution.py:302
  39.6 6.1 %collective-permute-start.13 = (bf16[64,512]{1,0:T(8,128)(2,1)S(1)}, bf16[64,512]{1,0:T(8,128)(2,1)S(1)}, u32[]{:S(2)}, u32[]{:S(2)}) collective-permute-start(bf16[64,512]{1,0:T(8,128)(2,1)S(1)} %shard_map.191.refs_0_.nodes_ref), channel_id=1, source_target_pairs={{0,12},{1,13},{2,14},{3,15},{4,8},{5,9},{6,10},{7,11},{8,4},{9,5},... | collective-permute-start | bytes 196616 | tf_op jit(solution)/shard_map/ppermute | solution.py:302
  45.6 4.3 %collective-permute-start.16 = (bf16[64,512]{1,0:T(8,128)(2,1)S(1)}, bf16[64,512]{1,0:T(8,128)(2,1)S(1)}, u32[]{:S(2)}, u32[]{:S(2)}) collective-permute-start(bf16[64,512]{1,0:T(8,128)(2,1)S(1)} %collective-permute-done.13), channel_id=1, source_target_pairs={{0,4},{1,5},{2,6},{3,7},{4,0},{5,1},{6,2},{7,3},{8,12},{9,13},{10,... | collective-permute-start | bytes 196616 | tf_op jit(solution)/shard_map/ppermute | solution.py:302
  45.7 5.9 %collective-permute-start.15 = (bf16[192,512]{1,0:T(8,128)(2,1)S(1)}, bf16[192,512]{1,0:T(8,128)(2,1)S(1)}, u32[]{:S(2)}, u32[]{:S(2)}) collective-permute-start(bf16[192,512]{1,0:T(8,128)(2,1)S(1)} %pad_maximum_fusion.2), channel_id=1, source_target_pairs={{0,2},{1,3},{2,0},{3,1},{4,6},{5,7},{6,4},{7,5},{8,10},{9,11},{10,... | collective-permute-start | bytes 589832 | tf_op jit(solution)/shard_map/ppermute | solution.py:302
  49.9 1.7 %collective-permute-start.18 = (bf16[256,512]{1,0:T(8,128)(2,1)S(1)}, bf16[256,512]{1,0:T(8,128)(2,1)S(1)}, u32[]{:S(2)}, u32[]{:S(2)}) collective-permute-start(bf16[256,512]{1,0:T(8,128)(2,1)S(1)} %pad_maximum_fusion.refs_4_), channel_id=1, source_target_pairs={{0,1},{1,0},{2,3},{3,2},{4,5},{5,4},{6,7},{7,6},{8,9},{9,8},{10,11... | collective-permute-start | bytes 786440 | tf_op jit(solution)/shard_map/ppermute | solution.py:302
  50.0 4.5 %collective-permute-start.17 = (bf16[64,512]{1,0:T(8,128)(2,1)S(1)}, bf16[64,512]{1,0:T(8,128)(2,1)S(1)}, u32[]{:S(2)}, u32[]{:S(2)}) collective-permute-start(bf16[64,512]{1,0:T(8,128)(2,1)S(1)} %collective-permute-done.16), channel_id=1, source_target_pairs={{0,2},{1,3},{2,0},{3,1},{4,6},{5,7},{6,4},{7,5},{8,10},{9,11},{10,... | collective-permute-start | bytes 196616 | tf_op jit(solution)/shard_map/ppermute | solution.py:302
  58.1 5.9 %collective-permute-start.23 = (bf16[160,512]{1,0:T(8,128)(2,1)S(1)}, bf16[160,512]{1,0:T(8,128)(2,1)S(1)}, u32[]{:S(2)}, u32[]{:S(2)}) collective-permute-start(bf16[160,512]{1,0:T(8,128)(2,1)S(1)} %get-tuple-element.190), channel_id=1, source_target_pairs={{0,1},{1,0},{2,3},{3,2},{4,5},{5,4},{6,7},{7,6},{8,9},{9,8},{10,11... | collective-permute-start | bytes 491528 | tf_op jit(solution)/shard_map/ppermute | solution.py:302
  58.3 11.3 %collective-permute-start.24 = (bf16[160,512]{1,0:T(8,128)(2,1)S(1)}, bf16[160,512]{1,0:T(8,128)(2,1)S(1)}, u32[]{:S(2)}, u32[]{:S(2)}) collective-permute-start(bf16[160,512]{1,0:T(8,128)(2,1)S(1)} %get-tuple-element.194), channel_id=1, source_target_pairs={{0,2},{1,3},{2,0},{3,1},{4,6},{5,7},{6,4},{7,5},{8,10},{9,11},{10,... | collective-permute-start | bytes 491528 | tf_op jit(solution)/shard_map/ppermute | solution.py:302
  59.8 9.8 %collective-permute-start.25 = (bf16[160,512]{1,0:T(8,128)(2,1)S(1)}, bf16[160,512]{1,0:T(8,128)(2,1)S(1)}, u32[]{:S(2)}, u32[]{:S(2)}) collective-permute-start(bf16[160,512]{1,0:T(8,128)(2,1)S(1)} %get-tuple-element.195), channel_id=1, source_target_pairs={{0,3},{1,2},{2,1},{3,0},{4,7},{5,6},{6,5},{7,4},{8,11},{9,10},{10,... | collective-permute-start | bytes 491528 | tf_op jit(solution)/shard_map/ppermute | solution.py:302
  60.0 7.4 %collective-permute-start.20 = (bf16[64,512]{1,0:T(8,128)(2,1)S(1)}, bf16[64,512]{1,0:T(8,128)(2,1)S(1)}, u32[]{:S(2)}, u32[]{:S(2)}) collective-permute-start(bf16[64,512]{1,0:T(8,128)(2,1)S(1)} %get-tuple-element.185), channel_id=1, source_target_pairs={{0,8},{1,9},{2,10},{3,11},{4,12},{5,13},{6,14},{7,15},{8,0},{9,1},... | collective-permute-start | bytes 196616 | tf_op jit(solution)/shard_map/ppermute | solution.py:302
  62.5 6.7 %collective-permute-start.21 = (bf16[64,512]{1,0:T(8,128)(2,1)S(1)}, bf16[64,512]{1,0:T(8,128)(2,1)S(1)}, u32[]{:S(2)}, u32[]{:S(2)}) collective-permute-start(bf16[64,512]{1,0:T(8,128)(2,1)S(1)} %get-tuple-element.186), channel_id=1, source_target_pairs={{0,12},{1,13},{2,14},{3,15},{4,8},{5,9},{6,10},{7,11},{8,4},{9,5},... | collective-permute-start | bytes 196616 | tf_op jit(solution)/shard_map/ppermute | solution.py:302
  64.0 5.6 %collective-permute-start.22 = (bf16[64,512]{1,0:T(8,128)(2,1)S(1)}, bf16[64,512]{1,0:T(8,128)(2,1)S(1)}, u32[]{:S(2)}, u32[]{:S(2)}) collective-permute-start(bf16[64,512]{1,0:T(8,128)(2,1)S(1)} %get-tuple-element.187), channel_id=1, source_target_pairs={{0,4},{1,5},{2,6},{3,7},{4,0},{5,1},{6,2},{7,3},{8,12},{9,13},{10,... | collective-permute-start | bytes 196616 | tf_op jit(solution)/shard_map/ppermute | solution.py:302
  (2 other events, 3.1 us)

commit v6 on v5

--- a/solution.py
+++ b/solution.py
@@ -93,10 +93,14 @@
     meta = jnp.where(row_at == 1, s_within, meta)
     meta = jnp.where(row_at == 2, r_block, meta)
     meta = jnp.where(row_at == 3, r_within, meta).astype(F32).astype(BF)
+    moved = match_columns(pos, PLANE * slot)
+    placed = mm(moved, fe_ref[...]).astype(BF)
     for m, ref in enumerate(slot_refs):
-        moved = match_columns(pos - m * slot, slot)
-        ref[0:slot, :] = mm(moved, fe_ref[...]).astype(BF)
-        tail = lax.dot_general(meta, moved, (((1,), (1,)), ((), ())), preferred_element_type=F32)
+        rows = slice(m * slot, (m + 1) * slot)
+        ref[0:slot, :] = placed[rows]
+        tail = lax.dot_general(
+            meta, moved[rows], (((1,), (1,)), ((), ())), preferred_element_type=F32
+        )
         ref[slot:, :] = jnp.zeros((ref.shape[0] - slot, ref.shape[1]), BF)
         ref[slot : slot + 16, 0:slot] = jnp.concatenate(
             [tail, jnp.zeros((8, slot), F32)], axis=0
@@ -129,7 +133,7 @@
     if before:
         new_ref[0 : rows.start, :] = before[0][0 : rows.start, :]
     total = before[1][...] if before else None
-    block = min(rows.stop - rows.start, 256)
+    block = min(rows.stop - rows.start, 512)
     for start in range(rows.start, rows.stop, block):
         send = send_ref[start : start + block].reshape(1, -1)
         recv = recv_ref[start : start + block].reshape(1, -1)
@@ -146,10 +150,10 @@
     sum_ref[...] = total
 
 
-def far_first_kernel(lines, slot, *refs):
-    slots, tables, win_ref = refs[0:PLANE], refs[PLANE : PLANE + 2], refs[PLANE + 2]
-    out_ref, late_ref, *scatter_refs = refs[PLANE + 3 :]
-    span, size = lines * COARSE, PLANE // len(scatter_refs)
+def far_ready_kernel(lines, slot, *refs):
+    slots, (table_ref, win_ref) = refs[0:PLANE], refs[PLANE : PLANE + 2]
+    out_ref, early_ref, late_ref, scatter_ref = refs[PLANE + 2 :]
+    span, width = lines * COARSE, table_ref.shape[1]
     columns_s, columns_r, rows_r = [], [], []
     for ref in slots:
         meta = ref[slot : slot + 16, :].astype(F32)[0:8, 0 : -(-slot // 128) * 128]
@@ -158,17 +162,20 @@
         columns_r.append((tall[:, 2:3] * COARSE + tall[:, 3:4]).astype(I32) - COARSE)
         rows_r.append((meta[2:3, 0:slot] * COARSE + meta[3:4, 0:slot]).astype(I32) - COARSE)
     column_s, column_r = jnp.concatenate(columns_s, axis=0), jnp.concatenate(columns_r, axis=0)
-    senders = None
-    for q, table in enumerate(tables):
-        piece = mm(match_rows(column_s, span, q * span), table[...])
-        senders = piece if senders is None else senders + piece
-    receivers = mm(match_rows(column_r, span), tables[0][...])
+    receivers = mm(match_rows(column_r, span), table_ref[...]).astype(BF)
     edges = jnp.concatenate([ref[0:slot, :] for ref in slots], axis=0)
-    stacked = jnp.concatenate([edges, senders.astype(BF), receivers.astype(BF)], axis=1)
-    out_ref[...] = mm(stacked, win_ref[...])
+    product = mm(edges, win_ref[0:width, :])
+    out_ref[...] = product + mm(receivers, win_ref[2 * width :, :])
+    early_ref[...] = match_rows(column_s, 2 * span)
     late_ref[...] = match_rows(column_s, 2 * span, 2 * span)
-    for i, ref in enumerate(scatter_refs):
-        ref[...] = match_columns(jnp.concatenate(rows_r[i * size : (i + 1) * size], axis=1), span)
+    scatter_ref[...] = match_columns(jnp.concatenate(rows_r, axis=1), span)
+
+
+def far_first_kernel(straight_ref, across_ref, pre_ref, early_ref, win_ref, out_ref):
+    width = pre_ref.shape[1]
+    table = jnp.concatenate([straight_ref[...], across_ref[...]], axis=0)
+    senders = mm(early_ref[...], table).astype(BF)
+    out_ref[...] = pre_ref[...] + mm(senders, win_ref[width : 2 * width, :])
 
 
 def far_second_kernel(layer, lines, slot, start, chained, keep, *refs):
@@ -199,20 +206,25 @@
         ref[...] = total[(i + 1) * COARSE : (i + 2) * COARSE, :].astype(BF)
 
 
-def node_update(layer, nodes, sums, win_ref, wout_ref, vec_refs):
-    stacked = jnp.concatenate([nodes, sums.astype(BF)], axis=1)
+def node_tail(layer, nodes, pre_act, wout_ref, vec_refs):
     bias, gain, shift = [v[layer : layer + 1, :] for v in vec_refs]
-    normed = edge_tail(mm(stacked, win_ref[layer]), wout_ref[layer], bias, gain, shift)
+    normed = edge_tail(pre_act, wout_ref[layer], bias, gain, shift)
     return (nodes.astype(F32) + normed).astype(BF)
 
 
-def rest_kernel(layer, nodes_ref, sum_ref, win_ref, wout_ref, *refs):
-    sums = sum_ref[COARSE:, :]
-    new = node_update(layer, nodes_ref[...], sums, win_ref, wout_ref, refs[0:3])
-    if len(refs) == 4:
-        refs[3][...] = new
+def rest_kernel(layer, coarse_ref, nodes_ref, sum_ref, win_ref, wout_ref, *refs):
+    nodes, width = nodes_ref[...], nodes_ref.shape[1]
+    both = jnp.concatenate([coarse_ref[...], nodes], axis=0)
+    pre_act = mm(both, win_ref[layer, 0:width, :])
+    vec_refs, refs, coarse_pre_ref = refs[0:3], refs[3:-1], refs[-1]
+    coarse_pre_ref[...] = pre_act[0:COARSE, :]
+    sums = sum_ref[COARSE:, :].astype(BF)
+    pre_act = pre_act[COARSE:, :] + mm(sums, win_ref[layer, width:, :])
+    new = node_tail(layer, nodes, pre_act, wout_ref, vec_refs)
+    if len(refs) == 1:
+        refs[0][...] = new
         return
-    pos_ref, *slot_refs, out_ref, half_ref, back_ref = refs[3:]
+    pos_ref, *slot_refs, out_ref, half_ref, back_ref = refs
     out_ref[...] = new
     column, count = as_column(pos_ref[...]), back_ref.shape[1]
     slots = jnp.concatenate([ref[...] for ref in slot_refs], axis=0)
@@ -220,7 +232,7 @@
     back_ref[...] = match_rows(column, count, count)
 
 
-def coarse_kernel(layer, lines, nodes_ref, sum_ref, *refs):
+def coarse_kernel(layer, lines, nodes_ref, pre_ref, sum_ref, *refs):
     part_refs, refs = refs[0:lines], refs[lines:]
     (win_ref, wout_ref), vec_refs, refs = refs[0:2], refs[2:5], refs[5:]
     copies = []
@@ -237,7 +249,8 @@
     sums = sum_ref[0:COARSE, :] + part_refs[0][...]
     for ref in part_refs[1:]:
         sums = sums + ref[...].astype(F32)
-    out_ref[...] = node_update(layer, nodes_ref[...], sums, win_ref, wout_ref, vec_refs)
+    pre_act = pre_ref[...] + mm(sums.astype(BF), win_ref[layer, sums.shape[1] :, :])
+    out_ref[...] = node_tail(layer, nodes_ref[...], pre_act, wout_ref, vec_refs)
     if copies:
         copies.append(pltpu.make_async_copy(out_ref, out_hbm.at[0:COARSE, :], sems.at[2]))
         copies[2].start()
@@ -375,14 +388,23 @@
         late = swap(z2, 2)
         table = jnp.concatenate([near, z2], axis=0)
         tables = [table, swap(table, 1)]
-        found = call(
-            functools.partial(far_first_kernel, lines, slot),
-            [shape((far_rows, width), F32), shape((far_rows, 2 * span), BF)]
+        pre_act, early, *found = call(
+            functools.partial(far_ready_kernel, lines, slot),
+            [shape((far_rows, width), F32)]
+            + [shape((far_rows, 2 * span), BF)] * 2
             + [shape((span, far_rows), BF)],
-            [*slots, *tables, weights[l][0]],
-            2 * far_rows * width * (3 * span + 3 * width),
+            [*slots, table, weights[l][0]],
+            2 * far_rows * width * (span + 2 * width),
             limit,
         )
+        pre_act = call(
+            far_first_kernel,
+            [shape((far_rows, width), F32)],
+            [*tables, pre_act, early, weights[l][0]],
+            2 * far_rows * width * (2 * span + width),
+            limit,
+        )
+        found = [*pre_act, *found]
         late, found, done = tied((late, found, done))
         late = jnp.concatenate([across, late], axis=0)
         late = [late, swap(late, 1)]
@@ -419,11 +441,12 @@
             node_in, node_out, node_vecs = *second[0:2], second[2:5]
             weights += [second[5 + 2 * i : 7 + 2 * i] for i in range(layers - 1)]
         ends = [node_in, node_out, *node_vecs]
-        rest = call(
+        *rest, coarse_pre = call(
             functools.partial(rest_kernel, l),
             [shape((node_count - COARSE, width), BF)]
-            + [shape((far_count, width), BF), shape((far_count, 2 * slot), BF)] * last,
-            [rest, sums, *ends] + [pos, *slots[0:2]] * last,
+            + [shape((far_count, width), BF), shape((far_count, 2 * slot), BF)] * last
+            + [shape((COARSE, width), F32)],
+            [coarse, rest, sums, *ends] + [pos, *slots[0:2]] * last,
             6 * (node_count - COARSE) * width * width,
             limit,
         )
@@ -437,7 +460,7 @@
         coarse, *far_out = call(
             functools.partial(coarse_kernel, l, lines),
             return_shapes,
-            [coarse, sums, *parts, *ends, *extra],
+            [coarse, coarse_pre, sums, *parts, *ends, *extra],
             6 * COARSE * width * width,
             limit,
             scratch=scratch if last else (),

time: 71.5 us -> 71.4 us (level)
    pallas_call x15 -> x17, Pallas kernels: 28 us -> 28.6 us  [call(): pl.pallas_call(kernel, out_shape=outs, in_specs=specs, out_specs=[pl.Bloc...]
  transfers between devices with their start and end apart: 26 -> 26, of which waited for: 10 -> 13; matrix products, arithmetic and copies ran while one was open for 0% -> 0% of each run, Pallas kernels for 28% -> 30%
where the time goes in v6:
time: 71.4 us; the launch traced here: 71.2 us
  Pallas kernels  28.6 us (40%)
  starting transfers between devices  27.4 us (38%)
  waiting for transfers between devices  14 us (20%)
  between operations  1.06 us (1%)
    pallas_call x17, Pallas kernels, call(): pl.pallas_call(kernel, out_shape=outs, in_specs=specs, out_specs=[pl.Bloc...  28.6 us
    ppermute x26, starting transfers between devices, swap(): lax.ppermute(values, 'patch', [(i, i ^ distance) for i in range(devices)])  27.4 us
    ppermute x26, waiting for transfers between devices, swap(): lax.ppermute(values, 'patch', [(i, i ^ distance) for i in range(devices)])  14 us
  transfers between devices with their start and end apart: 26, of which 13 were waited for; matrix products, arithmetic and copies ran while one was open for 0% of the time, Pallas kernels for 30%

profile of v6, /device:TPU:0, one launch (start us, length us, event | category | flops | bytes accessed | tf_op | source)
XLA Modules:
  0.0 71.2 jit_solution(16919816201552735665)
XLA Ops:
  0.6 1.5 %shard_map.184 = (s32[1,256]{1,0:T(1,128)S(1)}, bf16[64,512]{1,0:T(8,128)(2,1)S(1)}, bf16[192,512]{1,0:T(8,128)(2,1)S(1)}, bf16[176,512]{1,0:T(8,128)(2,1)S(1)},...) custom-call(s32[1]{0:T(128)} %bitcast.own_ref, s32[1,256]{1,0:T(1,128)} %bitcast.3, ...), custom_call_target="tpu_custom_call" | custom-call | flops 167772160 | bytes 1510404 | tf_op jit(solution)/shard_map/pallas_call | solution.py:271
  2.7 2.6 %collective-permute-start.3 = (bf16[176,512]{1,0:T(8,128)(2,1)S(1)}, bf16[176,512]{1,0:T(8,128)(2,1)S(1)}, u32[]{:S(2)}, u32[]{:S(2)}) collective-permute-start(bf16[176,512]{1,0:T(8,128)(2,1)S(1)} %get-tuple-element.120), channel_id=1, source_target_pairs={{0,2},{1,3},{2,0},{3,1},{4,6},{5,7},{6,4},{7,5},{8,10},{9,11},{10,... | collective-permute-start | bytes 540680 | tf_op jit(solution)/shard_map/ppermute | solution.py:315
  5.3 3.8 %collective-permute-start = (bf16[64,512]{1,0:T(8,128)(2,1)S(1)}, bf16[64,512]{1,0:T(8,128)(2,1)S(1)}, u32[]{:S(2)}, u32[]{:S(2)}) collective-permute-start(bf16[64,512]{1,0:T(8,128)(2,1)S(1)} %get-tuple-element.106.refs_0_.coarse_ref.nodes_ref), channel_id=1, source_target_pairs={{0,12},{1,13},{2,14},{3,15},{4,8},{5,9},{6,10},{7,11},{8,4},{9,5},... | collective-permute-start | bytes 196616 | tf_op jit(solution)/shard_map/ppermute | solution.py:315
  9.2 1.9 %shard_map.185 = (bf16[768,512]{1,0:T(8,128)(2,1)S(1)}, s32[768]{0:T(1024)S(1)}, s32[768]{0:T(1024)S(1)}, f32[2,512]{1,0:T(2,128)S(1)}, f32[2,512]{1,0:T(2,128)S...) custom-call(bf16[768,512]{1,0:T(8,128)(2,1)} %refs_0_.1, s32[768]{0:T(1024)} %refs_1_.1, ...), custom_call_target="tpu_custom_call" | custom-call | bytes 7901184 | tf_op jit(solution)/shard_map/pallas_call | solution.py:271
  11.1 2.6 %shard_map.186 = (bf16[512,512]{1,0:T(8,128)(2,1)S(1)}, f32[256,512]{1,0:T(8,128)S(1)}) custom-call(bf16[64,512]{1,0:T(8,128)(2,1)S(1)} %get-tuple-element.106.refs_0_.coarse_ref.nodes_ref, bf16[192,512]{1,0:T(8,128)(2,1)S(1)} %get-tuple-element.107.refs_1_.nodes_ref, bf16[768,512]{1,0:T(8,128)(2,1)S(1)} %get-tuple-element.108.refs_2_, ...), custom_call_target="tpu_custom_call" | custom-call | tf_op jit(solution)/shard_map/pallas_call | solution.py:271
  14.0 1.9 %collective-permute-start.5 = (bf16[64,512]{1,0:T(8,128)(2,1)S(1)}, bf16[64,512]{1,0:T(8,128)(2,1)S(1)}, u32[]{:S(2)}, u32[]{:S(2)}) collective-permute-start(bf16[64,512]{1,0:T(8,128)(2,1)S(1)} %collective-permute-done), channel_id=1, source_target_pairs={{0,4},{1,5},{2,6},{3,7},{4,0},{5,1},{6,2},{7,3},{8,12},{9,13},{10,... | collective-permute-start | bytes 196616 | tf_op jit(solution)/shard_map/ppermute | solution.py:315
  15.9 1.6 %collective-permute-start.8 = (bf16[192,512]{1,0:T(8,128)(2,1)S(1)}, bf16[192,512]{1,0:T(8,128)(2,1)S(1)}, u32[]{:S(2)}, u32[]{:S(2)}) collective-permute-start(bf16[192,512]{1,0:T(8,128)(2,1)S(1)} %pad_maximum_fusion.1), channel_id=1, source_target_pairs={{0,2},{1,3},{2,0},{3,1},{4,6},{5,7},{6,4},{7,5},{8,10},{9,11},{10,... | collective-permute-start | bytes 589832 | tf_op jit(solution)/shard_map/ppermute | solution.py:315
  18.3 1.6 %collective-permute-start.6 = (bf16[64,512]{1,0:T(8,128)(2,1)S(1)}, bf16[64,512]{1,0:T(8,128)(2,1)S(1)}, u32[]{:S(2)}, u32[]{:S(2)}) collective-permute-start(bf16[64,512]{1,0:T(8,128)(2,1)S(1)} %collective-permute-done.5), channel_id=1, source_target_pairs={{0,2},{1,3},{2,0},{3,1},{4,6},{5,7},{6,4},{7,5},{8,10},{9,11},{10,... | collective-permute-start | bytes 196616 | tf_op jit(solution)/shard_map/ppermute | solution.py:315
  19.9 1.7 %shard_map.189 = (bf16[768,512]{1,0:T(8,128)(2,1)S(1)}, f32[256,512]{1,0:T(8,128)S(1)}) custom-call(bf16[64,512]{1,0:T(8,128)(2,1)S(1)} %get-tuple-element.106.refs_0_.coarse_ref.nodes_ref, bf16[192,512]{1,0:T(8,128)(2,1)S(1)} %get-tuple-element.107.refs_1_.nodes_ref, bf16[768,512]{1,0:T(8,128)(2,1)S(1)} %get-tuple-element.108.refs_2_, ...), custom_call_target="tpu_custom_call" | custom-call | flops 738197504 | bytes 5523456 | tf_op jit(solution)/shard_map/pallas_call | solution.py:271
  21.6 1.8 %shard_map.187 = (f32[640,512]{1,0:T(8,128)S(1)}, bf16[640,512]{1,0:T(8,128)(2,1)S(1)}, bf16[640,512]{1,0:T(8,128)(2,1)S(1)}, bf16[256,640]{1,0:T(8,128)(2,1)S(1)}) custom-call(bf16[176,512]{1,0:T(8,128)(2,1)S(1)} %get-tuple-element.127.refs_0_.refs_10_, bf16[176,512]{1,0:T(8,128)(2,1)S(1)} %collective-permute-done.2.refs_1_.refs_11_, ...), custom_call_target="tpu_custom_call" | custom-call | flops 838860800 | bytes 5505024 | tf_op jit(solution)/shard_map/pallas_call | solution.py:271
  26.0 2.0 %shard_map.192 = (bf16[176,512]{1,0:T(8,128)(2,1)S(1)}, bf16[176,512]{1,0:T(8,128)(2,1)S(1)}, bf16[176,512]{1,0:T(8,128)(2,1)S(1)}, bf16[176,512]{1,0:T(8,128)(2...) custom-call(bf16[256,512]{1,0:T(8,128)(2,1)S(1)} %constant_dynamic-u, ...), custom_call_target="tpu_custom_call" | custom-call | flops 1174405120 | bytes 6696960 | tf_op jit(solution)/shard_map/pallas_call | solution.py:271
  28.0 2.7 %collective-permute-start.10 = (bf16[64,512]{1,0:T(8,128)(2,1)S(1)}, bf16[64,512]{1,0:T(8,128)(2,1)S(1)}, u32[]{:S(2)}, u32[]{:S(2)}) collective-permute-start(bf16[64,512]{1,0:T(8,128)(2,1)S(1)} %get-tuple-element.159), channel_id=1, source_target_pairs={{0,8},{1,9},{2,10},{3,11},{4,12},{5,13},{6,14},{7,15},{8,0},{9,1},... | collective-permute-start | bytes 196616 | tf_op jit(solution)/shard_map/ppermute | solution.py:315
  30.7 1.6 %collective-permute-start.11 = (bf16[64,512]{1,0:T(8,128)(2,1)S(1)}, bf16[64,512]{1,0:T(8,128)(2,1)S(1)}, u32[]{:S(2)}, u32[]{:S(2)}) collective-permute-start(bf16[64,512]{1,0:T(8,128)(2,1)S(1)} %get-tuple-element.160), channel_id=1, source_target_pairs={{0,12},{1,13},{2,14},{3,15},{4,8},{5,9},{6,10},{7,11},{8,4},{9,5},... | collective-permute-start | bytes 196616 | tf_op jit(solution)/shard_map/ppermute | solution.py:315
  32.3 2.6 %shard_map.190 = (bf16[2,1024,512]{2,1,0:T(8,128)(2,1)S(1)}, bf16[2,512,512]{2,1,0:T(8,128)(2,1)S(1)}, f32[2,512]{1,0:T(2,128)S(1)}, f32[2,512]{1,0:T(2,128)S(1)...) custom-call(bf16[2,1024,512]{2,1,0:T(8,128)(2,1)} %refs_0_.2, ...), custom_call_target="tpu_custom_call" | custom-call | bytes 12607488 | tf_op jit(solution)/shard_map/pallas_call | solution.py:271
  35.7 1.6 %collective-permute-done.11.refs_2_ = bf16[64,512]{1,0:T(8,128)(2,1)S(1)} collective-permute-done((bf16[64,512]{1,0:T(8,128)(2,1)S(1)}, bf16[64,512]{1,0:T(8,128)(2,1)S(1)}, u32[]{:S(2)}, u32[]{:S(2)}) %collective-permute-start.11) | collective-permute-done | bytes 65568 | tf_op jit(solution)/shard_map/ppermute | solution.py:315
  38.1 3.5 %collective-permute-start.13 = (bf16[64,512]{1,0:T(8,128)(2,1)S(1)}, bf16[64,512]{1,0:T(8,128)(2,1)S(1)}, u32[]{:S(2)}, u32[]{:S(2)}) collective-permute-start(bf16[64,512]{1,0:T(8,128)(2,1)S(1)} %shard_map.193.refs_0_.coarse_ref.nodes_ref), channel_id=1, source_target_pairs={{0,12},{1,13},{2,14},{3,15},{4,8},{5,9},{6,10},{7,11},{8,4},{9,5},... | collective-permute-start | bytes 196616 | tf_op jit(solution)/shard_map/ppermute | solution.py:315
  41.7 2.6 %shard_map.194 = (bf16[512,512]{1,0:T(8,128)(2,1)S(1)}, f32[256,512]{1,0:T(8,128)S(1)}) custom-call(bf16[64,512]{1,0:T(8,128)(2,1)S(1)} %shard_map.193.refs_0_.coarse_ref.nodes_ref, bf16[192,512]{1,0:T(8,128)(2,1)S(1)} %get-tuple-element.162.refs_1_.nodes_ref, bf16[768,512]{1,0:T(8,128)(2,1)S(1)} %get-tuple-element.163.refs_2_, ...), custom_call_target="tpu_custom_call" | custom-call | flops 1476395008 | bytes 4212736 | tf_op jit(solution)/shard_map/pallas_call | solution.py:271
  47.1 3.1 %collective-permute-done.16 = bf16[64,512]{1,0:T(8,128)(2,1)S(1)} collective-permute-done((bf16[64,512]{1,0:T(8,128)(2,1)S(1)}, bf16[64,512]{1,0:T(8,128)(2,1)S(1)}, u32[]{:S(2)}, u32[]{:S(2)}) %collective-permute-start.16) | collective-permute-done | bytes 65568 | tf_op jit(solution)/shard_map/ppermute | solution.py:315
  50.7 1.8 %shard_map.195 = (f32[640,512]{1,0:T(8,128)S(1)}, bf16[640,512]{1,0:T(8,128)(2,1)S(1)}, bf16[640,512]{1,0:T(8,128)(2,1)S(1)}, bf16[256,640]{1,0:T(8,128)(2,1)S(1)}) custom-call(bf16[176,512]{1,0:T(8,128)(2,1)S(1)} %get-tuple-element.170.refs_0_.refs_10_, bf16[176,512]{1,0:T(8,128)(2,1)S(1)} %get-tuple-element.171.refs_1_.refs_11_, ...), custom_call_target="tpu_custom_call" | custom-call | flops 838860800 | bytes 5505024 | tf_op jit(solution)/shard_map/pallas_call | solution.py:271
  54.8 1.5 %collective-permute-done.19.refs_1_ = bf16[256,512]{1,0:T(8,128)(2,1)S(1)} collective-permute-done((bf16[256,512]{1,0:T(8,128)(2,1)S(1)}, bf16[256,512]{1,0:T(8,128)(2,1)S(1)}, u32[]{:S(2)}, u32[]{:S(2)}) %collective-permute-start.19) | collective-permute-done | bytes 262176 | tf_op jit(solution)/shard_map/ppermute | solution.py:315
  56.3 2.0 %shard_map.197 = (bf16[160,512]{1,0:T(8,128)(2,1)S(1)}, bf16[160,512]{1,0:T(8,128)(2,1)S(1)}, bf16[160,512]{1,0:T(8,128)(2,1)S(1)}, bf16[160,512]{1,0:T(8,128)(2...) custom-call(bf16[256,512]{1,0:T(8,128)(2,1)S(1)} %constant_dynamic-u, ...), custom_call_target="tpu_custom_call" | custom-call | flops 1174405120 | bytes 6631424 | tf_op jit(solution)/shard_map/pallas_call | solution.py:271
  61.3 2.4 %collective-permute-start.22 = (bf16[64,512]{1,0:T(8,128)(2,1)S(1)}, bf16[64,512]{1,0:T(8,128)(2,1)S(1)}, u32[]{:S(2)}, u32[]{:S(2)}) collective-permute-start(bf16[64,512]{1,0:T(8,128)(2,1)S(1)} %get-tuple-element.199), channel_id=1, source_target_pairs={{0,12},{1,13},{2,14},{3,15},{4,8},{5,9},{6,10},{7,11},{8,4},{9,5},... | collective-permute-start | bytes 196616 | tf_op jit(solution)/shard_map/ppermute | solution.py:315
  63.8 2.5 %shard_map.198 = (bf16[768,512]{1,0:T(8,128)(2,1)}, f32[256,512]{1,0:T(8,128)S(1)}) custom-call(bf16[64,512]{1,0:T(8,128)(2,1)S(1)} %shard_map.193.refs_0_.coarse_ref.nodes_ref, bf16[192,512]{1,0:T(8,128)(2,1)S(1)} %get-tuple-element.162.refs_1_.nodes_ref, bf16[768,512]{1,0:T(8,128)(2,1)S(1)} %get-tuple-element.163.refs_2_, ...), custom_call_target="tpu_custom_call" | custom-call | flops 738197504 | bytes 5523456 | tf_op jit(solution)/shard_map/pallas_call | solution.py:271
  67.1 1.8 %collective-permute-done.21.refs_1_ = bf16[64,512]{1,0:T(8,128)(2,1)S(1)} collective-permute-done((bf16[64,512]{1,0:T(8,128)(2,1)S(1)}, bf16[64,512]{1,0:T(8,128)(2,1)S(1)}, u32[]{:S(2)}, u32[]{:S(2)}) %collective-permute-start.21) | collective-permute-done | bytes 65568 | tf_op jit(solution)/shard_map/ppermute | solution.py:315
  (56 shorter events, 17.4 us)
Async XLA Ops:
  2.2 11.6 %collective-permute-start.2 = (bf16[176,512]{1,0:T(8,128)(2,1)S(1)}, bf16[176,512]{1,0:T(8,128)(2,1)S(1)}, u32[]{:S(2)}, u32[]{:S(2)}) collective-permute-start(bf16[176,512]{1,0:T(8,128)(2,1)S(1)} %get-tuple-element.119), channel_id=1, source_target_pairs={{0,1},{1,0},{2,3},{3,2},{4,5},{5,4},{6,7},{7,6},{8,9},{9,8},{10,11... | collective-permute-start | bytes 540680 | tf_op jit(solution)/shard_map/ppermute | solution.py:315
  2.7 11.1 %collective-permute-start.3 = (bf16[176,512]{1,0:T(8,128)(2,1)S(1)}, bf16[176,512]{1,0:T(8,128)(2,1)S(1)}, u32[]{:S(2)}, u32[]{:S(2)}) collective-permute-start(bf16[176,512]{1,0:T(8,128)(2,1)S(1)} %get-tuple-element.120), channel_id=1, source_target_pairs={{0,2},{1,3},{2,0},{3,1},{4,6},{5,7},{6,4},{7,5},{8,10},{9,11},{10,... | collective-permute-start | bytes 540680 | tf_op jit(solution)/shard_map/ppermute | solution.py:315
  5.3 8.7 %collective-permute-start.4 = (bf16[176,512]{1,0:T(8,128)(2,1)S(1)}, bf16[176,512]{1,0:T(8,128)(2,1)S(1)}, u32[]{:S(2)}, u32[]{:S(2)}) collective-permute-start(bf16[176,512]{1,0:T(8,128)(2,1)S(1)} %get-tuple-element.121), channel_id=1, source_target_pairs={{0,3},{1,2},{2,1},{3,0},{4,7},{5,6},{6,5},{7,4},{8,11},{9,10},{10,... | collective-permute-start | bytes 540680 | tf_op jit(solution)/shard_map/ppermute | solution.py:315
  5.3 8.4 %collective-permute-start = (bf16[64,512]{1,0:T(8,128)(2,1)S(1)}, bf16[64,512]{1,0:T(8,128)(2,1)S(1)}, u32[]{:S(2)}, u32[]{:S(2)}) collective-permute-start(bf16[64,512]{1,0:T(8,128)(2,1)S(1)} %get-tuple-element.106.refs_0_.coarse_ref.nodes_ref), channel_id=1, source_target_pairs={{0,12},{1,13},{2,14},{3,15},{4,8},{5,9},{6,10},{7,11},{8,4},{9,5},... | collective-permute-start | bytes 196616 | tf_op jit(solution)/shard_map/ppermute | solution.py:315
  9.2 4.6 %collective-permute-start.1 = (bf16[64,512]{1,0:T(8,128)(2,1)S(1)}, bf16[64,512]{1,0:T(8,128)(2,1)S(1)}, u32[]{:S(2)}, u32[]{:S(2)}) collective-permute-start(bf16[64,512]{1,0:T(8,128)(2,1)S(1)} %get-tuple-element.106.refs_0_.coarse_ref.nodes_ref), channel_id=1, source_target_pairs={{0,4},{1,5},{2,6},{3,7},{4,0},{5,1},{6,2},{7,3},{8,12},{9,13},{10,... | collective-permute-start | bytes 196616 | tf_op jit(solution)/shard_map/ppermute | solution.py:315
  14.0 4.3 %collective-permute-start.5 = (bf16[64,512]{1,0:T(8,128)(2,1)S(1)}, bf16[64,512]{1,0:T(8,128)(2,1)S(1)}, u32[]{:S(2)}, u32[]{:S(2)}) collective-permute-start(bf16[64,512]{1,0:T(8,128)(2,1)S(1)} %collective-permute-done), channel_id=1, source_target_pairs={{0,4},{1,5},{2,6},{3,7},{4,0},{5,1},{6,2},{7,3},{8,12},{9,13},{10,... | collective-permute-start | bytes 196616 | tf_op jit(solution)/shard_map/ppermute | solution.py:315
  15.9 7.4 %collective-permute-start.8 = (bf16[192,512]{1,0:T(8,128)(2,1)S(1)}, bf16[192,512]{1,0:T(8,128)(2,1)S(1)}, u32[]{:S(2)}, u32[]{:S(2)}) collective-permute-start(bf16[192,512]{1,0:T(8,128)(2,1)S(1)} %pad_maximum_fusion.1), channel_id=1, source_target_pairs={{0,2},{1,3},{2,0},{3,1},{4,6},{5,7},{6,4},{7,5},{8,10},{9,11},{10,... | collective-permute-start | bytes 589832 | tf_op jit(solution)/shard_map/ppermute | solution.py:315
  18.3 6.0 %collective-permute-start.6 = (bf16[64,512]{1,0:T(8,128)(2,1)S(1)}, bf16[64,512]{1,0:T(8,128)(2,1)S(1)}, u32[]{:S(2)}, u32[]{:S(2)}) collective-permute-start(bf16[64,512]{1,0:T(8,128)(2,1)S(1)} %collective-permute-done.5), channel_id=1, source_target_pairs={{0,2},{1,3},{2,0},{3,1},{4,6},{5,7},{6,4},{7,5},{8,10},{9,11},{10,... | collective-permute-start | bytes 196616 | tf_op jit(solution)/shard_map/ppermute | solution.py:315
  19.9 3.5 %collective-permute-start.7 = (bf16[256,512]{1,0:T(8,128)(2,1)S(1)}, bf16[256,512]{1,0:T(8,128)(2,1)S(1)}, u32[]{:S(2)}, u32[]{:S(2)}) collective-permute-start(bf16[256,512]{1,0:T(8,128)(2,1)S(1)} %constant_dynamic-update-slice_fusion.refs_4_.straight_ref), channel_id=1, source_target_pairs={{0,1},{1,0},{2,3},{3,2},{4,5},{5,4},{6,7},{7,6},{8,9},{9,8},{10,11... | collective-permute-start | bytes 786440 | tf_op jit(solution)/shard_map/ppermute | solution.py:315
  28.0 7.7 %collective-permute-start.10 = (bf16[64,512]{1,0:T(8,128)(2,1)S(1)}, bf16[64,512]{1,0:T(8,128)(2,1)S(1)}, u32[]{:S(2)}, u32[]{:S(2)}) collective-permute-start(bf16[64,512]{1,0:T(8,128)(2,1)S(1)} %get-tuple-element.159), channel_id=1, source_target_pairs={{0,8},{1,9},{2,10},{3,11},{4,12},{5,13},{6,14},{7,15},{8,0},{9,1},... | collective-permute-start | bytes 196616 | tf_op jit(solution)/shard_map/ppermute | solution.py:315
  30.7 6.6 %collective-permute-start.11 = (bf16[64,512]{1,0:T(8,128)(2,1)S(1)}, bf16[64,512]{1,0:T(8,128)(2,1)S(1)}, u32[]{:S(2)}, u32[]{:S(2)}) collective-permute-start(bf16[64,512]{1,0:T(8,128)(2,1)S(1)} %get-tuple-element.160), channel_id=1, source_target_pairs={{0,12},{1,13},{2,14},{3,15},{4,8},{5,9},{6,10},{7,11},{8,4},{9,5},... | collective-permute-start | bytes 196616 | tf_op jit(solution)/shard_map/ppermute | solution.py:315
  32.3 5.2 %collective-permute-start.12 = (bf16[64,512]{1,0:T(8,128)(2,1)S(1)}, bf16[64,512]{1,0:T(8,128)(2,1)S(1)}, u32[]{:S(2)}, u32[]{:S(2)}) collective-permute-start(bf16[64,512]{1,0:T(8,128)(2,1)S(1)} %get-tuple-element.161), channel_id=1, source_target_pairs={{0,4},{1,5},{2,6},{3,7},{4,0},{5,1},{6,2},{7,3},{8,12},{9,13},{10,... | collective-permute-start | bytes 196616 | tf_op jit(solution)/shard_map/ppermute | solution.py:315
  38.1 6.5 %collective-permute-start.13 = (bf16[64,512]{1,0:T(8,128)(2,1)S(1)}, bf16[64,512]{1,0:T(8,128)(2,1)S(1)}, u32[]{:S(2)}, u32[]{:S(2)}) collective-permute-start(bf16[64,512]{1,0:T(8,128)(2,1)S(1)} %shard_map.193.refs_0_.coarse_ref.nodes_ref), channel_id=1, source_target_pairs={{0,12},{1,13},{2,14},{3,15},{4,8},{5,9},{6,10},{7,11},{8,4},{9,5},... | collective-permute-start | bytes 196616 | tf_op jit(solution)/shard_map/ppermute | solution.py:315
  41.6 4.3 %collective-permute-start.14 = (bf16[64,512]{1,0:T(8,128)(2,1)S(1)}, bf16[64,512]{1,0:T(8,128)(2,1)S(1)}, u32[]{:S(2)}, u32[]{:S(2)}) collective-permute-start(bf16[64,512]{1,0:T(8,128)(2,1)S(1)} %shard_map.193.refs_0_.coarse_ref.nodes_ref), channel_id=1, source_target_pairs={{0,4},{1,5},{2,6},{3,7},{4,0},{5,1},{6,2},{7,3},{8,12},{9,13},{10,... | collective-permute-start | bytes 196616 | tf_op jit(solution)/shard_map/ppermute | solution.py:315
  45.9 4.3 %collective-permute-start.16 = (bf16[64,512]{1,0:T(8,128)(2,1)S(1)}, bf16[64,512]{1,0:T(8,128)(2,1)S(1)}, u32[]{:S(2)}, u32[]{:S(2)}) collective-permute-start(bf16[64,512]{1,0:T(8,128)(2,1)S(1)} %collective-permute-done.13), channel_id=1, source_target_pairs={{0,4},{1,5},{2,6},{3,7},{4,0},{5,1},{6,2},{7,3},{8,12},{9,13},{10,... | collective-permute-start | bytes 196616 | tf_op jit(solution)/shard_map/ppermute | solution.py:315
  47.0 5.7 %collective-permute-start.15 = (bf16[192,512]{1,0:T(8,128)(2,1)S(1)}, bf16[192,512]{1,0:T(8,128)(2,1)S(1)}, u32[]{:S(2)}, u32[]{:S(2)}) collective-permute-start(bf16[192,512]{1,0:T(8,128)(2,1)S(1)} %pad_maximum_fusion.2), channel_id=1, source_target_pairs={{0,2},{1,3},{2,0},{3,1},{4,6},{5,7},{6,4},{7,5},{8,10},{9,11},{10,... | collective-permute-start | bytes 589832 | tf_op jit(solution)/shard_map/ppermute | solution.py:315
  50.2 2.5 %collective-permute-start.18 = (bf16[256,512]{1,0:T(8,128)(2,1)S(1)}, bf16[256,512]{1,0:T(8,128)(2,1)S(1)}, u32[]{:S(2)}, u32[]{:S(2)}) collective-permute-start(bf16[256,512]{1,0:T(8,128)(2,1)S(1)} %pad_maximum_fusion.refs_4_.straight_ref), channel_id=1, source_target_pairs={{0,1},{1,0},{2,3},{3,2},{4,5},{5,4},{6,7},{7,6},{8,9},{9,8},{10,11... | collective-permute-start | bytes 786440 | tf_op jit(solution)/shard_map/ppermute | solution.py:315
  50.3 4.5 %collective-permute-start.17 = (bf16[64,512]{1,0:T(8,128)(2,1)S(1)}, bf16[64,512]{1,0:T(8,128)(2,1)S(1)}, u32[]{:S(2)}, u32[]{:S(2)}) collective-permute-start(bf16[64,512]{1,0:T(8,128)(2,1)S(1)} %collective-permute-done.16), channel_id=1, source_target_pairs={{0,2},{1,3},{2,0},{3,1},{4,6},{5,7},{6,4},{7,5},{8,10},{9,11},{10,... | collective-permute-start | bytes 196616 | tf_op jit(solution)/shard_map/ppermute | solution.py:315
  58.4 5.4 %collective-permute-start.20 = (bf16[160,512]{1,0:T(8,128)(2,1)S(1)}, bf16[160,512]{1,0:T(8,128)(2,1)S(1)}, u32[]{:S(2)}, u32[]{:S(2)}) collective-permute-start(bf16[160,512]{1,0:T(8,128)(2,1)S(1)} %get-tuple-element.195), channel_id=1, source_target_pairs={{0,1},{1,0},{2,3},{3,2},{4,5},{5,4},{6,7},{7,6},{8,9},{9,8},{10,11... | collective-permute-start | bytes 491528 | tf_op jit(solution)/shard_map/ppermute | solution.py:315
  58.6 11.1 %collective-permute-start.24 = (bf16[160,512]{1,0:T(8,128)(2,1)S(1)}, bf16[160,512]{1,0:T(8,128)(2,1)S(1)}, u32[]{:S(2)}, u32[]{:S(2)}) collective-permute-start(bf16[160,512]{1,0:T(8,128)(2,1)S(1)} %get-tuple-element.204), channel_id=1, source_target_pairs={{0,2},{1,3},{2,0},{3,1},{4,6},{5,7},{6,4},{7,5},{8,10},{9,11},{10,... | collective-permute-start | bytes 491528 | tf_op jit(solution)/shard_map/ppermute | solution.py:315
  59.1 10.5 %collective-permute-start.25 = (bf16[160,512]{1,0:T(8,128)(2,1)S(1)}, bf16[160,512]{1,0:T(8,128)(2,1)S(1)}, u32[]{:S(2)}, u32[]{:S(2)}) collective-permute-start(bf16[160,512]{1,0:T(8,128)(2,1)S(1)} %get-tuple-element.205), channel_id=1, source_target_pairs={{0,3},{1,2},{2,1},{3,0},{4,7},{5,6},{6,5},{7,4},{8,11},{9,10},{10,... | collective-permute-start | bytes 491528 | tf_op jit(solution)/shard_map/ppermute | solution.py:315
  60.3 8.6 %collective-permute-start.21 = (bf16[64,512]{1,0:T(8,128)(2,1)S(1)}, bf16[64,512]{1,0:T(8,128)(2,1)S(1)}, u32[]{:S(2)}, u32[]{:S(2)}) collective-permute-start(bf16[64,512]{1,0:T(8,128)(2,1)S(1)} %get-tuple-element.198), channel_id=1, source_target_pairs={{0,8},{1,9},{2,10},{3,11},{4,12},{5,13},{6,14},{7,15},{8,0},{9,1},... | collective-permute-start | bytes 196616 | tf_op jit(solution)/shard_map/ppermute | solution.py:315
  61.3 7.6 %collective-permute-start.22 = (bf16[64,512]{1,0:T(8,128)(2,1)S(1)}, bf16[64,512]{1,0:T(8,128)(2,1)S(1)}, u32[]{:S(2)}, u32[]{:S(2)}) collective-permute-start(bf16[64,512]{1,0:T(8,128)(2,1)S(1)} %get-tuple-element.199), channel_id=1, source_target_pairs={{0,12},{1,13},{2,14},{3,15},{4,8},{5,9},{6,10},{7,11},{8,4},{9,5},... | collective-permute-start | bytes 196616 | tf_op jit(solution)/shard_map/ppermute | solution.py:315
  63.7 5.9 %collective-permute-start.23 = (bf16[64,512]{1,0:T(8,128)(2,1)S(1)}, bf16[64,512]{1,0:T(8,128)(2,1)S(1)}, u32[]{:S(2)}, u32[]{:S(2)}) collective-permute-start(bf16[64,512]{1,0:T(8,128)(2,1)S(1)} %get-tuple-element.200), channel_id=1, source_target_pairs={{0,4},{1,5},{2,6},{3,7},{4,0},{5,1},{6,2},{7,3},{8,12},{9,13},{10,... | collective-permute-start | bytes 196616 | tf_op jit(solution)/shard_map/ppermute | solution.py:315
  (2 other events, 3.3 us)

commit v7 on v6

--- a/solution.py
+++ b/solution.py
@@ -76,9 +76,9 @@
     member = r_q ^ own_q
     s_rel = s_patch ^ (own_z * PLANE + r_q)
     s_z = lax.shift_right_logical(s_rel, bits(PLANE))
-    s_block = (s_rel & (PLANE - 1)) * lines + (s_z ^ lax.shift_right_logical(s_z, 1))
+    s_block = (s_rel & (PLANE - 1)) * lines + s_z
     r_z = lax.shift_right_logical(r_patch, bits(PLANE)) ^ own_z
-    r_block = (r_z ^ lax.shift_right_logical(r_z, 1)) + 1
+    r_block = r_z + 1
     flags = jnp.where(lax.broadcasted_iota(I32, (8, count), 0) == member, 1.0, 0.0)
     before = jnp.where(
         lax.broadcasted_iota(I32, (count, count), 0) < lax.broadcasted_iota(I32, (count, count), 1),
@@ -307,9 +307,6 @@
     layers = edge_in.shape[0]
     limit = (24 if lines <= 4 else 56) * 2**20
     shape = jax.ShapeDtypeStruct
-    place = [0] * lines
-    for z in range(lines):
-        place[z ^ (z >> 1)] = z
 
     def swap(values, distance):
         return lax.ppermute(values, "patch", [(i, i ^ distance) for i in range(devices)])
@@ -369,24 +366,24 @@
 
         done = local_part(pieces[0], share=min(l, 1))
         if lines == 4:
-            z3, z1 = swap(coarse, 12), swap(coarse, 4)
+            z2, z1 = swap(coarse, 8), swap(coarse, 4)
             if l:
-                z3, z1, done = tied((z3, z1, done))
+                z2, z1, done = tied((z2, z1, done))
             else:
-                z3, z1, done, slots = tied((z3, z1, done, slots))
-            near = jnp.concatenate([coarse, z1, z3], axis=0)
-            z2 = swap(z3, 4)
+                z2, z1, done, slots = tied((z2, z1, done, slots))
+            near = jnp.concatenate([coarse, z1, z2], axis=0)
+            far_end = swap(z2, 4)
             across = swap(near, 2)
         else:
-            near = [coarse if z == 0 else swap(coarse, PLANE * z) for z in place]
-            near, z2 = jnp.concatenate(near[:-1], axis=0), near[-1]
+            near = [coarse] + [swap(coarse, PLANE * z) for z in range(1, lines)]
+            near, far_end = jnp.concatenate(near[:-1], axis=0), near[-1]
             across = swap(near, 2)
         if not last:
-            z2, done = tied((z2, done))
+            far_end, done = tied((far_end, done))
             for rows in pieces[1:]:
                 done = local_part(rows, done)
-        late = swap(z2, 2)
-        table = jnp.concatenate([near, z2], axis=0)
+        late = swap(far_end, 2)
+        table = jnp.concatenate([near, far_end], axis=0)
         tables = [table, swap(table, 1)]
         pre_act, early, *found = call(
             functools.partial(far_ready_kernel, lines, slot),
@@ -429,7 +426,7 @@
             for rows in pieces[1:]:
                 done = local_part(rows, done)
         local, sums = done
-        far_parts = [swap(parts[i], PLANE * place[i]) for i in range(lines - 1, 0, -1)]
+        far_parts = [swap(parts[z], PLANE * z) for z in [*range(2, lines), 1]]
         parts = [parts[0], *far_parts]
         if l == 0:
             sources = [node_in, node_out, node_bias, node_gain, node_shift]

time: 71.4 us -> 71 us (level)
  transfers between devices with their start and end apart: 26 -> 26, of which waited for: 13 -> 12; matrix products, arithmetic and copies ran while one was open for 0% -> 0% of each run, Pallas kernels for 30% -> 30%
where the time goes in v7:
time: 71 us; the launch traced here: 70.8 us
  Pallas kernels  28.6 us (40%)
  starting transfers between devices  27.4 us (39%)
  waiting for transfers between devices  13.7 us (19%)
  between operations  1.06 us (1%)
    pallas_call x17, Pallas kernels, call(): pl.pallas_call(kernel, out_shape=outs, in_specs=specs, out_specs=[pl.Bloc...  28.6 us
    ppermute x26, starting transfers between devices, swap(): lax.ppermute(values, 'patch', [(i, i ^ distance) for i in range(devices)])  27.4 us
    ppermute x26, waiting for transfers between devices, swap(): lax.ppermute(values, 'patch', [(i, i ^ distance) for i in range(devices)])  13.7 us
  transfers between devices with their start and end apart: 26, of which 12 were waited for; matrix products, arithmetic and copies ran while one was open for 0% of the time, Pallas kernels for 30%

profile of v7, /device:TPU:0, one launch (start us, length us, event | category | flops | bytes accessed | tf_op | source)
XLA Modules:
  0.0 70.8 jit_solution(6635236424346627503)
XLA Ops:
  0.6 1.5 %shard_map.184 = (s32[1,256]{1,0:T(1,128)S(1)}, bf16[64,512]{1,0:T(8,128)(2,1)S(1)}, bf16[192,512]{1,0:T(8,128)(2,1)S(1)}, bf16[176,512]{1,0:T(8,128)(2,1)S(1)},...) custom-call(s32[1]{0:T(128)} %bitcast.own_ref, s32[1,256]{1,0:T(1,128)} %bitcast.3, ...), custom_call_target="tpu_custom_call" | custom-call | flops 167772160 | bytes 1510404 | tf_op jit(solution)/shard_map/pallas_call | solution.py:271
  2.7 2.6 %collective-permute-start.3 = (bf16[176,512]{1,0:T(8,128)(2,1)S(1)}, bf16[176,512]{1,0:T(8,128)(2,1)S(1)}, u32[]{:S(2)}, u32[]{:S(2)}) collective-permute-start(bf16[176,512]{1,0:T(8,128)(2,1)S(1)} %get-tuple-element.120), channel_id=1, source_target_pairs={{0,2},{1,3},{2,0},{3,1},{4,6},{5,7},{6,4},{7,5},{8,10},{9,11},{10,... | collective-permute-start | bytes 540680 | tf_op jit(solution)/shard_map/ppermute | solution.py:312
  5.3 2.8 %collective-permute-start = (bf16[64,512]{1,0:T(8,128)(2,1)S(1)}, bf16[64,512]{1,0:T(8,128)(2,1)S(1)}, u32[]{:S(2)}, u32[]{:S(2)}) collective-permute-start(bf16[64,512]{1,0:T(8,128)(2,1)S(1)} %get-tuple-element.106.refs_0_.coarse_ref.nodes_ref), channel_id=1, source_target_pairs={{0,8},{1,9},{2,10},{3,11},{4,12},{5,13},{6,14},{7,15},{8,0},{9,1},... | collective-permute-start | bytes 196616 | tf_op jit(solution)/shard_map/ppermute | solution.py:312
  8.2 1.6 %collective-permute-start.1 = (bf16[64,512]{1,0:T(8,128)(2,1)S(1)}, bf16[64,512]{1,0:T(8,128)(2,1)S(1)}, u32[]{:S(2)}, u32[]{:S(2)}) collective-permute-start(bf16[64,512]{1,0:T(8,128)(2,1)S(1)} %get-tuple-element.106.refs_0_.coarse_ref.nodes_ref), channel_id=1, source_target_pairs={{0,4},{1,5},{2,6},{3,7},{4,0},{5,1},{6,2},{7,3},{8,12},{9,13},{10,... | collective-permute-start | bytes 196616 | tf_op jit(solution)/shard_map/ppermute | solution.py:312
  9.7 1.9 %shard_map.185 = (bf16[768,512]{1,0:T(8,128)(2,1)S(1)}, s32[768]{0:T(1024)S(1)}, s32[768]{0:T(1024)S(1)}, f32[2,512]{1,0:T(2,128)S(1)}, f32[2,512]{1,0:T(2,128)S...) custom-call(bf16[768,512]{1,0:T(8,128)(2,1)} %refs_0_.1, s32[768]{0:T(1024)} %refs_1_.1, ...), custom_call_target="tpu_custom_call" | custom-call | bytes 7901184 | tf_op jit(solution)/shard_map/pallas_call | solution.py:271
  11.7 2.7 %shard_map.186 = (bf16[512,512]{1,0:T(8,128)(2,1)S(1)}, f32[256,512]{1,0:T(8,128)S(1)}) custom-call(bf16[64,512]{1,0:T(8,128)(2,1)S(1)} %get-tuple-element.106.refs_0_.coarse_ref.nodes_ref, bf16[192,512]{1,0:T(8,128)(2,1)S(1)} %get-tuple-element.107.refs_1_.nodes_ref, bf16[768,512]{1,0:T(8,128)(2,1)S(1)} %get-tuple-element.108.refs_2_, ...), custom_call_target="tpu_custom_call" | custom-call | tf_op jit(solution)/shard_map/pallas_call | solution.py:271
  15.7 1.5 %collective-permute-start.8 = (bf16[192,512]{1,0:T(8,128)(2,1)S(1)}, bf16[192,512]{1,0:T(8,128)(2,1)S(1)}, u32[]{:S(2)}, u32[]{:S(2)}) collective-permute-start(bf16[192,512]{1,0:T(8,128)(2,1)S(1)} %pad_maximum_fusion.1), channel_id=1, source_target_pairs={{0,2},{1,3},{2,0},{3,1},{4,6},{5,7},{6,4},{7,5},{8,10},{9,11},{10,... | collective-permute-start | bytes 589832 | tf_op jit(solution)/shard_map/ppermute | solution.py:312
  17.3 1.5 %collective-permute-done.5 = bf16[64,512]{1,0:T(8,128)(2,1)S(1)} collective-permute-done((bf16[64,512]{1,0:T(8,128)(2,1)S(1)}, bf16[64,512]{1,0:T(8,128)(2,1)S(1)}, u32[]{:S(2)}, u32[]{:S(2)}) %collective-permute-start.5) | collective-permute-done | bytes 65568 | tf_op jit(solution)/shard_map/ppermute | solution.py:312
  18.7 1.5 %collective-permute-start.6 = (bf16[64,512]{1,0:T(8,128)(2,1)S(1)}, bf16[64,512]{1,0:T(8,128)(2,1)S(1)}, u32[]{:S(2)}, u32[]{:S(2)}) collective-permute-start(bf16[64,512]{1,0:T(8,128)(2,1)S(1)} %collective-permute-done.5), channel_id=1, source_target_pairs={{0,2},{1,3},{2,0},{3,1},{4,6},{5,7},{6,4},{7,5},{8,10},{9,11},{10,... | collective-permute-start | bytes 196616 | tf_op jit(solution)/shard_map/ppermute | solution.py:312
  20.2 1.7 %shard_map.189 = (bf16[768,512]{1,0:T(8,128)(2,1)S(1)}, f32[256,512]{1,0:T(8,128)S(1)}) custom-call(bf16[64,512]{1,0:T(8,128)(2,1)S(1)} %get-tuple-element.106.refs_0_.coarse_ref.nodes_ref, bf16[192,512]{1,0:T(8,128)(2,1)S(1)} %get-tuple-element.107.refs_1_.nodes_ref, bf16[768,512]{1,0:T(8,128)(2,1)S(1)} %get-tuple-element.108.refs_2_, ...), custom_call_target="tpu_custom_call" | custom-call | flops 738197504 | bytes 5523456 | tf_op jit(solution)/shard_map/pallas_call | solution.py:271
  21.9 1.8 %shard_map.187 = (f32[640,512]{1,0:T(8,128)S(1)}, bf16[640,512]{1,0:T(8,128)(2,1)S(1)}, bf16[640,512]{1,0:T(8,128)(2,1)S(1)}, bf16[256,640]{1,0:T(8,128)(2,1)S(1)}) custom-call(bf16[176,512]{1,0:T(8,128)(2,1)S(1)} %get-tuple-element.127.refs_0_.refs_10_, bf16[176,512]{1,0:T(8,128)(2,1)S(1)} %collective-permute-done.2.refs_1_.refs_11_, ...), custom_call_target="tpu_custom_call" | custom-call | flops 838860800 | bytes 5505024 | tf_op jit(solution)/shard_map/pallas_call | solution.py:271
  26.4 2.0 %shard_map.192 = (bf16[176,512]{1,0:T(8,128)(2,1)S(1)}, bf16[176,512]{1,0:T(8,128)(2,1)S(1)}, bf16[176,512]{1,0:T(8,128)(2,1)S(1)}, bf16[176,512]{1,0:T(8,128)(2...) custom-call(bf16[256,512]{1,0:T(8,128)(2,1)S(1)} %constant_dynamic-u, ...), custom_call_target="tpu_custom_call" | custom-call | flops 1174405120 | bytes 6696960 | tf_op jit(solution)/shard_map/pallas_call | solution.py:271
  28.4 2.3 %collective-permute-start.10 = (bf16[64,512]{1,0:T(8,128)(2,1)S(1)}, bf16[64,512]{1,0:T(8,128)(2,1)S(1)}, u32[]{:S(2)}, u32[]{:S(2)}) collective-permute-start(bf16[64,512]{1,0:T(8,128)(2,1)S(1)} %get-tuple-element.159), channel_id=1, source_target_pairs={{0,8},{1,9},{2,10},{3,11},{4,12},{5,13},{6,14},{7,15},{8,0},{9,1},... | collective-permute-start | bytes 196616 | tf_op jit(solution)/shard_map/ppermute | solution.py:312
  32.3 2.6 %shard_map.190 = (bf16[2,1024,512]{2,1,0:T(8,128)(2,1)S(1)}, bf16[2,512,512]{2,1,0:T(8,128)(2,1)S(1)}, f32[2,512]{1,0:T(2,128)S(1)}, f32[2,512]{1,0:T(2,128)S(1)...) custom-call(bf16[2,1024,512]{2,1,0:T(8,128)(2,1)} %refs_0_.2, ...), custom_call_target="tpu_custom_call" | custom-call | bytes 12607488 | tf_op jit(solution)/shard_map/pallas_call | solution.py:271
  38.5 2.4 %collective-permute-start.13 = (bf16[64,512]{1,0:T(8,128)(2,1)S(1)}, bf16[64,512]{1,0:T(8,128)(2,1)S(1)}, u32[]{:S(2)}, u32[]{:S(2)}) collective-permute-start(bf16[64,512]{1,0:T(8,128)(2,1)S(1)} %shard_map.193.refs_0_.coarse_ref.nodes_ref), channel_id=1, source_target_pairs={{0,8},{1,9},{2,10},{3,11},{4,12},{5,13},{6,14},{7,15},{8,0},{9,1},... | collective-permute-start | bytes 196616 | tf_op jit(solution)/shard_map/ppermute | solution.py:312
  42.1 2.6 %shard_map.194 = (bf16[512,512]{1,0:T(8,128)(2,1)S(1)}, f32[256,512]{1,0:T(8,128)S(1)}) custom-call(bf16[64,512]{1,0:T(8,128)(2,1)S(1)} %shard_map.193.refs_0_.coarse_ref.nodes_ref, bf16[192,512]{1,0:T(8,128)(2,1)S(1)} %get-tuple-element.162.refs_1_.nodes_ref, bf16[768,512]{1,0:T(8,128)(2,1)S(1)} %get-tuple-element.163.refs_2_, ...), custom_call_target="tpu_custom_call" | custom-call | flops 1476395008 | bytes 4212736 | tf_op jit(solution)/shard_map/pallas_call | solution.py:271
  46.9 2.8 %collective-permute-done.16 = bf16[64,512]{1,0:T(8,128)(2,1)S(1)} collective-permute-done((bf16[64,512]{1,0:T(8,128)(2,1)S(1)}, bf16[64,512]{1,0:T(8,128)(2,1)S(1)}, u32[]{:S(2)}, u32[]{:S(2)}) %collective-permute-start.16) | collective-permute-done | bytes 65568 | tf_op jit(solution)/shard_map/ppermute | solution.py:312
  50.2 1.8 %shard_map.195 = (f32[640,512]{1,0:T(8,128)S(1)}, bf16[640,512]{1,0:T(8,128)(2,1)S(1)}, bf16[640,512]{1,0:T(8,128)(2,1)S(1)}, bf16[256,640]{1,0:T(8,128)(2,1)S(1)}) custom-call(bf16[176,512]{1,0:T(8,128)(2,1)S(1)} %get-tuple-element.170.refs_0_.refs_10_, bf16[176,512]{1,0:T(8,128)(2,1)S(1)} %get-tuple-element.171.refs_1_.refs_11_, ...), custom_call_target="tpu_custom_call" | custom-call | flops 838860800 | bytes 5505024 | tf_op jit(solution)/shard_map/pallas_call | solution.py:271
  54.3 1.5 %collective-permute-done.19.refs_1_ = bf16[256,512]{1,0:T(8,128)(2,1)S(1)} collective-permute-done((bf16[256,512]{1,0:T(8,128)(2,1)S(1)}, bf16[256,512]{1,0:T(8,128)(2,1)S(1)}, u32[]{:S(2)}, u32[]{:S(2)}) %collective-permute-start.19) | collective-permute-done | bytes 262176 | tf_op jit(solution)/shard_map/ppermute | solution.py:312
  55.8 2.0 %shard_map.197 = (bf16[160,512]{1,0:T(8,128)(2,1)S(1)}, bf16[160,512]{1,0:T(8,128)(2,1)S(1)}, bf16[160,512]{1,0:T(8,128)(2,1)S(1)}, bf16[160,512]{1,0:T(8,128)(2...) custom-call(bf16[256,512]{1,0:T(8,128)(2,1)S(1)} %constant_dynamic-u, ...), custom_call_target="tpu_custom_call" | custom-call | flops 1174405120 | bytes 6631424 | tf_op jit(solution)/shard_map/pallas_call | solution.py:271
  60.9 2.2 %collective-permute-start.22 = (bf16[64,512]{1,0:T(8,128)(2,1)S(1)}, bf16[64,512]{1,0:T(8,128)(2,1)S(1)}, u32[]{:S(2)}, u32[]{:S(2)}) collective-permute-start(bf16[64,512]{1,0:T(8,128)(2,1)S(1)} %get-tuple-element.199), channel_id=1, source_target_pairs={{0,12},{1,13},{2,14},{3,15},{4,8},{5,9},{6,10},{7,11},{8,4},{9,5},... | collective-permute-start | bytes 196616 | tf_op jit(solution)/shard_map/ppermute | solution.py:312
  63.3 2.5 %shard_map.198 = (bf16[768,512]{1,0:T(8,128)(2,1)}, f32[256,512]{1,0:T(8,128)S(1)}) custom-call(bf16[64,512]{1,0:T(8,128)(2,1)S(1)} %shard_map.193.refs_0_.coarse_ref.nodes_ref, bf16[192,512]{1,0:T(8,128)(2,1)S(1)} %get-tuple-element.162.refs_1_.nodes_ref, bf16[768,512]{1,0:T(8,128)(2,1)S(1)} %get-tuple-element.163.refs_2_, ...), custom_call_target="tpu_custom_call" | custom-call | flops 738197504 | bytes 5523456 | tf_op jit(solution)/shard_map/pallas_call | solution.py:271
  66.6 1.8 %collective-permute-done.21.refs_1_ = bf16[64,512]{1,0:T(8,128)(2,1)S(1)} collective-permute-done((bf16[64,512]{1,0:T(8,128)(2,1)S(1)}, bf16[64,512]{1,0:T(8,128)(2,1)S(1)}, u32[]{:S(2)}, u32[]{:S(2)}) %collective-permute-start.21) | collective-permute-done | bytes 65568 | tf_op jit(solution)/shard_map/ppermute | solution.py:312
  69.3 1.4 %shard_map.200 = (bf16[256,512]{1,0:T(8,128)(2,1)}, bf16[256,512]{1,0:T(8,128)(2,1)}) custom-call(bf16[64,512]{1,0:T(8,128)(2,1)S(1)} %shard_map.193.refs_0_.coarse_ref.nodes_ref, f32[64,512]{1,0:T(8,128)S(1)} %get-tuple-element.196.pre_ref, f32[256,512]{1,0:T(8,128)S(1)} %get-tuple-element.192.sum_ref, f32[64,512]{1,0:T(8,128)S(1)} %get-tuple-element.197.refs_0_, ...), custom_call_target="tpu_custom_call" | custom-call | flops 100663296 | bytes 5681152 | tf_op jit(solution)/shard_map/pallas_call | solution.py:271
  (56 shorter events, 20.9 us)
Async XLA Ops:
  2.2 12.2 %collective-permute-start.2 = (bf16[176,512]{1,0:T(8,128)(2,1)S(1)}, bf16[176,512]{1,0:T(8,128)(2,1)S(1)}, u32[]{:S(2)}, u32[]{:S(2)}) collective-permute-start(bf16[176,512]{1,0:T(8,128)(2,1)S(1)} %get-tuple-element.119), channel_id=1, source_target_pairs={{0,1},{1,0},{2,3},{3,2},{4,5},{5,4},{6,7},{7,6},{8,9},{9,8},{10,11... | collective-permute-start | bytes 540680 | tf_op jit(solution)/shard_map/ppermute | solution.py:312
  2.7 11.7 %collective-permute-start.3 = (bf16[176,512]{1,0:T(8,128)(2,1)S(1)}, bf16[176,512]{1,0:T(8,128)(2,1)S(1)}, u32[]{:S(2)}, u32[]{:S(2)}) collective-permute-start(bf16[176,512]{1,0:T(8,128)(2,1)S(1)} %get-tuple-element.120), channel_id=1, source_target_pairs={{0,2},{1,3},{2,0},{3,1},{4,6},{5,7},{6,4},{7,5},{8,10},{9,11},{10,... | collective-permute-start | bytes 540680 | tf_op jit(solution)/shard_map/ppermute | solution.py:312
  5.3 9.1 %collective-permute-start.4 = (bf16[176,512]{1,0:T(8,128)(2,1)S(1)}, bf16[176,512]{1,0:T(8,128)(2,1)S(1)}, u32[]{:S(2)}, u32[]{:S(2)}) collective-permute-start(bf16[176,512]{1,0:T(8,128)(2,1)S(1)} %get-tuple-element.121), channel_id=1, source_target_pairs={{0,3},{1,2},{2,1},{3,0},{4,7},{5,6},{6,5},{7,4},{8,11},{9,10},{10,... | collective-permute-start | bytes 540680 | tf_op jit(solution)/shard_map/ppermute | solution.py:312
  5.3 9.0 %collective-permute-start = (bf16[64,512]{1,0:T(8,128)(2,1)S(1)}, bf16[64,512]{1,0:T(8,128)(2,1)S(1)}, u32[]{:S(2)}, u32[]{:S(2)}) collective-permute-start(bf16[64,512]{1,0:T(8,128)(2,1)S(1)} %get-tuple-element.106.refs_0_.coarse_ref.nodes_ref), channel_id=1, source_target_pairs={{0,8},{1,9},{2,10},{3,11},{4,12},{5,13},{6,14},{7,15},{8,0},{9,1},... | collective-permute-start | bytes 196616 | tf_op jit(solution)/shard_map/ppermute | solution.py:312
  8.2 6.2 %collective-permute-start.1 = (bf16[64,512]{1,0:T(8,128)(2,1)S(1)}, bf16[64,512]{1,0:T(8,128)(2,1)S(1)}, u32[]{:S(2)}, u32[]{:S(2)}) collective-permute-start(bf16[64,512]{1,0:T(8,128)(2,1)S(1)} %get-tuple-element.106.refs_0_.coarse_ref.nodes_ref), channel_id=1, source_target_pairs={{0,4},{1,5},{2,6},{3,7},{4,0},{5,1},{6,2},{7,3},{8,12},{9,13},{10,... | collective-permute-start | bytes 196616 | tf_op jit(solution)/shard_map/ppermute | solution.py:312
  14.4 4.3 %collective-permute-start.5 = (bf16[64,512]{1,0:T(8,128)(2,1)S(1)}, bf16[64,512]{1,0:T(8,128)(2,1)S(1)}, u32[]{:S(2)}, u32[]{:S(2)}) collective-permute-start(bf16[64,512]{1,0:T(8,128)(2,1)S(1)} %collective-permute-done), channel_id=1, source_target_pairs={{0,4},{1,5},{2,6},{3,7},{4,0},{5,1},{6,2},{7,3},{8,12},{9,13},{10,... | collective-permute-start | bytes 196616 | tf_op jit(solution)/shard_map/ppermute | solution.py:312
  15.7 8.0 %collective-permute-start.8 = (bf16[192,512]{1,0:T(8,128)(2,1)S(1)}, bf16[192,512]{1,0:T(8,128)(2,1)S(1)}, u32[]{:S(2)}, u32[]{:S(2)}) collective-permute-start(bf16[192,512]{1,0:T(8,128)(2,1)S(1)} %pad_maximum_fusion.1), channel_id=1, source_target_pairs={{0,2},{1,3},{2,0},{3,1},{4,6},{5,7},{6,4},{7,5},{8,10},{9,11},{10,... | collective-permute-start | bytes 589832 | tf_op jit(solution)/shard_map/ppermute | solution.py:312
  18.7 5.9 %collective-permute-start.6 = (bf16[64,512]{1,0:T(8,128)(2,1)S(1)}, bf16[64,512]{1,0:T(8,128)(2,1)S(1)}, u32[]{:S(2)}, u32[]{:S(2)}) collective-permute-start(bf16[64,512]{1,0:T(8,128)(2,1)S(1)} %collective-permute-done.5), channel_id=1, source_target_pairs={{0,2},{1,3},{2,0},{3,1},{4,6},{5,7},{6,4},{7,5},{8,10},{9,11},{10,... | collective-permute-start | bytes 196616 | tf_op jit(solution)/shard_map/ppermute | solution.py:312
  20.2 3.5 %collective-permute-start.7 = (bf16[256,512]{1,0:T(8,128)(2,1)S(1)}, bf16[256,512]{1,0:T(8,128)(2,1)S(1)}, u32[]{:S(2)}, u32[]{:S(2)}) collective-permute-start(bf16[256,512]{1,0:T(8,128)(2,1)S(1)} %constant_dynamic-update-slice_fusion.refs_4_.straight_ref), channel_id=1, source_target_pairs={{0,1},{1,0},{2,3},{3,2},{4,5},{5,4},{6,7},{7,6},{8,9},{9,8},{10,11... | collective-permute-start | bytes 786440 | tf_op jit(solution)/shard_map/ppermute | solution.py:312
  28.4 8.3 %collective-permute-start.10 = (bf16[64,512]{1,0:T(8,128)(2,1)S(1)}, bf16[64,512]{1,0:T(8,128)(2,1)S(1)}, u32[]{:S(2)}, u32[]{:S(2)}) collective-permute-start(bf16[64,512]{1,0:T(8,128)(2,1)S(1)} %get-tuple-element.159), channel_id=1, source_target_pairs={{0,8},{1,9},{2,10},{3,11},{4,12},{5,13},{6,14},{7,15},{8,0},{9,1},... | collective-permute-start | bytes 196616 | tf_op jit(solution)/shard_map/ppermute | solution.py:312
  30.7 6.6 %collective-permute-start.11 = (bf16[64,512]{1,0:T(8,128)(2,1)S(1)}, bf16[64,512]{1,0:T(8,128)(2,1)S(1)}, u32[]{:S(2)}, u32[]{:S(2)}) collective-permute-start(bf16[64,512]{1,0:T(8,128)(2,1)S(1)} %get-tuple-element.160), channel_id=1, source_target_pairs={{0,12},{1,13},{2,14},{3,15},{4,8},{5,9},{6,10},{7,11},{8,4},{9,5},... | collective-permute-start | bytes 196616 | tf_op jit(solution)/shard_map/ppermute | solution.py:312
  32.1 5.9 %collective-permute-start.12 = (bf16[64,512]{1,0:T(8,128)(2,1)S(1)}, bf16[64,512]{1,0:T(8,128)(2,1)S(1)}, u32[]{:S(2)}, u32[]{:S(2)}) collective-permute-start(bf16[64,512]{1,0:T(8,128)(2,1)S(1)} %get-tuple-element.161), channel_id=1, source_target_pairs={{0,4},{1,5},{2,6},{3,7},{4,0},{5,1},{6,2},{7,3},{8,12},{9,13},{10,... | collective-permute-start | bytes 196616 | tf_op jit(solution)/shard_map/ppermute | solution.py:312
  38.5 6.2 %collective-permute-start.13 = (bf16[64,512]{1,0:T(8,128)(2,1)S(1)}, bf16[64,512]{1,0:T(8,128)(2,1)S(1)}, u32[]{:S(2)}, u32[]{:S(2)}) collective-permute-start(bf16[64,512]{1,0:T(8,128)(2,1)S(1)} %shard_map.193.refs_0_.coarse_ref.nodes_ref), channel_id=1, source_target_pairs={{0,8},{1,9},{2,10},{3,11},{4,12},{5,13},{6,14},{7,15},{8,0},{9,1},... | collective-permute-start | bytes 196616 | tf_op jit(solution)/shard_map/ppermute | solution.py:312
  40.9 4.5 %collective-permute-start.14 = (bf16[64,512]{1,0:T(8,128)(2,1)S(1)}, bf16[64,512]{1,0:T(8,128)(2,1)S(1)}, u32[]{:S(2)}, u32[]{:S(2)}) collective-permute-start(bf16[64,512]{1,0:T(8,128)(2,1)S(1)} %shard_map.193.refs_0_.coarse_ref.nodes_ref), channel_id=1, source_target_pairs={{0,4},{1,5},{2,6},{3,7},{4,0},{5,1},{6,2},{7,3},{8,12},{9,13},{10,... | collective-permute-start | bytes 196616 | tf_op jit(solution)/shard_map/ppermute | solution.py:312
  45.4 4.3 %collective-permute-start.16 = (bf16[64,512]{1,0:T(8,128)(2,1)S(1)}, bf16[64,512]{1,0:T(8,128)(2,1)S(1)}, u32[]{:S(2)}, u32[]{:S(2)}) collective-permute-start(bf16[64,512]{1,0:T(8,128)(2,1)S(1)} %collective-permute-done.13), channel_id=1, source_target_pairs={{0,4},{1,5},{2,6},{3,7},{4,0},{5,1},{6,2},{7,3},{8,12},{9,13},{10,... | collective-permute-start | bytes 196616 | tf_op jit(solution)/shard_map/ppermute | solution.py:312
  46.4 5.7 %collective-permute-start.15 = (bf16[192,512]{1,0:T(8,128)(2,1)S(1)}, bf16[192,512]{1,0:T(8,128)(2,1)S(1)}, u32[]{:S(2)}, u32[]{:S(2)}) collective-permute-start(bf16[192,512]{1,0:T(8,128)(2,1)S(1)} %pad_maximum_fusion.2), channel_id=1, source_target_pairs={{0,2},{1,3},{2,0},{3,1},{4,6},{5,7},{6,4},{7,5},{8,10},{9,11},{10,... | collective-permute-start | bytes 589832 | tf_op jit(solution)/shard_map/ppermute | solution.py:312
  49.7 2.4 %collective-permute-start.18 = (bf16[256,512]{1,0:T(8,128)(2,1)S(1)}, bf16[256,512]{1,0:T(8,128)(2,1)S(1)}, u32[]{:S(2)}, u32[]{:S(2)}) collective-permute-start(bf16[256,512]{1,0:T(8,128)(2,1)S(1)} %pad_maximum_fusion.refs_4_.straight_ref), channel_id=1, source_target_pairs={{0,1},{1,0},{2,3},{3,2},{4,5},{5,4},{6,7},{7,6},{8,9},{9,8},{10,11... | collective-permute-start | bytes 786440 | tf_op jit(solution)/shard_map/ppermute | solution.py:312
  49.8 4.5 %collective-permute-start.17 = (bf16[64,512]{1,0:T(8,128)(2,1)S(1)}, bf16[64,512]{1,0:T(8,128)(2,1)S(1)}, u32[]{:S(2)}, u32[]{:S(2)}) collective-permute-start(bf16[64,512]{1,0:T(8,128)(2,1)S(1)} %collective-permute-done.16), channel_id=1, source_target_pairs={{0,2},{1,3},{2,0},{3,1},{4,6},{5,7},{6,4},{7,5},{8,10},{9,11},{10,... | collective-permute-start | bytes 196616 | tf_op jit(solution)/shard_map/ppermute | solution.py:312
  57.8 5.3 %collective-permute-start.20 = (bf16[160,512]{1,0:T(8,128)(2,1)S(1)}, bf16[160,512]{1,0:T(8,128)(2,1)S(1)}, u32[]{:S(2)}, u32[]{:S(2)}) collective-permute-start(bf16[160,512]{1,0:T(8,128)(2,1)S(1)} %get-tuple-element.195), channel_id=1, source_target_pairs={{0,1},{1,0},{2,3},{3,2},{4,5},{5,4},{6,7},{7,6},{8,9},{9,8},{10,11... | collective-permute-start | bytes 491528 | tf_op jit(solution)/shard_map/ppermute | solution.py:312
  58.0 11.2 %collective-permute-start.24 = (bf16[160,512]{1,0:T(8,128)(2,1)S(1)}, bf16[160,512]{1,0:T(8,128)(2,1)S(1)}, u32[]{:S(2)}, u32[]{:S(2)}) collective-permute-start(bf16[160,512]{1,0:T(8,128)(2,1)S(1)} %get-tuple-element.204), channel_id=1, source_target_pairs={{0,2},{1,3},{2,0},{3,1},{4,6},{5,7},{6,4},{7,5},{8,10},{9,11},{10,... | collective-permute-start | bytes 491528 | tf_op jit(solution)/shard_map/ppermute | solution.py:312
  58.6 10.7 %collective-permute-start.25 = (bf16[160,512]{1,0:T(8,128)(2,1)S(1)}, bf16[160,512]{1,0:T(8,128)(2,1)S(1)}, u32[]{:S(2)}, u32[]{:S(2)}) collective-permute-start(bf16[160,512]{1,0:T(8,128)(2,1)S(1)} %get-tuple-element.205), channel_id=1, source_target_pairs={{0,3},{1,2},{2,1},{3,0},{4,7},{5,6},{6,5},{7,4},{8,11},{9,10},{10,... | collective-permute-start | bytes 491528 | tf_op jit(solution)/shard_map/ppermute | solution.py:312
  59.8 8.6 %collective-permute-start.21 = (bf16[64,512]{1,0:T(8,128)(2,1)S(1)}, bf16[64,512]{1,0:T(8,128)(2,1)S(1)}, u32[]{:S(2)}, u32[]{:S(2)}) collective-permute-start(bf16[64,512]{1,0:T(8,128)(2,1)S(1)} %get-tuple-element.198), channel_id=1, source_target_pairs={{0,8},{1,9},{2,10},{3,11},{4,12},{5,13},{6,14},{7,15},{8,0},{9,1},... | collective-permute-start | bytes 196616 | tf_op jit(solution)/shard_map/ppermute | solution.py:312
  60.9 7.5 %collective-permute-start.22 = (bf16[64,512]{1,0:T(8,128)(2,1)S(1)}, bf16[64,512]{1,0:T(8,128)(2,1)S(1)}, u32[]{:S(2)}, u32[]{:S(2)}) collective-permute-start(bf16[64,512]{1,0:T(8,128)(2,1)S(1)} %get-tuple-element.199), channel_id=1, source_target_pairs={{0,12},{1,13},{2,14},{3,15},{4,8},{5,9},{6,10},{7,11},{8,4},{9,5},... | collective-permute-start | bytes 196616 | tf_op jit(solution)/shard_map/ppermute | solution.py:312
  63.1 6.2 %collective-permute-start.23 = (bf16[64,512]{1,0:T(8,128)(2,1)S(1)}, bf16[64,512]{1,0:T(8,128)(2,1)S(1)}, u32[]{:S(2)}, u32[]{:S(2)}) collective-permute-start(bf16[64,512]{1,0:T(8,128)(2,1)S(1)} %get-tuple-element.200), channel_id=1, source_target_pairs={{0,4},{1,5},{2,6},{3,7},{4,0},{5,1},{6,2},{7,3},{8,12},{9,13},{10,... | collective-permute-start | bytes 196616 | tf_op jit(solution)/shard_map/ppermute | solution.py:312
  (2 other events, 3.3 us)

commit v8 on v7

--- a/solution.py
+++ b/solution.py
@@ -394,6 +394,9 @@
             2 * far_rows * width * (span + 2 * width),
             limit,
         )
+        late, pre_act, found, done = tied((late, pre_act, found, done))
+        late = jnp.concatenate([across, late], axis=0)
+        late = [late, swap(late, 1)]
         pre_act = call(
             far_first_kernel,
             [shape((far_rows, width), F32)],
@@ -402,9 +405,6 @@
             limit,
         )
         found = [*pre_act, *found]
-        late, found, done = tied((late, found, done))
-        late = jnp.concatenate([across, late], axis=0)
-        late = [late, swap(late, 1)]
         moved = shape((slot if last else padded, width), BF)
         parts_shape = [shape((COARSE, width), F32)] + [shape((COARSE, width), BF)] * (lines - 1)
 

time: 71 us -> 70.2 us (0.989)
  waiting for transfers between devices: 13.7 us -> 12.1 us
  starting transfers between devices: 27.4 us -> 28.2 us
    ppermute x26, waiting for transfers between devices: 13.7 us -> 12.1 us  [swap(): lax.ppermute(values, 'patch', [(i, i ^ distance) for i in range(devices)])]
    ppermute x26, starting transfers between devices: 27.4 us -> 28.2 us  [swap(): lax.ppermute(values, 'patch', [(i, i ^ distance) for i in range(devices)])]
where the time goes in v8:
time: 70.2 us; the launch traced here: 70 us
  Pallas kernels  28.6 us (41%)
  starting transfers between devices  28.2 us (40%)
  waiting for transfers between devices  12.1 us (17%)
  between operations  1.05 us (1%)
    pallas_call x17, Pallas kernels, call(): pl.pallas_call(kernel, out_shape=outs, in_specs=specs, out_specs=[pl.Bloc...  28.6 us
    ppermute x26, starting transfers between devices, swap(): lax.ppermute(values, 'patch', [(i, i ^ distance) for i in range(devices)])  28.2 us
    ppermute x26, waiting for transfers between devices, swap(): lax.ppermute(values, 'patch', [(i, i ^ distance) for i in range(devices)])  12.1 us
  transfers between devices with their start and end apart: 26, of which 12 were waited for; matrix products, arithmetic and copies ran while one was open for 0% of the time, Pallas kernels for 30%

profile of v8, /device:TPU:0, one launch (start us, length us, event | category | flops | bytes accessed | tf_op | source)
XLA Modules:
  0.0 70.0 jit_solution(3739554939194327892)
XLA Ops:
  0.6 1.5 %shard_map.184 = (s32[1,256]{1,0:T(1,128)S(1)}, bf16[64,512]{1,0:T(8,128)(2,1)S(1)}, bf16[192,512]{1,0:T(8,128)(2,1)S(1)}, bf16[176,512]{1,0:T(8,128)(2,1)S(1)},...) custom-call(s32[1]{0:T(128)} %bitcast.own_ref, s32[1,256]{1,0:T(1,128)} %bitcast.3, ...), custom_call_target="tpu_custom_call" | custom-call | flops 167772160 | bytes 1510404 | tf_op jit(solution)/shard_map/pallas_call | solution.py:271
  2.7 2.6 %collective-permute-start.3 = (bf16[176,512]{1,0:T(8,128)(2,1)S(1)}, bf16[176,512]{1,0:T(8,128)(2,1)S(1)}, u32[]{:S(2)}, u32[]{:S(2)}) collective-permute-start(bf16[176,512]{1,0:T(8,128)(2,1)S(1)} %get-tuple-element.120), channel_id=1, source_target_pairs={{0,2},{1,3},{2,0},{3,1},{4,6},{5,7},{6,4},{7,5},{8,10},{9,11},{10,... | collective-permute-start | bytes 540680 | tf_op jit(solution)/shard_map/ppermute | solution.py:312
  5.3 2.8 %collective-permute-start = (bf16[64,512]{1,0:T(8,128)(2,1)S(1)}, bf16[64,512]{1,0:T(8,128)(2,1)S(1)}, u32[]{:S(2)}, u32[]{:S(2)}) collective-permute-start(bf16[64,512]{1,0:T(8,128)(2,1)S(1)} %get-tuple-element.106.refs_0_.coarse_ref.nodes_ref), channel_id=1, source_target_pairs={{0,8},{1,9},{2,10},{3,11},{4,12},{5,13},{6,14},{7,15},{8,0},{9,1},... | collective-permute-start | bytes 196616 | tf_op jit(solution)/shard_map/ppermute | solution.py:312
  8.2 1.6 %collective-permute-start.1 = (bf16[64,512]{1,0:T(8,128)(2,1)S(1)}, bf16[64,512]{1,0:T(8,128)(2,1)S(1)}, u32[]{:S(2)}, u32[]{:S(2)}) collective-permute-start(bf16[64,512]{1,0:T(8,128)(2,1)S(1)} %get-tuple-element.106.refs_0_.coarse_ref.nodes_ref), channel_id=1, source_target_pairs={{0,4},{1,5},{2,6},{3,7},{4,0},{5,1},{6,2},{7,3},{8,12},{9,13},{10,... | collective-permute-start | bytes 196616 | tf_op jit(solution)/shard_map/ppermute | solution.py:312
  9.7 1.9 %shard_map.185 = (bf16[768,512]{1,0:T(8,128)(2,1)S(1)}, s32[768]{0:T(1024)S(1)}, s32[768]{0:T(1024)S(1)}, f32[2,512]{1,0:T(2,128)S(1)}, f32[2,512]{1,0:T(2,128)S...) custom-call(bf16[768,512]{1,0:T(8,128)(2,1)} %refs_0_.1, s32[768]{0:T(1024)} %refs_1_.1, ...), custom_call_target="tpu_custom_call" | custom-call | bytes 7901184 | tf_op jit(solution)/shard_map/pallas_call | solution.py:271
  11.7 2.7 %shard_map.186 = (bf16[512,512]{1,0:T(8,128)(2,1)S(1)}, f32[256,512]{1,0:T(8,128)S(1)}) custom-call(bf16[64,512]{1,0:T(8,128)(2,1)S(1)} %get-tuple-element.106.refs_0_.coarse_ref.nodes_ref, bf16[192,512]{1,0:T(8,128)(2,1)S(1)} %get-tuple-element.107.refs_1_.nodes_ref, bf16[768,512]{1,0:T(8,128)(2,1)S(1)} %get-tuple-element.108.refs_2_, ...), custom_call_target="tpu_custom_call" | custom-call | tf_op jit(solution)/shard_map/pallas_call | solution.py:271
  15.7 1.5 %collective-permute-start.7 = (bf16[192,512]{1,0:T(8,128)(2,1)S(1)}, bf16[192,512]{1,0:T(8,128)(2,1)S(1)}, u32[]{:S(2)}, u32[]{:S(2)}) collective-permute-start(bf16[192,512]{1,0:T(8,128)(2,1)S(1)} %pad_maximum_fusion.1), channel_id=1, source_target_pairs={{0,2},{1,3},{2,0},{3,1},{4,6},{5,7},{6,4},{7,5},{8,10},{9,11},{10,... | collective-permute-start | bytes 589832 | tf_op jit(solution)/shard_map/ppermute | solution.py:312
  17.3 1.5 %collective-permute-done.5 = bf16[64,512]{1,0:T(8,128)(2,1)S(1)} collective-permute-done((bf16[64,512]{1,0:T(8,128)(2,1)S(1)}, bf16[64,512]{1,0:T(8,128)(2,1)S(1)}, u32[]{:S(2)}, u32[]{:S(2)}) %collective-permute-start.5) | collective-permute-done | bytes 65568 | tf_op jit(solution)/shard_map/ppermute | solution.py:312
  18.7 1.5 %collective-permute-start.6 = (bf16[64,512]{1,0:T(8,128)(2,1)S(1)}, bf16[64,512]{1,0:T(8,128)(2,1)S(1)}, u32[]{:S(2)}, u32[]{:S(2)}) collective-permute-start(bf16[64,512]{1,0:T(8,128)(2,1)S(1)} %collective-permute-done.5), channel_id=1, source_target_pairs={{0,2},{1,3},{2,0},{3,1},{4,6},{5,7},{6,4},{7,5},{8,10},{9,11},{10,... | collective-permute-start | bytes 196616 | tf_op jit(solution)/shard_map/ppermute | solution.py:312
  20.2 1.8 %shard_map.187 = (f32[640,512]{1,0:T(8,128)S(1)}, bf16[640,512]{1,0:T(8,128)(2,1)S(1)}, bf16[640,512]{1,0:T(8,128)(2,1)S(1)}, bf16[256,640]{1,0:T(8,128)(2,1)S(1)}) custom-call(bf16[176,512]{1,0:T(8,128)(2,1)S(1)} %get-tuple-element.126.refs_0_.refs_10_, bf16[176,512]{1,0:T(8,128)(2,1)S(1)} %collective-permute-done.2.refs_1_.refs_11_, ...), custom_call_target="tpu_custom_call" | custom-call | flops 838860800 | bytes 5505024 | tf_op jit(solution)/shard_map/pallas_call | solution.py:271
  22.0 1.7 %shard_map.188 = (bf16[768,512]{1,0:T(8,128)(2,1)S(1)}, f32[256,512]{1,0:T(8,128)S(1)}) custom-call(bf16[64,512]{1,0:T(8,128)(2,1)S(1)} %get-tuple-element.106.refs_0_.coarse_ref.nodes_ref, bf16[192,512]{1,0:T(8,128)(2,1)S(1)} %get-tuple-element.107.refs_1_.nodes_ref, bf16[768,512]{1,0:T(8,128)(2,1)S(1)} %get-tuple-element.108.refs_2_, ...), custom_call_target="tpu_custom_call" | custom-call | flops 738197504 | bytes 5523456 | tf_op jit(solution)/shard_map/pallas_call | solution.py:271
  25.6 2.0 %shard_map.192 = (bf16[176,512]{1,0:T(8,128)(2,1)S(1)}, bf16[176,512]{1,0:T(8,128)(2,1)S(1)}, bf16[176,512]{1,0:T(8,128)(2,1)S(1)}, bf16[176,512]{1,0:T(8,128)(2...) custom-call(bf16[256,512]{1,0:T(8,128)(2,1)S(1)} %constant_dynamic-u, ...), custom_call_target="tpu_custom_call" | custom-call | flops 1174405120 | bytes 6696960 | tf_op jit(solution)/shard_map/pallas_call | solution.py:271
  27.7 2.6 %collective-permute-start.10 = (bf16[64,512]{1,0:T(8,128)(2,1)S(1)}, bf16[64,512]{1,0:T(8,128)(2,1)S(1)}, u32[]{:S(2)}, u32[]{:S(2)}) collective-permute-start(bf16[64,512]{1,0:T(8,128)(2,1)S(1)} %get-tuple-element.159), channel_id=1, source_target_pairs={{0,8},{1,9},{2,10},{3,11},{4,12},{5,13},{6,14},{7,15},{8,0},{9,1},... | collective-permute-start | bytes 196616 | tf_op jit(solution)/shard_map/ppermute | solution.py:312
  31.4 2.6 %shard_map.189 = (bf16[2,1024,512]{2,1,0:T(8,128)(2,1)S(1)}, bf16[2,512,512]{2,1,0:T(8,128)(2,1)S(1)}, f32[2,512]{1,0:T(2,128)S(1)}, f32[2,512]{1,0:T(2,128)S(1)...) custom-call(bf16[2,1024,512]{2,1,0:T(8,128)(2,1)} %refs_0_.2, ...), custom_call_target="tpu_custom_call" | custom-call | bytes 12607488 | tf_op jit(solution)/shard_map/pallas_call | solution.py:271
  37.7 2.5 %collective-permute-start.13 = (bf16[64,512]{1,0:T(8,128)(2,1)S(1)}, bf16[64,512]{1,0:T(8,128)(2,1)S(1)}, u32[]{:S(2)}, u32[]{:S(2)}) collective-permute-start(bf16[64,512]{1,0:T(8,128)(2,1)S(1)} %shard_map.193.refs_0_.coarse_ref.nodes_ref), channel_id=1, source_target_pairs={{0,8},{1,9},{2,10},{3,11},{4,12},{5,13},{6,14},{7,15},{8,0},{9,1},... | collective-permute-start | bytes 196616 | tf_op jit(solution)/shard_map/ppermute | solution.py:312
  41.2 2.6 %shard_map.194 = (bf16[512,512]{1,0:T(8,128)(2,1)S(1)}, f32[256,512]{1,0:T(8,128)S(1)}) custom-call(bf16[64,512]{1,0:T(8,128)(2,1)S(1)} %shard_map.193.refs_0_.coarse_ref.nodes_ref, bf16[192,512]{1,0:T(8,128)(2,1)S(1)} %get-tuple-element.162.refs_1_.nodes_ref, bf16[768,512]{1,0:T(8,128)(2,1)S(1)} %get-tuple-element.163.refs_2_, ...), custom_call_target="tpu_custom_call" | custom-call | flops 1476395008 | bytes 4212736 | tf_op jit(solution)/shard_map/pallas_call | solution.py:271
  46.3 2.4 %collective-permute-done.16 = bf16[64,512]{1,0:T(8,128)(2,1)S(1)} collective-permute-done((bf16[64,512]{1,0:T(8,128)(2,1)S(1)}, bf16[64,512]{1,0:T(8,128)(2,1)S(1)}, u32[]{:S(2)}, u32[]{:S(2)}) %collective-permute-start.16) | collective-permute-done | bytes 65568 | tf_op jit(solution)/shard_map/ppermute | solution.py:312
  50.2 1.8 %shard_map.195 = (f32[640,512]{1,0:T(8,128)S(1)}, bf16[640,512]{1,0:T(8,128)(2,1)S(1)}, bf16[640,512]{1,0:T(8,128)(2,1)S(1)}, bf16[256,640]{1,0:T(8,128)(2,1)S(1)}) custom-call(bf16[176,512]{1,0:T(8,128)(2,1)S(1)} %get-tuple-element.170.refs_0_.refs_10_, bf16[176,512]{1,0:T(8,128)(2,1)S(1)} %get-tuple-element.171.refs_1_.refs_11_, ...), custom_call_target="tpu_custom_call" | custom-call | flops 838860800 | bytes 5505024 | tf_op jit(solution)/shard_map/pallas_call | solution.py:271
  51.9 1.4 %collective-permute-done.17 = bf16[64,512]{1,0:T(8,128)(2,1)S(1)} collective-permute-done((bf16[64,512]{1,0:T(8,128)(2,1)S(1)}, bf16[64,512]{1,0:T(8,128)(2,1)S(1)}, u32[]{:S(2)}, u32[]{:S(2)}) %collective-permute-start.17) | collective-permute-done | bytes 65568 | tf_op jit(solution)/shard_map/ppermute | solution.py:312
  55.0 2.0 %shard_map.197 = (bf16[160,512]{1,0:T(8,128)(2,1)S(1)}, bf16[160,512]{1,0:T(8,128)(2,1)S(1)}, bf16[160,512]{1,0:T(8,128)(2,1)S(1)}, bf16[160,512]{1,0:T(8,128)(2...) custom-call(bf16[256,512]{1,0:T(8,128)(2,1)S(1)} %constant_dynamic-u, ...), custom_call_target="tpu_custom_call" | custom-call | flops 1174405120 | bytes 6631424 | tf_op jit(solution)/shard_map/pallas_call | solution.py:271
  60.1 2.1 %collective-permute-start.22 = (bf16[64,512]{1,0:T(8,128)(2,1)S(1)}, bf16[64,512]{1,0:T(8,128)(2,1)S(1)}, u32[]{:S(2)}, u32[]{:S(2)}) collective-permute-start(bf16[64,512]{1,0:T(8,128)(2,1)S(1)} %get-tuple-element.199), channel_id=1, source_target_pairs={{0,12},{1,13},{2,14},{3,15},{4,8},{5,9},{6,10},{7,11},{8,4},{9,5},... | collective-permute-start | bytes 196616 | tf_op jit(solution)/shard_map/ppermute | solution.py:312
  62.5 2.5 %shard_map.198 = (bf16[768,512]{1,0:T(8,128)(2,1)}, f32[256,512]{1,0:T(8,128)S(1)}) custom-call(bf16[64,512]{1,0:T(8,128)(2,1)S(1)} %shard_map.193.refs_0_.coarse_ref.nodes_ref, bf16[192,512]{1,0:T(8,128)(2,1)S(1)} %get-tuple-element.162.refs_1_.nodes_ref, bf16[768,512]{1,0:T(8,128)(2,1)S(1)} %get-tuple-element.163.refs_2_, ...), custom_call_target="tpu_custom_call" | custom-call | flops 738197504 | bytes 5523456 | tf_op jit(solution)/shard_map/pallas_call | solution.py:271
  65.8 1.7 %collective-permute-done.21.refs_1_ = bf16[64,512]{1,0:T(8,128)(2,1)S(1)} collective-permute-done((bf16[64,512]{1,0:T(8,128)(2,1)S(1)}, bf16[64,512]{1,0:T(8,128)(2,1)S(1)}, u32[]{:S(2)}, u32[]{:S(2)}) %collective-permute-start.21) | collective-permute-done | bytes 65568 | tf_op jit(solution)/shard_map/ppermute | solution.py:312
  68.5 1.4 %shard_map.200 = (bf16[256,512]{1,0:T(8,128)(2,1)}, bf16[256,512]{1,0:T(8,128)(2,1)}) custom-call(bf16[64,512]{1,0:T(8,128)(2,1)S(1)} %shard_map.193.refs_0_.coarse_ref.nodes_ref, f32[64,512]{1,0:T(8,128)S(1)} %get-tuple-element.196.pre_ref, f32[256,512]{1,0:T(8,128)S(1)} %get-tuple-element.192.sum_ref, f32[64,512]{1,0:T(8,128)S(1)} %get-tuple-element.197.refs_0_, ...), custom_call_target="tpu_custom_call" | custom-call | flops 100663296 | bytes 5681152 | tf_op jit(solution)/shard_map/pallas_call | solution.py:271
  (56 shorter events, 20.2 us)
Async XLA Ops:
  2.2 12.2 %collective-permute-start.2 = (bf16[176,512]{1,0:T(8,128)(2,1)S(1)}, bf16[176,512]{1,0:T(8,128)(2,1)S(1)}, u32[]{:S(2)}, u32[]{:S(2)}) collective-permute-start(bf16[176,512]{1,0:T(8,128)(2,1)S(1)} %get-tuple-element.119), channel_id=1, source_target_pairs={{0,1},{1,0},{2,3},{3,2},{4,5},{5,4},{6,7},{7,6},{8,9},{9,8},{10,11... | collective-permute-start | bytes 540680 | tf_op jit(solution)/shard_map/ppermute | solution.py:312
  2.7 11.7 %collective-permute-start.3 = (bf16[176,512]{1,0:T(8,128)(2,1)S(1)}, bf16[176,512]{1,0:T(8,128)(2,1)S(1)}, u32[]{:S(2)}, u32[]{:S(2)}) collective-permute-start(bf16[176,512]{1,0:T(8,128)(2,1)S(1)} %get-tuple-element.120), channel_id=1, source_target_pairs={{0,2},{1,3},{2,0},{3,1},{4,6},{5,7},{6,4},{7,5},{8,10},{9,11},{10,... | collective-permute-start | bytes 540680 | tf_op jit(solution)/shard_map/ppermute | solution.py:312
  5.3 9.1 %collective-permute-start.4 = (bf16[176,512]{1,0:T(8,128)(2,1)S(1)}, bf16[176,512]{1,0:T(8,128)(2,1)S(1)}, u32[]{:S(2)}, u32[]{:S(2)}) collective-permute-start(bf16[176,512]{1,0:T(8,128)(2,1)S(1)} %get-tuple-element.121), channel_id=1, source_target_pairs={{0,3},{1,2},{2,1},{3,0},{4,7},{5,6},{6,5},{7,4},{8,11},{9,10},{10,... | collective-permute-start | bytes 540680 | tf_op jit(solution)/shard_map/ppermute | solution.py:312
  5.3 9.0 %collective-permute-start = (bf16[64,512]{1,0:T(8,128)(2,1)S(1)}, bf16[64,512]{1,0:T(8,128)(2,1)S(1)}, u32[]{:S(2)}, u32[]{:S(2)}) collective-permute-start(bf16[64,512]{1,0:T(8,128)(2,1)S(1)} %get-tuple-element.106.refs_0_.coarse_ref.nodes_ref), channel_id=1, source_target_pairs={{0,8},{1,9},{2,10},{3,11},{4,12},{5,13},{6,14},{7,15},{8,0},{9,1},... | collective-permute-start | bytes 196616 | tf_op jit(solution)/shard_map/ppermute | solution.py:312
  8.2 6.2 %collective-permute-start.1 = (bf16[64,512]{1,0:T(8,128)(2,1)S(1)}, bf16[64,512]{1,0:T(8,128)(2,1)S(1)}, u32[]{:S(2)}, u32[]{:S(2)}) collective-permute-start(bf16[64,512]{1,0:T(8,128)(2,1)S(1)} %get-tuple-element.106.refs_0_.coarse_ref.nodes_ref), channel_id=1, source_target_pairs={{0,4},{1,5},{2,6},{3,7},{4,0},{5,1},{6,2},{7,3},{8,12},{9,13},{10,... | collective-permute-start | bytes 196616 | tf_op jit(solution)/shard_map/ppermute | solution.py:312
  14.4 4.3 %collective-permute-start.5 = (bf16[64,512]{1,0:T(8,128)(2,1)S(1)}, bf16[64,512]{1,0:T(8,128)(2,1)S(1)}, u32[]{:S(2)}, u32[]{:S(2)}) collective-permute-start(bf16[64,512]{1,0:T(8,128)(2,1)S(1)} %collective-permute-done), channel_id=1, source_target_pairs={{0,4},{1,5},{2,6},{3,7},{4,0},{5,1},{6,2},{7,3},{8,12},{9,13},{10,... | collective-permute-start | bytes 196616 | tf_op jit(solution)/shard_map/ppermute | solution.py:312
  15.7 8.3 %collective-permute-start.7 = (bf16[192,512]{1,0:T(8,128)(2,1)S(1)}, bf16[192,512]{1,0:T(8,128)(2,1)S(1)}, u32[]{:S(2)}, u32[]{:S(2)}) collective-permute-start(bf16[192,512]{1,0:T(8,128)(2,1)S(1)} %pad_maximum_fusion.1), channel_id=1, source_target_pairs={{0,2},{1,3},{2,0},{3,1},{4,6},{5,7},{6,4},{7,5},{8,10},{9,11},{10,... | collective-permute-start | bytes 589832 | tf_op jit(solution)/shard_map/ppermute | solution.py:312
  18.7 5.3 %collective-permute-start.6 = (bf16[64,512]{1,0:T(8,128)(2,1)S(1)}, bf16[64,512]{1,0:T(8,128)(2,1)S(1)}, u32[]{:S(2)}, u32[]{:S(2)}) collective-permute-start(bf16[64,512]{1,0:T(8,128)(2,1)S(1)} %collective-permute-done.5), channel_id=1, source_target_pairs={{0,2},{1,3},{2,0},{3,1},{4,6},{5,7},{6,4},{7,5},{8,10},{9,11},{10,... | collective-permute-start | bytes 196616 | tf_op jit(solution)/shard_map/ppermute | solution.py:312
  20.2 4.1 %collective-permute-start.9 = (bf16[256,512]{1,0:T(8,128)(2,1)S(1)}, bf16[256,512]{1,0:T(8,128)(2,1)S(1)}, u32[]{:S(2)}, u32[]{:S(2)}) collective-permute-start(bf16[256,512]{1,0:T(8,128)(2,1)S(1)} %constant_dynamic-update-slice_fusion.refs_4_.straight_ref), channel_id=1, source_target_pairs={{0,1},{1,0},{2,3},{3,2},{4,5},{5,4},{6,7},{7,6},{8,9},{9,8},{10,11... | collective-permute-start | bytes 786440 | tf_op jit(solution)/shard_map/ppermute | solution.py:312
  27.7 8.0 %collective-permute-start.10 = (bf16[64,512]{1,0:T(8,128)(2,1)S(1)}, bf16[64,512]{1,0:T(8,128)(2,1)S(1)}, u32[]{:S(2)}, u32[]{:S(2)}) collective-permute-start(bf16[64,512]{1,0:T(8,128)(2,1)S(1)} %get-tuple-element.159), channel_id=1, source_target_pairs={{0,8},{1,9},{2,10},{3,11},{4,12},{5,13},{6,14},{7,15},{8,0},{9,1},... | collective-permute-start | bytes 196616 | tf_op jit(solution)/shard_map/ppermute | solution.py:312
  30.3 6.4 %collective-permute-start.11 = (bf16[64,512]{1,0:T(8,128)(2,1)S(1)}, bf16[64,512]{1,0:T(8,128)(2,1)S(1)}, u32[]{:S(2)}, u32[]{:S(2)}) collective-permute-start(bf16[64,512]{1,0:T(8,128)(2,1)S(1)} %get-tuple-element.160), channel_id=1, source_target_pairs={{0,12},{1,13},{2,14},{3,15},{4,8},{5,9},{6,10},{7,11},{8,4},{9,5},... | collective-permute-start | bytes 196616 | tf_op jit(solution)/shard_map/ppermute | solution.py:312
  31.2 5.9 %collective-permute-start.12 = (bf16[64,512]{1,0:T(8,128)(2,1)S(1)}, bf16[64,512]{1,0:T(8,128)(2,1)S(1)}, u32[]{:S(2)}, u32[]{:S(2)}) collective-permute-start(bf16[64,512]{1,0:T(8,128)(2,1)S(1)} %get-tuple-element.161), channel_id=1, source_target_pairs={{0,4},{1,5},{2,6},{3,7},{4,0},{5,1},{6,2},{7,3},{8,12},{9,13},{10,... | collective-permute-start | bytes 196616 | tf_op jit(solution)/shard_map/ppermute | solution.py:312
  37.7 6.2 %collective-permute-start.13 = (bf16[64,512]{1,0:T(8,128)(2,1)S(1)}, bf16[64,512]{1,0:T(8,128)(2,1)S(1)}, u32[]{:S(2)}, u32[]{:S(2)}) collective-permute-start(bf16[64,512]{1,0:T(8,128)(2,1)S(1)} %shard_map.193.refs_0_.coarse_ref.nodes_ref), channel_id=1, source_target_pairs={{0,8},{1,9},{2,10},{3,11},{4,12},{5,13},{6,14},{7,15},{8,0},{9,1},... | collective-permute-start | bytes 196616 | tf_op jit(solution)/shard_map/ppermute | solution.py:312
  40.1 4.4 %collective-permute-start.14 = (bf16[64,512]{1,0:T(8,128)(2,1)S(1)}, bf16[64,512]{1,0:T(8,128)(2,1)S(1)}, u32[]{:S(2)}, u32[]{:S(2)}) collective-permute-start(bf16[64,512]{1,0:T(8,128)(2,1)S(1)} %shard_map.193.refs_0_.coarse_ref.nodes_ref), channel_id=1, source_target_pairs={{0,4},{1,5},{2,6},{3,7},{4,0},{5,1},{6,2},{7,3},{8,12},{9,13},{10,... | collective-permute-start | bytes 196616 | tf_op jit(solution)/shard_map/ppermute | solution.py:312
  44.5 4.3 %collective-permute-start.16 = (bf16[64,512]{1,0:T(8,128)(2,1)S(1)}, bf16[64,512]{1,0:T(8,128)(2,1)S(1)}, u32[]{:S(2)}, u32[]{:S(2)}) collective-permute-start(bf16[64,512]{1,0:T(8,128)(2,1)S(1)} %collective-permute-done.13), channel_id=1, source_target_pairs={{0,4},{1,5},{2,6},{3,7},{4,0},{5,1},{6,2},{7,3},{8,12},{9,13},{10,... | collective-permute-start | bytes 196616 | tf_op jit(solution)/shard_map/ppermute | solution.py:312
  45.5 7.9 %collective-permute-start.15 = (bf16[192,512]{1,0:T(8,128)(2,1)S(1)}, bf16[192,512]{1,0:T(8,128)(2,1)S(1)}, u32[]{:S(2)}, u32[]{:S(2)}) collective-permute-start(bf16[192,512]{1,0:T(8,128)(2,1)S(1)} %pad_maximum_fusion.2), channel_id=1, source_target_pairs={{0,2},{1,3},{2,0},{3,1},{4,6},{5,7},{6,4},{7,5},{8,10},{9,11},{10,... | collective-permute-start | bytes 589832 | tf_op jit(solution)/shard_map/ppermute | solution.py:312
  48.8 4.7 %collective-permute-start.19 = (bf16[256,512]{1,0:T(8,128)(2,1)S(1)}, bf16[256,512]{1,0:T(8,128)(2,1)S(1)}, u32[]{:S(2)}, u32[]{:S(2)}) collective-permute-start(bf16[256,512]{1,0:T(8,128)(2,1)S(1)} %pad_maximum_fusion.refs_4_.straight_ref), channel_id=1, source_target_pairs={{0,1},{1,0},{2,3},{3,2},{4,5},{5,4},{6,7},{7,6},{8,9},{9,8},{10,11... | collective-permute-start | bytes 786440 | tf_op jit(solution)/shard_map/ppermute | solution.py:312
  48.9 4.5 %collective-permute-start.17 = (bf16[64,512]{1,0:T(8,128)(2,1)S(1)}, bf16[64,512]{1,0:T(8,128)(2,1)S(1)}, u32[]{:S(2)}, u32[]{:S(2)}) collective-permute-start(bf16[64,512]{1,0:T(8,128)(2,1)S(1)} %collective-permute-done.16), channel_id=1, source_target_pairs={{0,2},{1,3},{2,0},{3,1},{4,6},{5,7},{6,4},{7,5},{8,10},{9,11},{10,... | collective-permute-start | bytes 196616 | tf_op jit(solution)/shard_map/ppermute | solution.py:312
  57.0 5.2 %collective-permute-start.20 = (bf16[160,512]{1,0:T(8,128)(2,1)S(1)}, bf16[160,512]{1,0:T(8,128)(2,1)S(1)}, u32[]{:S(2)}, u32[]{:S(2)}) collective-permute-start(bf16[160,512]{1,0:T(8,128)(2,1)S(1)} %get-tuple-element.195), channel_id=1, source_target_pairs={{0,1},{1,0},{2,3},{3,2},{4,5},{5,4},{6,7},{7,6},{8,9},{9,8},{10,11... | collective-permute-start | bytes 491528 | tf_op jit(solution)/shard_map/ppermute | solution.py:312
  57.3 11.2 %collective-permute-start.24 = (bf16[160,512]{1,0:T(8,128)(2,1)S(1)}, bf16[160,512]{1,0:T(8,128)(2,1)S(1)}, u32[]{:S(2)}, u32[]{:S(2)}) collective-permute-start(bf16[160,512]{1,0:T(8,128)(2,1)S(1)} %get-tuple-element.204), channel_id=1, source_target_pairs={{0,2},{1,3},{2,0},{3,1},{4,6},{5,7},{6,4},{7,5},{8,10},{9,11},{10,... | collective-permute-start | bytes 491528 | tf_op jit(solution)/shard_map/ppermute | solution.py:312
  58.5 10.0 %collective-permute-start.25 = (bf16[160,512]{1,0:T(8,128)(2,1)S(1)}, bf16[160,512]{1,0:T(8,128)(2,1)S(1)}, u32[]{:S(2)}, u32[]{:S(2)}) collective-permute-start(bf16[160,512]{1,0:T(8,128)(2,1)S(1)} %get-tuple-element.205), channel_id=1, source_target_pairs={{0,3},{1,2},{2,1},{3,0},{4,7},{5,6},{6,5},{7,4},{8,11},{9,10},{10,... | collective-permute-start | bytes 491528 | tf_op jit(solution)/shard_map/ppermute | solution.py:312
  59.0 8.6 %collective-permute-start.21 = (bf16[64,512]{1,0:T(8,128)(2,1)S(1)}, bf16[64,512]{1,0:T(8,128)(2,1)S(1)}, u32[]{:S(2)}, u32[]{:S(2)}) collective-permute-start(bf16[64,512]{1,0:T(8,128)(2,1)S(1)} %get-tuple-element.198), channel_id=1, source_target_pairs={{0,8},{1,9},{2,10},{3,11},{4,12},{5,13},{6,14},{7,15},{8,0},{9,1},... | collective-permute-start | bytes 196616 | tf_op jit(solution)/shard_map/ppermute | solution.py:312
  60.1 7.4 %collective-permute-start.22 = (bf16[64,512]{1,0:T(8,128)(2,1)S(1)}, bf16[64,512]{1,0:T(8,128)(2,1)S(1)}, u32[]{:S(2)}, u32[]{:S(2)}) collective-permute-start(bf16[64,512]{1,0:T(8,128)(2,1)S(1)} %get-tuple-element.199), channel_id=1, source_target_pairs={{0,12},{1,13},{2,14},{3,15},{4,8},{5,9},{6,10},{7,11},{8,4},{9,5},... | collective-permute-start | bytes 196616 | tf_op jit(solution)/shard_map/ppermute | solution.py:312
  62.3 6.2 %collective-permute-start.23 = (bf16[64,512]{1,0:T(8,128)(2,1)S(1)}, bf16[64,512]{1,0:T(8,128)(2,1)S(1)}, u32[]{:S(2)}, u32[]{:S(2)}) collective-permute-start(bf16[64,512]{1,0:T(8,128)(2,1)S(1)} %get-tuple-element.200), channel_id=1, source_target_pairs={{0,4},{1,5},{2,6},{3,7},{4,0},{5,1},{6,2},{7,3},{8,12},{9,13},{10,... | collective-permute-start | bytes 196616 | tf_op jit(solution)/shard_map/ppermute | solution.py:312
  (2 other events, 3.2 us)
